TPU v7x, 512 devices: a whole 4x4x16 slice. The times are simulated.
512 devices in a mesh: context: 16 (over z), dp: 8 (over x, core), tensor: 4 (over y).
Axes of the slice: x: 4, y: 4, z: 16, core: 2. Of those that a mesh axis runs over, the one named last changes fastest.
Arguments:
- conv_input: bfloat16 [8, 4096, 4, 2048], P('dp', 'context', None, 'tensor'), may hold values from -6 to 6
- output_grad: bfloat16 [8, 4096, 4, 2048], P('dp', 'context', None, 'tensor'), may hold values from -6 to 6
- b_matrix: bfloat16 [8, 4096, 4, 128], P('dp', 'context'), may hold values from -0.59765625 to 0.59765625
- c_matrix: bfloat16 [8, 4096, 4, 128], P('dp', 'context'), may hold values from -0.59765625 to 0.59765625
- step_size: float32 [8, 4096, 4, 32], P('dp', 'context', None, 'tensor'), may hold values from 0.18 to 5.76, as said below
- decay_rate: float32 [4, 32], P(None, 'tensor'), may hold values from 1e-05 to 0.08
- skip_gain: float32 [4, 32], P(None, 'tensor'), may hold values from 0.5 to 1.5
- conv_weight: float32 [4, 4, 2048], P(None, None, 'tensor'), may hold values from -3 to 3
- conv_bias: float32 [4, 2048], P(None, 'tensor'), may hold values from -3 to 3
- saved_state: bfloat16 [8, 16, 4, 32, 64, 128], P('dp', 'context', None, 'tensor'), may hold values from -0.59765625 to 0.59765625
- doc_lengths: int32 [8, 6], P('dp'), may hold values from 1 to 2048, 4096 in all within a row
Outputs:
- grad_input: bfloat16 [8, 4096, 4, 2048], P('dp', 'context', None, 'tensor')
- grad_b: float32 [8, 4096, 4, 128], P('dp', 'context', 'tensor')
- grad_c: float32 [8, 4096, 4, 128], P('dp', 'context', 'tensor')
- grad_step: float32 [8, 4096, 4, 32], P('dp', 'context', None, 'tensor')
- grad_weight: float32 [4, 4, 2048], P(None, None, 'tensor')
- grad_bias: float32 [4, 2048], P(None, 'tensor')
- grad_rate: float32 [4, 32], P(None, 'tensor')
- grad_skip: float32 [4, 32], P(None, 'tensor')
Inputs may be any that keep to these rules, and one draw needn't show every extreme that they name: `step_size`: step sizes vary from position to position and from head to head. `doc_lengths`: the lengths of each row sum to 4096; the longest document of a row has exactly 2048 positions.
All inputs are finite; a program needn't handle non-finite values.
Results may differ from a plain program's by a relative error of at most 0.022.
Values may be sent and summed in bfloat16 or wider, within the bound.
No kernel may reach another device: no remote copies, remote signals or barrier semaphores. Data moves between devices by JAX's collectives and lax.ppermute only.
A program may use at most 128 MiB of HBM per device.

v0:
```python
import jax
import jax.numpy as jnp
from jax import lax
from jax.sharding import PartitionSpec as P

exact_prec = lax.Precision.HIGHEST


def passed_along(block, axis, distance):
    devices = range(lax.axis_size(axis))
    route = [(i - distance, i) for i in devices if i - distance in devices]
    return lax.ppermute(block, axis, route)


def mixed(form, left, right):
    return jnp.einsum(form, left, right, preferred_element_type=jnp.float32)


def segment_ids(doc_lengths, positions):
    starts = jnp.cumsum(doc_lengths, axis=-1) - doc_lengths
    before = starts[:, None, :] <= positions[None, :, None]
    return jnp.sum(before.astype(jnp.int32), axis=-1)


def conv_forward(extended, seg_ext, conv_weight, conv_bias):
    kernel_width = conv_weight.shape[0]
    row_count = extended.shape[1] - kernel_width + 1
    seg_now = seg_ext[:, kernel_width - 1 :]
    summed = jnp.zeros(extended[:, kernel_width - 1 :].shape, jnp.float32) + conv_bias
    for lag_index in range(kernel_width):
        first_row = kernel_width - 1 - lag_index
        window_rows = extended[:, first_row : first_row + row_count].astype(jnp.float32)
        same_doc = (seg_ext[:, first_row : first_row + row_count] == seg_now)[:, :, None, None]
        summed = summed + jnp.where(same_doc, conv_weight[lag_index] * window_rows, 0.0)
    return summed


def conv_input_grad(grad_ext, seg_ext, conv_weight):
    kernel_width = conv_weight.shape[0]
    row_count = grad_ext.shape[1] - kernel_width + 1
    seg_now = seg_ext[:, :row_count]
    summed = jnp.zeros(grad_ext[:, :row_count].shape, jnp.float32)
    for lag_index in range(kernel_width):
        window_rows = grad_ext[:, lag_index : lag_index + row_count]
        same_doc = (seg_ext[:, lag_index : lag_index + row_count] == seg_now)[:, :, None, None]
        summed = summed + jnp.where(same_doc, conv_weight[lag_index] * window_rows, 0.0)
    return summed


def conv_weight_grad(extended, seg_ext, grad_pre):
    kernel_width = extended.shape[1] - grad_pre.shape[1] + 1
    row_count = grad_pre.shape[1]
    seg_now = seg_ext[:, kernel_width - 1 :]
    lag_terms = []
    for lag_index in range(kernel_width):
        first_row = kernel_width - 1 - lag_index
        window_rows = extended[:, first_row : first_row + row_count].astype(jnp.float32)
        same_doc = (seg_ext[:, first_row : first_row + row_count] == seg_now)[:, :, None, None]
        lag_terms.append(jnp.sum(jnp.where(same_doc, grad_pre * window_rows, 0.0), axis=(0, 1)))
    return jnp.stack(lag_terms)


def lower_ones(row_count):
    row_index = jnp.arange(row_count)
    return (row_index[:, None] >= row_index[None, :]).astype(jnp.float32)


def decay_terms(step_size, decay_rate, segment, segment_before):
    row_count = step_size.shape[1]
    log_decay = -step_size * decay_rate
    cumulative = jnp.einsum("ts,bsgk->btgk", lower_ones(row_count), log_decay, precision=exact_prec)
    alive = (segment == segment_before[:, None])[:, :, None, None]
    from_start = jnp.where(alive, jnp.exp(cumulative), 0.0)
    through = from_start[:, -1]
    same_end = (segment == segment[:, -1:])[:, :, None, None]
    to_end = jnp.where(same_end, jnp.exp(jnp.minimum(cumulative[:, -1:] - cumulative, 0.0)), 0.0)
    return (cumulative, from_start, to_end, through)


def group_intra(update, grad_y, b_group, c_group, cumulative, from_start, start_state, segment):
    row_count = cumulative.shape[1]
    row_index = jnp.arange(row_count)
    causal = row_index[:, None] >= row_index[None, :]
    same_doc = causal[None] & (segment[:, :, None] == segment[:, None, :])
    cum_heads = jnp.moveaxis(cumulative, 2, 1)
    log_gaps = cum_heads[:, :, :, None] - cum_heads[:, :, None, :]
    decay_mask = jnp.where(same_doc[:, None], jnp.exp(jnp.minimum(log_gaps, 0.0)), 0.0)
    gram_matrix = mixed("btn,bsn->bts", c_group, b_group)
    scores = decay_mask * gram_matrix[:, None]
    score_bf = scores.astype(jnp.bfloat16)
    grad_update = mixed("bkts,btkp->bskp", score_bf, grad_y)
    grad_score = mixed("btkp,bskp->bkts", grad_y, update)
    product = scores * grad_score
    grad_cum = jnp.sum(product, axis=3) - jnp.sum(product, axis=2)
    grad_gram = jnp.sum(decay_mask * grad_score, axis=1).astype(jnp.bfloat16)
    grad_c = mixed("bts,bsn->btn", grad_gram, b_group)
    grad_b = mixed("bts,btn->bsn", grad_gram, c_group)
    state_c = mixed("bkpn,btn->btkp", start_state, c_group)
    grad_cum = jnp.moveaxis(grad_cum, 1, 2) + from_start * jnp.sum(
        grad_y.astype(jnp.float32) * state_c, axis=-1
    )
    grad_state = mixed("btkp,bkpn->btkn", grad_y, start_state)
    grad_c = grad_c + jnp.sum(from_start[..., None] * grad_state, axis=2)
    scaled_grad = (from_start[..., None] * grad_y.astype(jnp.float32)).astype(jnp.bfloat16)
    offset = mixed("btkp,btn->bkpn", scaled_grad, c_group)
    return (grad_update, grad_cum, grad_c, grad_b, offset)


def group_carry(state_grad, update, b_group, to_end, start_state, through):
    state_bf = state_grad.astype(jnp.bfloat16)
    carry_b = mixed("bkpn,bsn->bskp", state_bf, b_group)
    grad_update = to_end[..., None] * carry_b
    along_end = to_end * jnp.sum(update.astype(jnp.float32) * carry_b, axis=-1)
    update_carry = mixed("bskp,bkpn->bskn", update, state_bf)
    grad_b = jnp.sum(to_end[..., None] * update_carry, axis=2)
    last_term = jnp.sum(along_end, axis=1) + through * jnp.sum(
        state_grad * start_state.astype(jnp.float32), axis=(2, 3)
    )
    row_count = along_end.shape[1]
    is_last = (jnp.arange(row_count) == row_count - 1)[None, :, None]
    grad_cum = jnp.where(is_last, last_term[:, None, :], 0.0) - along_end
    return (grad_update, grad_cum, grad_b)


def stretch_intra(update, grad_y, b_matrix, c_matrix, cumulative, from_start, start_state, segment):

    def one_group(group_items):
        return group_intra(*group_items, segment)

    results = lax.map(
        one_group,
        (
            jnp.moveaxis(update, 2, 0),
            jnp.moveaxis(grad_y, 2, 0),
            jnp.moveaxis(b_matrix, 2, 0),
            jnp.moveaxis(c_matrix, 2, 0),
            jnp.moveaxis(cumulative, 2, 0),
            jnp.moveaxis(from_start, 2, 0),
            jnp.moveaxis(start_state, 1, 0),
        ),
    )
    return (
        jnp.moveaxis(results[0], 0, 2),
        jnp.moveaxis(results[1], 0, 2),
        jnp.moveaxis(results[2], 0, 2),
        jnp.moveaxis(results[3], 0, 2),
        jnp.moveaxis(results[4], 0, 1),
    )


def stretch_carry(state_grad, update, b_matrix, to_end, start_state, through):

    def one_group(group_items):
        return group_carry(*group_items)

    results = lax.map(
        one_group,
        (
            jnp.moveaxis(state_grad, 1, 0),
            jnp.moveaxis(update, 2, 0),
            jnp.moveaxis(b_matrix, 2, 0),
            jnp.moveaxis(to_end, 2, 0),
            jnp.moveaxis(start_state, 1, 0),
            jnp.moveaxis(through, 1, 0),
        ),
    )
    return (
        jnp.moveaxis(results[0], 0, 2),
        jnp.moveaxis(results[1], 0, 2),
        jnp.moveaxis(results[2], 0, 2),
    )


def finish(grad_update, grad_cum, step_size, conv_heads, grad_y, decay_rate, skip_gain):
    row_count = grad_cum.shape[1]
    grad_log = jnp.einsum("ts,btgk->bsgk", lower_ones(row_count), grad_cum, precision=exact_prec)
    grad_step = -decay_rate * grad_log + jnp.sum(
        grad_update * conv_heads.astype(jnp.float32), axis=-1
    )
    grad_conv = step_size[..., None] * grad_update + skip_gain[..., None] * grad_y.astype(
        jnp.float32
    )
    grad_rate = -jnp.sum(step_size * grad_log, axis=(0, 1))
    grad_skip = jnp.sum(
        jnp.sum(grad_y.astype(jnp.float32) * conv_heads.astype(jnp.float32), axis=-1), axis=(0, 1)
    )
    return (grad_step, grad_conv, grad_rate, grad_skip)


def body(
    conv_input,
    output_grad,
    b_matrix,
    c_matrix,
    step_size,
    decay_rate,
    skip_gain,
    conv_weight,
    conv_bias,
    saved_state,
    doc_lengths,
):
    seq_count, row_count, groups, features = conv_input.shape
    kernel_width = conv_weight.shape[0]
    head_count = step_size.shape[3]
    head_dim = features // head_count
    shard_index = lax.axis_index("context")
    shard_count = lax.axis_size("context")
    first_pos = shard_index * row_count
    positions = first_pos - (kernel_width - 1) + jnp.arange(row_count + 2 * (kernel_width - 1))
    seg_all = segment_ids(doc_lengths, positions)
    seg_before = seg_all[:, : row_count + kernel_width - 1]
    seg_here = seg_all[:, kernel_width - 1 : kernel_width - 1 + row_count]
    seg_after = seg_all[:, kernel_width - 1 :]
    seg_first = seg_all[:, kernel_width - 2]
    left_rows = passed_along(conv_input[:, row_count - (kernel_width - 1) :], "context", 1)
    extended = jnp.concatenate([left_rows, conv_input], axis=1)
    pre_act = conv_forward(extended, seg_before, conv_weight, conv_bias)
    conv_out = jax.nn.silu(pre_act).astype(jnp.bfloat16)
    conv_heads = conv_out.reshape(seq_count, row_count, groups, head_count, head_dim)
    grad_heads = output_grad.reshape(seq_count, row_count, groups, head_count, head_dim)
    update = (step_size[..., None] * conv_heads.astype(jnp.float32)).astype(jnp.bfloat16)
    start_state = saved_state[:, 0]
    cumulative, from_start, to_end, through = decay_terms(
        step_size, decay_rate, seg_here, seg_first
    )
    update_one, cum_one, grad_c, b_one, offset = stretch_intra(
        update, grad_heads, b_matrix, c_matrix, cumulative, from_start, start_state, seg_here
    )
    zero_state = jnp.zeros(offset.shape, jnp.float32)

    def pass_link(turn_index, state_grad):
        return passed_along(
            (through[..., None, None] * state_grad + offset).astype(jnp.bfloat16), "context", -1
        ).astype(jnp.float32)

    state_grad = lax.fori_loop(0, shard_count - 1, pass_link, zero_state)
    update_two, cum_two, b_two = stretch_carry(
        state_grad, update, b_matrix, to_end, start_state, through
    )
    grad_step, grad_conv, grad_rate, grad_skip = finish(
        update_one + update_two,
        cum_one + cum_two,
        step_size,
        conv_heads,
        grad_heads,
        decay_rate,
        skip_gain,
    )
    grad_conv = grad_conv.reshape(seq_count, row_count, groups, features)
    sigmoid_pre = jax.nn.sigmoid(pre_act)
    grad_pre = grad_conv * (sigmoid_pre * (1.0 + pre_act * (1.0 - sigmoid_pre)))
    right_rows = passed_along(grad_pre[:, : kernel_width - 1], "context", -1)
    grad_ext = jnp.concatenate([grad_pre, right_rows], axis=1)
    grad_input = conv_input_grad(grad_ext, seg_after, conv_weight).astype(jnp.bfloat16)
    grad_weight = conv_weight_grad(extended, seg_before, grad_pre)
    grad_bias = jnp.sum(grad_pre, axis=(0, 1))
    grad_weight, grad_bias, grad_rate, grad_skip = lax.psum(
        (grad_weight, grad_bias, grad_rate, grad_skip), ("context", "dp")
    )
    grad_b, grad_c = (
        lax.psum_scatter(
            (b_one + b_two).astype(jnp.bfloat16), "tensor", scatter_dimension=2, tiled=True
        ).astype(jnp.float32),
        lax.psum_scatter(
            grad_c.astype(jnp.bfloat16), "tensor", scatter_dimension=2, tiled=True
        ).astype(jnp.float32),
    )
    return (grad_input, grad_b, grad_c, grad_step, grad_weight, grad_bias, grad_rate, grad_skip)


def solution(mesh):
    return jax.shard_map(
        body,
        mesh=mesh,
        in_specs=(
            P("dp", "context", None, "tensor"),
            P("dp", "context", None, "tensor"),
            P("dp", "context", None, None),
            P("dp", "context", None, None),
            P("dp", "context", None, "tensor"),
            P(None, "tensor"),
            P(None, "tensor"),
            P(None, None, "tensor"),
            P(None, "tensor"),
            P("dp", "context", None, "tensor", None, None),
            P("dp", None),
        ),
        out_specs=(
            P("dp", "context", None, "tensor"),
            P("dp", "context", "tensor", None),
            P("dp", "context", "tensor", None),
            P("dp", "context", None, "tensor"),
            P(None, None, "tensor"),
            P(None, "tensor"),
            P(None, "tensor"),
            P(None, "tensor"),
        ),
        check_vma=False,
    )
```

profile of v0, /device:TPU:1, one launch (start us, length us, event | category | flops | bytes accessed | tf_op | source)
XLA Modules:
  0.0 896.2 jit_solution(14197363565717074198)
XLA Ops:
  9.1 5.2 collective-permute-start.1
  17.9 1.9 compare_reduce_fusion.2
  20.4 1.6 fusion.118
  22.1 2.1 fusion.135
  25.6 1.9 copy_bitcast_fusion
  27.6 1.6 copy.93
  29.8 1.6 copy.90
  32.2 7.4 multiply_reduce_fusion.3
  41.1 1.6 broadcast.241.clone
  43.5 51.8 %while.43 = (s32[]{:T(128)}, f32[4,1,256,8,64]{2,4,3,1,0:T(8,128)}, f32[4,1,256,8]{2,3,1,0:T(8,128)}, bf16[4,1,256,128]{3,2,1,0:T(8,128)(2,1)}, f32[4,1,256,128]...) while((s32[]{:T(128)}, f32[4,1,256,8,64]{2,4,3,1,0:T(8,128)}, ...), condition=%wide.region_8.9_spmd, body=%wide.region_2.8_spmd.sunk | while | flops 293994496 | bytes 7424685 | solution.py:130
  46.9 2.3 fusion.187
  53.1 1.6 fusion.189
  54.7 1.7 fusion.190
  58.3 1.5 fusion.185
  59.8 2.3 fusion.187
  66.0 1.6 fusion.189
  67.7 1.7 fusion.190
  72.8 2.3 fusion.187
  79.0 1.6 fusion.189
  80.6 1.7 fusion.190
  84.2 1.5 fusion.185
  85.7 2.3 fusion.187
  91.9 1.6 fusion.189
  93.6 1.7 fusion.190
  95.3 237.3 %while.45 = (s32[]{:T(128)}, f32[1,4,8,64,128]{4,3,2,1,0:T(8,128)S(1)}, f32[1,1,4,8]{3,2,1,0:T(4,128)S(1)}, f32[1,4,8,64,128]{4,3,2,1,0:T(8,128)S(1)}, s32[]{:T(128)}, /*index=5*/s32[]{:T(128)}) while((s32[]{:T(128)}, f32[1,4,8,64,128]{4,3,2,1,0:T(8,128)S(1)}, f32[1,1,4,8]{3,2,1,0:T(4,128)S(1)}, ...), condition=%wide.region_10.11_spmd.clone, body=%wide.region_9.10_spmd.clone.sunk | while | flops 1310723 | bytes 6291703 | solution.py:237
  97.6 10.5 %collective-permute-done = bf16[1,4,8,64,128]{4,3,2,1,0:T(8,128)(2,1)} collective-permute-done((bf16[1,4,8,64,128]{4,3,2,1,0:T(8,128)(2,1)}, bf16[1,4,8,64,128]{4,3,2,1,0:T(8,128)(2,1)}, u32[]{:S(2)}, u32[]{:S(2)}) %collective-permute-start) | collective-permute-done | bytes 524320 | tf_op jit(solution)/shard_map/while/body/eval_jaxpr/ppermute | solution.py:12
  111.6 14.9 %collective-permute-done = bf16[1,4,8,64,128]{4,3,2,1,0:T(8,128)(2,1)} collective-permute-done((bf16[1,4,8,64,128]{4,3,2,1,0:T(8,128)(2,1)}, bf16[1,4,8,64,128]{4,3,2,1,0:T(8,128)(2,1)}, u32[]{:S(2)}, u32[]{:S(2)}) %collective-permute-start) | collective-permute-done | bytes 524320 | tf_op jit(solution)/shard_map/while/body/eval_jaxpr/ppermute | solution.py:12
  129.9 14.8 %collective-permute-done = bf16[1,4,8,64,128]{4,3,2,1,0:T(8,128)(2,1)} collective-permute-done((bf16[1,4,8,64,128]{4,3,2,1,0:T(8,128)(2,1)}, bf16[1,4,8,64,128]{4,3,2,1,0:T(8,128)(2,1)}, u32[]{:S(2)}, u32[]{:S(2)}) %collective-permute-start) | collective-permute-done | bytes 524320 | tf_op jit(solution)/shard_map/while/body/eval_jaxpr/ppermute | solution.py:12
  148.1 11.7 %collective-permute-done = bf16[1,4,8,64,128]{4,3,2,1,0:T(8,128)(2,1)} collective-permute-done((bf16[1,4,8,64,128]{4,3,2,1,0:T(8,128)(2,1)}, bf16[1,4,8,64,128]{4,3,2,1,0:T(8,128)(2,1)}, u32[]{:S(2)}, u32[]{:S(2)}) %collective-permute-start) | collective-permute-done | bytes 524320 | tf_op jit(solution)/shard_map/while/body/eval_jaxpr/ppermute | solution.py:12
  163.3 10.9 %collective-permute-done = bf16[1,4,8,64,128]{4,3,2,1,0:T(8,128)(2,1)} collective-permute-done((bf16[1,4,8,64,128]{4,3,2,1,0:T(8,128)(2,1)}, bf16[1,4,8,64,128]{4,3,2,1,0:T(8,128)(2,1)}, u32[]{:S(2)}, u32[]{:S(2)}) %collective-permute-start) | collective-permute-done | bytes 524320 | tf_op jit(solution)/shard_map/while/body/eval_jaxpr/ppermute | solution.py:12
  177.7 10.0 %collective-permute-done = bf16[1,4,8,64,128]{4,3,2,1,0:T(8,128)(2,1)} collective-permute-done((bf16[1,4,8,64,128]{4,3,2,1,0:T(8,128)(2,1)}, bf16[1,4,8,64,128]{4,3,2,1,0:T(8,128)(2,1)}, u32[]{:S(2)}, u32[]{:S(2)}) %collective-permute-start) | collective-permute-done | bytes 524320 | tf_op jit(solution)/shard_map/while/body/eval_jaxpr/ppermute | solution.py:12
  191.1 9.3 %collective-permute-done = bf16[1,4,8,64,128]{4,3,2,1,0:T(8,128)(2,1)} collective-permute-done((bf16[1,4,8,64,128]{4,3,2,1,0:T(8,128)(2,1)}, bf16[1,4,8,64,128]{4,3,2,1,0:T(8,128)(2,1)}, u32[]{:S(2)}, u32[]{:S(2)}) %collective-permute-start) | collective-permute-done | bytes 524320 | tf_op jit(solution)/shard_map/while/body/eval_jaxpr/ppermute | solution.py:12
  203.9 9.5 %collective-permute-done = bf16[1,4,8,64,128]{4,3,2,1,0:T(8,128)(2,1)} collective-permute-done((bf16[1,4,8,64,128]{4,3,2,1,0:T(8,128)(2,1)}, bf16[1,4,8,64,128]{4,3,2,1,0:T(8,128)(2,1)}, u32[]{:S(2)}, u32[]{:S(2)}) %collective-permute-start) | collective-permute-done | bytes 524320 | tf_op jit(solution)/shard_map/while/body/eval_jaxpr/ppermute | solution.py:12
  216.9 10.2 %collective-permute-done = bf16[1,4,8,64,128]{4,3,2,1,0:T(8,128)(2,1)} collective-permute-done((bf16[1,4,8,64,128]{4,3,2,1,0:T(8,128)(2,1)}, bf16[1,4,8,64,128]{4,3,2,1,0:T(8,128)(2,1)}, u32[]{:S(2)}, u32[]{:S(2)}) %collective-permute-start) | collective-permute-done | bytes 524320 | tf_op jit(solution)/shard_map/while/body/eval_jaxpr/ppermute | solution.py:12
  230.5 10.8 %collective-permute-done = bf16[1,4,8,64,128]{4,3,2,1,0:T(8,128)(2,1)} collective-permute-done((bf16[1,4,8,64,128]{4,3,2,1,0:T(8,128)(2,1)}, bf16[1,4,8,64,128]{4,3,2,1,0:T(8,128)(2,1)}, u32[]{:S(2)}, u32[]{:S(2)}) %collective-permute-start) | collective-permute-done | bytes 524320 | tf_op jit(solution)/shard_map/while/body/eval_jaxpr/ppermute | solution.py:12
  244.7 12.1 %collective-permute-done = bf16[1,4,8,64,128]{4,3,2,1,0:T(8,128)(2,1)} collective-permute-done((bf16[1,4,8,64,128]{4,3,2,1,0:T(8,128)(2,1)}, bf16[1,4,8,64,128]{4,3,2,1,0:T(8,128)(2,1)}, u32[]{:S(2)}, u32[]{:S(2)}) %collective-permute-start) | collective-permute-done | bytes 524320 | tf_op jit(solution)/shard_map/while/body/eval_jaxpr/ppermute | solution.py:12
  260.3 13.6 %collective-permute-done = bf16[1,4,8,64,128]{4,3,2,1,0:T(8,128)(2,1)} collective-permute-done((bf16[1,4,8,64,128]{4,3,2,1,0:T(8,128)(2,1)}, bf16[1,4,8,64,128]{4,3,2,1,0:T(8,128)(2,1)}, u32[]{:S(2)}, u32[]{:S(2)}) %collective-permute-start) | collective-permute-done | bytes 524320 | tf_op jit(solution)/shard_map/while/body/eval_jaxpr/ppermute | solution.py:12
  277.4 14.8 %collective-permute-done = bf16[1,4,8,64,128]{4,3,2,1,0:T(8,128)(2,1)} collective-permute-done((bf16[1,4,8,64,128]{4,3,2,1,0:T(8,128)(2,1)}, bf16[1,4,8,64,128]{4,3,2,1,0:T(8,128)(2,1)}, u32[]{:S(2)}, u32[]{:S(2)}) %collective-permute-start) | collective-permute-done | bytes 524320 | tf_op jit(solution)/shard_map/while/body/eval_jaxpr/ppermute | solution.py:12
  295.6 15.9 %collective-permute-done = bf16[1,4,8,64,128]{4,3,2,1,0:T(8,128)(2,1)} collective-permute-done((bf16[1,4,8,64,128]{4,3,2,1,0:T(8,128)(2,1)}, bf16[1,4,8,64,128]{4,3,2,1,0:T(8,128)(2,1)}, u32[]{:S(2)}, u32[]{:S(2)}) %collective-permute-start) | collective-permute-done | bytes 524320 | tf_op jit(solution)/shard_map/while/body/eval_jaxpr/ppermute | solution.py:12
  315.0 16.5 %collective-permute-done = bf16[1,4,8,64,128]{4,3,2,1,0:T(8,128)(2,1)} collective-permute-done((bf16[1,4,8,64,128]{4,3,2,1,0:T(8,128)(2,1)}, bf16[1,4,8,64,128]{4,3,2,1,0:T(8,128)(2,1)}, u32[]{:S(2)}, u32[]{:S(2)}) %collective-permute-start) | collective-permute-done | bytes 524320 | tf_op jit(solution)/shard_map/while/body/eval_jaxpr/ppermute | solution.py:12
  332.6 1.6 broadcast.241
  335.1 24.4 %while.44 = (s32[]{:T(128)}, f32[4,1,256,8,64]{2,4,3,1,0:T(8,128)}, f32[4,1,256,8]{2,3,1,0:T(8,128)S(1)}, f32[4,1,256,128]{3,2,1,0:T(8,128)}, f32[4,1,256,8]{2,3...) while((s32[]{:T(128)}, f32[4,1,256,8,64]{2,4,3,1,0:T(8,128)}, ...), condition=%wide.region_16.17_spmd, body=%wide.region_11.16_spmd.sunk | while | flops 68329728 | bytes 3552317 | solution.py:156
  359.5 1.8 fusion.115
  361.5 4.1 fusion.110
  365.6 4.9 fusion.90
  374.2 504.1 %all-reduce = (f32[4,4,512]{2,1,0:T(4,128)}, f32[4,512]{1,0:T(4,128)}, f32[4,8]{1,0:T(4,128)}, f32[4,8]{1,0:T(4,128)}) all-reduce(f32[4,4,512]{2,1,0:T(4,128)S(1)} %pad_maximum_fusion.2, f32[4,512]{1,0:T(4,128)S(1)} %get-tuple-element.327, f32[4,8]{1,0:T(4,128)S(1)} %neg.17, ...), channel_id=1, replica_groups=mesh['context'=16,'dp'=8,'tensor'=4] {'context','dp'}, use_global_device_ids=true, to_apply=%region_24.25 | all-reduce | flops 10304 | bytes 82432 | tf_op jit(solution)/shard_map/psum | solution.py:258
  878.7 5.0 fusion.102
  883.7 2.6 copy.115
  (229 shorter events, 121.0 us)
Async XLA Ops:
  7.2 20.4 %copy-start.4 = (bf16[1,256,4,512]{3,2,1,0:T(4,128)(2,1)S(1)}, bf16[1,256,4,512]{3,2,1,0:T(4,128)(2,1)}, u32[]{:S(2)}) copy-start(bf16[1,256,4,512]{3,2,1,0:T(4,128)(2,1)} %param.17) | copy-start | bytes 3145732
  7.2 879.1 %reduce-scatter.3.cloned.1.call-start = ((), (), s32[]{:S(2)}) async-start(), calls=%async_computation.2 | async-start | bytes 327680 | tf_op jit(solution)/shard_map/reduce_scatter | solution.py:262
  8.0 21.2 %copy-start.29 = (f32[4,8]{1,0:T(4,128)S(1)}, f32[4,8]{1,0:T(4,128)}, u32[]{:S(2)}) copy-start(f32[4,8]{1,0:T(4,128)} %param.22) | copy-start | bytes 388
  9.1 23.1 %collective-permute-start.1 = (bf16[1,3,4,512]{1,3,2,0:T(8,128)(2,1)}, bf16[1,3,4,512]{1,3,2,0:T(8,128)(2,1)}, u32[]{:S(2)}, u32[]{:S(2)}) collective-permute-start(bf16[1,3,4,512]{1,3,2,0:T(8,128)(2,1)} %copy.94), channel_id=1, source_target_pairs={{0,32},{32,64},{64,96},{96,128},{128,160},{160,192},{192,224},{224... | collective-permute-start | bytes 36872 | tf_op jit(solution)/shard_map/ppermute | solution.py:12
  17.9 14.3 %copy-start.11 = (f32[4,512]{1,0:T(4,128)}, f32[4,512]{1,0:T(4,128)S(1)}, u32[]{:S(2)}) copy-start(f32[4,512]{1,0:T(4,128)S(1)} %get-tuple-element.416) | copy-start | bytes 24580
  17.9 14.3 %copy-start.13 = (f32[4,512]{1,0:T(4,128)}, f32[4,512]{1,0:T(4,128)S(1)}, u32[]{:S(2)}) copy-start(f32[4,512]{1,0:T(4,128)S(1)} %get-tuple-element.417) | copy-start | bytes 24580
  17.9 14.3 %copy-start.15 = (f32[4,512]{1,0:T(4,128)}, f32[4,512]{1,0:T(4,128)S(1)}, u32[]{:S(2)}) copy-start(f32[4,512]{1,0:T(4,128)S(1)} %get-tuple-element.418) | copy-start | bytes 24580
  19.8 12.3 %copy-start.20 = (pred[256]{0:T(512)(128)(4,1)}, pred[256]{0:T(512)(128)(4,1)S(1)}, u32[]{:S(2)}) copy-start(pred[256]{0:T(512)(128)(4,1)S(1)} %get-tuple-element.333) | copy-start | bytes 772
  19.8 12.3 %copy-start.22 = (pred[256]{0:T(512)(128)(4,1)}, pred[256]{0:T(512)(128)(4,1)S(1)}, u32[]{:S(2)}) copy-start(pred[256]{0:T(512)(128)(4,1)S(1)} %get-tuple-element.334) | copy-start | bytes 772
  19.8 12.3 %copy-start.24 = (pred[256]{0:T(512)(128)(4,1)}, pred[256]{0:T(512)(128)(4,1)S(1)}, u32[]{:S(2)}) copy-start(pred[256]{0:T(512)(128)(4,1)S(1)} %get-tuple-element.335) | copy-start | bytes 772
  27.5 13.6 %copy-start.9 = (f32[4,1,256,8]{2,3,1,0:T(8,128)}, f32[4,1,256,8]{2,3,1,0:T(8,128)S(1)}, u32[]{:S(2)}) copy-start(f32[4,1,256,8]{2,3,1,0:T(8,128)S(1)} %broadcast_bitcast_fusion) | copy-start | bytes 98308
  27.6 4.6 copy-start.18
  32.2 7.4 copy-start.7
  39.6 3.1 copy-start
  96.3 11.8 %collective-permute-start = (bf16[1,4,8,64,128]{4,3,2,1,0:T(8,128)(2,1)}, bf16[1,4,8,64,128]{4,3,2,1,0:T(8,128)(2,1)}, u32[]{:S(2)}, u32[]{:S(2)}) collective-permute-start(bf16[1,4,8,64,128]{4,3,2,1,0:T(8,128)(2,1)} %fusion.198), channel_id=1, source_target_pairs={{32,0},{64,32},{96,64},{128,96},{160,128},{192,160},{224,192},{256... | collective-permute-start | bytes 1572872 | tf_op jit(solution)/shard_map/while/body/eval_jaxpr/ppermute | solution.py:12
  110.3 16.2 %collective-permute-start = (bf16[1,4,8,64,128]{4,3,2,1,0:T(8,128)(2,1)}, bf16[1,4,8,64,128]{4,3,2,1,0:T(8,128)(2,1)}, u32[]{:S(2)}, u32[]{:S(2)}) collective-permute-start(bf16[1,4,8,64,128]{4,3,2,1,0:T(8,128)(2,1)} %fusion.198), channel_id=1, source_target_pairs={{32,0},{64,32},{96,64},{128,96},{160,128},{192,160},{224,192},{256... | collective-permute-start | bytes 1572872 | tf_op jit(solution)/shard_map/while/body/eval_jaxpr/ppermute | solution.py:12
  128.6 16.1 %collective-permute-start = (bf16[1,4,8,64,128]{4,3,2,1,0:T(8,128)(2,1)}, bf16[1,4,8,64,128]{4,3,2,1,0:T(8,128)(2,1)}, u32[]{:S(2)}, u32[]{:S(2)}) collective-permute-start(bf16[1,4,8,64,128]{4,3,2,1,0:T(8,128)(2,1)} %fusion.198), channel_id=1, source_target_pairs={{32,0},{64,32},{96,64},{128,96},{160,128},{192,160},{224,192},{256... | collective-permute-start | bytes 1572872 | tf_op jit(solution)/shard_map/while/body/eval_jaxpr/ppermute | solution.py:12
  146.8 13.0 %collective-permute-start = (bf16[1,4,8,64,128]{4,3,2,1,0:T(8,128)(2,1)}, bf16[1,4,8,64,128]{4,3,2,1,0:T(8,128)(2,1)}, u32[]{:S(2)}, u32[]{:S(2)}) collective-permute-start(bf16[1,4,8,64,128]{4,3,2,1,0:T(8,128)(2,1)} %fusion.198), channel_id=1, source_target_pairs={{32,0},{64,32},{96,64},{128,96},{160,128},{192,160},{224,192},{256... | collective-permute-start | bytes 1572872 | tf_op jit(solution)/shard_map/while/body/eval_jaxpr/ppermute | solution.py:12
  162.0 12.2 %collective-permute-start = (bf16[1,4,8,64,128]{4,3,2,1,0:T(8,128)(2,1)}, bf16[1,4,8,64,128]{4,3,2,1,0:T(8,128)(2,1)}, u32[]{:S(2)}, u32[]{:S(2)}) collective-permute-start(bf16[1,4,8,64,128]{4,3,2,1,0:T(8,128)(2,1)} %fusion.198), channel_id=1, source_target_pairs={{32,0},{64,32},{96,64},{128,96},{160,128},{192,160},{224,192},{256... | collective-permute-start | bytes 1572872 | tf_op jit(solution)/shard_map/while/body/eval_jaxpr/ppermute | solution.py:12
  176.4 11.3 %collective-permute-start = (bf16[1,4,8,64,128]{4,3,2,1,0:T(8,128)(2,1)}, bf16[1,4,8,64,128]{4,3,2,1,0:T(8,128)(2,1)}, u32[]{:S(2)}, u32[]{:S(2)}) collective-permute-start(bf16[1,4,8,64,128]{4,3,2,1,0:T(8,128)(2,1)} %fusion.198), channel_id=1, source_target_pairs={{32,0},{64,32},{96,64},{128,96},{160,128},{192,160},{224,192},{256... | collective-permute-start | bytes 1572872 | tf_op jit(solution)/shard_map/while/body/eval_jaxpr/ppermute | solution.py:12
  189.8 10.6 %collective-permute-start = (bf16[1,4,8,64,128]{4,3,2,1,0:T(8,128)(2,1)}, bf16[1,4,8,64,128]{4,3,2,1,0:T(8,128)(2,1)}, u32[]{:S(2)}, u32[]{:S(2)}) collective-permute-start(bf16[1,4,8,64,128]{4,3,2,1,0:T(8,128)(2,1)} %fusion.198), channel_id=1, source_target_pairs={{32,0},{64,32},{96,64},{128,96},{160,128},{192,160},{224,192},{256... | collective-permute-start | bytes 1572872 | tf_op jit(solution)/shard_map/while/body/eval_jaxpr/ppermute | solution.py:12
  202.6 10.8 %collective-permute-start = (bf16[1,4,8,64,128]{4,3,2,1,0:T(8,128)(2,1)}, bf16[1,4,8,64,128]{4,3,2,1,0:T(8,128)(2,1)}, u32[]{:S(2)}, u32[]{:S(2)}) collective-permute-start(bf16[1,4,8,64,128]{4,3,2,1,0:T(8,128)(2,1)} %fusion.198), channel_id=1, source_target_pairs={{32,0},{64,32},{96,64},{128,96},{160,128},{192,160},{224,192},{256... | collective-permute-start | bytes 1572872 | tf_op jit(solution)/shard_map/while/body/eval_jaxpr/ppermute | solution.py:12
  215.6 11.4 %collective-permute-start = (bf16[1,4,8,64,128]{4,3,2,1,0:T(8,128)(2,1)}, bf16[1,4,8,64,128]{4,3,2,1,0:T(8,128)(2,1)}, u32[]{:S(2)}, u32[]{:S(2)}) collective-permute-start(bf16[1,4,8,64,128]{4,3,2,1,0:T(8,128)(2,1)} %fusion.198), channel_id=1, source_target_pairs={{32,0},{64,32},{96,64},{128,96},{160,128},{192,160},{224,192},{256... | collective-permute-start | bytes 1572872 | tf_op jit(solution)/shard_map/while/body/eval_jaxpr/ppermute | solution.py:12
  229.2 12.1 %collective-permute-start = (bf16[1,4,8,64,128]{4,3,2,1,0:T(8,128)(2,1)}, bf16[1,4,8,64,128]{4,3,2,1,0:T(8,128)(2,1)}, u32[]{:S(2)}, u32[]{:S(2)}) collective-permute-start(bf16[1,4,8,64,128]{4,3,2,1,0:T(8,128)(2,1)} %fusion.198), channel_id=1, source_target_pairs={{32,0},{64,32},{96,64},{128,96},{160,128},{192,160},{224,192},{256... | collective-permute-start | bytes 1572872 | tf_op jit(solution)/shard_map/while/body/eval_jaxpr/ppermute | solution.py:12
  243.4 13.4 %collective-permute-start = (bf16[1,4,8,64,128]{4,3,2,1,0:T(8,128)(2,1)}, bf16[1,4,8,64,128]{4,3,2,1,0:T(8,128)(2,1)}, u32[]{:S(2)}, u32[]{:S(2)}) collective-permute-start(bf16[1,4,8,64,128]{4,3,2,1,0:T(8,128)(2,1)} %fusion.198), channel_id=1, source_target_pairs={{32,0},{64,32},{96,64},{128,96},{160,128},{192,160},{224,192},{256... | collective-permute-start | bytes 1572872 | tf_op jit(solution)/shard_map/while/body/eval_jaxpr/ppermute | solution.py:12
  259.0 14.9 %collective-permute-start = (bf16[1,4,8,64,128]{4,3,2,1,0:T(8,128)(2,1)}, bf16[1,4,8,64,128]{4,3,2,1,0:T(8,128)(2,1)}, u32[]{:S(2)}, u32[]{:S(2)}) collective-permute-start(bf16[1,4,8,64,128]{4,3,2,1,0:T(8,128)(2,1)} %fusion.198), channel_id=1, source_target_pairs={{32,0},{64,32},{96,64},{128,96},{160,128},{192,160},{224,192},{256... | collective-permute-start | bytes 1572872 | tf_op jit(solution)/shard_map/while/body/eval_jaxpr/ppermute | solution.py:12
  276.1 16.1 %collective-permute-start = (bf16[1,4,8,64,128]{4,3,2,1,0:T(8,128)(2,1)}, bf16[1,4,8,64,128]{4,3,2,1,0:T(8,128)(2,1)}, u32[]{:S(2)}, u32[]{:S(2)}) collective-permute-start(bf16[1,4,8,64,128]{4,3,2,1,0:T(8,128)(2,1)} %fusion.198), channel_id=1, source_target_pairs={{32,0},{64,32},{96,64},{128,96},{160,128},{192,160},{224,192},{256... | collective-permute-start | bytes 1572872 | tf_op jit(solution)/shard_map/while/body/eval_jaxpr/ppermute | solution.py:12
  294.3 17.2 %collective-permute-start = (bf16[1,4,8,64,128]{4,3,2,1,0:T(8,128)(2,1)}, bf16[1,4,8,64,128]{4,3,2,1,0:T(8,128)(2,1)}, u32[]{:S(2)}, u32[]{:S(2)}) collective-permute-start(bf16[1,4,8,64,128]{4,3,2,1,0:T(8,128)(2,1)} %fusion.198), channel_id=1, source_target_pairs={{32,0},{64,32},{96,64},{128,96},{160,128},{192,160},{224,192},{256... | collective-permute-start | bytes 1572872 | tf_op jit(solution)/shard_map/while/body/eval_jaxpr/ppermute | solution.py:12
  313.7 17.8 %collective-permute-start = (bf16[1,4,8,64,128]{4,3,2,1,0:T(8,128)(2,1)}, bf16[1,4,8,64,128]{4,3,2,1,0:T(8,128)(2,1)}, u32[]{:S(2)}, u32[]{:S(2)}) collective-permute-start(bf16[1,4,8,64,128]{4,3,2,1,0:T(8,128)(2,1)} %fusion.198), channel_id=1, source_target_pairs={{32,0},{64,32},{96,64},{128,96},{160,128},{192,160},{224,192},{256... | collective-permute-start | bytes 1572872 | tf_op jit(solution)/shard_map/while/body/eval_jaxpr/ppermute | solution.py:12
  332.6 2.5 copy-start.6
  335.1 24.4 %copy-start.3 = (f32[4,1,256,128]{3,2,1,0:T(8,128)S(1)}, f32[4,1,256,128]{3,2,1,0:T(8,128)}, u32[]{:S(2)}) copy-start(f32[4,1,256,128]{3,2,1,0:T(8,128)} %get-tuple-element.164) | copy-start | bytes 1572868
  335.1 26.3 %copy-start.8 = (f32[1,256,4,8]{1,3,2,0:T(8,128)S(1)}, f32[1,256,4,8]{1,3,2,0:T(8,128)}, u32[]{:S(2)}) copy-start(f32[1,256,4,8]{1,3,2,0:T(8,128)} %param.21) | copy-start | bytes 98308
  335.1 26.3 %copy-start.30 = (f32[4,8]{1,0:T(4,128)S(1)}, f32[4,8]{1,0:T(4,128)}, u32[]{:S(2)}) copy-start(f32[4,8]{1,0:T(4,128)} %param.23) | copy-start | bytes 388
  361.3 526.5 %reduce-scatter.5.cloned.1.call-start = ((), (), s32[]{:S(2)}) async-start(), calls=%async_computation.3 | async-start | bytes 327680 | tf_op jit(solution)/shard_map/reduce_scatter | solution.py:265
  361.4 4.1 copy-start.1
  361.4 4.1 copy-start.2
  361.4 4.1 copy-start.21
  361.4 4.1 copy-start.23
  361.4 4.1 copy-start.25
  370.5 2.8 copy-start.19
  370.5 3.5 copy-start.17
  370.5 508.2 %copy-start.12 = (f32[4,512]{1,0:T(4,128)S(1)}, f32[4,512]{1,0:T(4,128)}, u32[]{:S(2)}) copy-start(f32[4,512]{1,0:T(4,128)} %copy-done.11) | copy-start | bytes 24580
  370.5 508.2 %copy-start.14 = (f32[4,512]{1,0:T(4,128)S(1)}, f32[4,512]{1,0:T(4,128)}, u32[]{:S(2)}) copy-start(f32[4,512]{1,0:T(4,128)} %copy-done.13) | copy-start | bytes 24580
  370.5 508.2 %copy-start.16 = (f32[4,512]{1,0:T(4,128)S(1)}, f32[4,512]{1,0:T(4,128)}, u32[]{:S(2)}) copy-start(f32[4,512]{1,0:T(4,128)} %copy-done.15) | copy-start | bytes 24580
  370.5 508.2 %copy-start.26 = (pred[256]{0:T(512)(128)(4,1)S(1)}, pred[256]{0:T(512)(128)(4,1)}, u32[]{:S(2)}) copy-start(pred[256]{0:T(512)(128)(4,1)} %get-tuple-element.328) | copy-start | bytes 772
  370.5 508.2 %copy-start.27 = (pred[256]{0:T(512)(128)(4,1)S(1)}, pred[256]{0:T(512)(128)(4,1)}, u32[]{:S(2)}) copy-start(pred[256]{0:T(512)(128)(4,1)} %get-tuple-element.331) | copy-start | bytes 772
  370.5 508.2 %copy-start.28 = (pred[256]{0:T(512)(128)(4,1)S(1)}, pred[256]{0:T(512)(128)(4,1)}, u32[]{:S(2)}) copy-start(pred[256]{0:T(512)(128)(4,1)} %get-tuple-element.332) | copy-start | bytes 772
  370.9 507.4 %collective-permute-start.2 = (f32[1,3,4,512]{3,2,1,0:T(4,128)S(1)}, f32[1,3,4,512]{3,2,1,0:T(4,128)S(1)}, u32[]{:S(2)}, u32[]{:S(2)}) collective-permute-start(f32[1,3,4,512]{3,2,1,0:T(4,128)S(1)} %copy.111), channel_id=1, source_target_pairs={{32,0},{64,32},{96,64},{128,96},{160,128},{192,160},{224,192},{256... | collective-permute-start | bytes 73736 | tf_op jit(solution)/shard_map/ppermute | solution.py:12
  (5 other events, 11.5 us)
Sparse Core Ops, SparseCore 0:
  361.5 46.9 reduce-scatter.2
  411.5 28.0 reduce-scatter.4
where the time goes:
time: 906 us; the launch traced here: 896 us
  blocking collectives  504 us (56%)
  waiting for transfers between devices  185 us (20%)
  other arithmetic  85.8 us (9%)
  matrix products  55.5 us (6%)
  starting transfers between devices  25.7 us (3%)
  local copies, waits for them, and re-layouts  24.3 us (3%)
  between operations  14.5 us (2%)
    psum x1, blocking collectives, body(): lax.psum((grad_weight, grad_bias, grad_rate, grad_skip), ('context', 'dp'))  504 us
    ppermute x17, waiting for transfers between devices, passed_along(): return lax.ppermute(block, axis, route)  185 us
    dot_general x40, matrix products, mixed(): return jnp.einsum(form, left, right, preferred_element_type=jnp.float32)  52.9 us
    ppermute x17, starting transfers between devices, passed_along(): return lax.ppermute(block, axis, route)  25.7 us
  transfers between devices with their start and end apart: 19, of which 15 were waited for; matrix products, arithmetic and copies ran while one was open for 4% of the time, Pallas kernels for 0%

commit v1 on v0

v1 whole, which is shorter than its diff:
```python
import jax
import jax.numpy as jnp
from jax import lax
from jax.experimental import pallas as pl
from jax.experimental.pallas import tpu as pltpu
from jax.sharding import PartitionSpec as P

F32 = jnp.float32
BF16 = jnp.bfloat16
LOG2E = 1.4426950408889634
FULL = lax.Precision.HIGHEST
HEAD = 64
HALO = 8
EXTRA = 16
FAR = 1 << 28


def dot(a, b, dims=((1,), (0,)), precision=None):
    return lax.dot_general(a, b, (dims, ((), ())), precision=precision, preferred_element_type=F32)


NT = ((1,), (1,))
TN = ((0,), (0,))


def iota(shape, axis):
    return lax.broadcasted_iota(jnp.int32, shape, axis)


def doc_bounds(first, lengths, rows):
    pos = first + iota((1, rows), 1)
    low = jnp.zeros((1, rows), jnp.int32)
    high = jnp.full((1, rows), FAR, jnp.int32)
    start = jnp.int32(0)
    for d in range(lengths.shape[1]):
        low = jnp.where(pos >= start, start, low)
        start = start + lengths[0, d]
        high = jnp.minimum(high, jnp.where(start > pos, start - 1, FAR))
    return low, high


def per_head(values, group, shape):
    column = jnp.zeros(shape, F32)
    for h in range(shape[0]):
        column = jnp.where(iota(shape, 0) == h, values[group, h], column)
    return column


def running_log(step, rate):
    rows = step.shape[1]
    upto = (iota((rows, rows), 0) <= iota((rows, rows), 1)).astype(F32)
    return dot(step * (rate * (-LOG2E)), upto, precision=FULL)


def offset_kernel(first, lengths, rate, step, gy, cm, pay, gyt, rows_out):
    g = pl.program_id(0)
    rows = step.shape[2]
    heads = step.shape[1]
    low, high = doc_bounds(first[0], lengths, rows)
    cum = running_log(step[0], per_head(rate, g, (heads, rows)))
    from_start = jnp.where(low < first[0], jnp.exp2(cum), 0.0)
    last = jnp.broadcast_to(cum[:, rows - 1 :], (heads, rows))
    to_end = jnp.where(high >= first[0] + rows - 1, jnp.exp2(jnp.minimum(last - cum, 0.0)), 0.0)
    rows_out[0, 0] = cum
    rows_out[0, 1] = from_start
    rows_out[0, 2] = to_end
    gt = jnp.transpose(gy[0].astype(F32))
    gyt[0] = gt.astype(BF16)
    scaled = jnp.concatenate(
        [gt[h * HEAD : (h + 1) * HEAD] * from_start[h : h + 1] for h in range(heads)], axis=0
    ).astype(BF16)
    offset = dot(scaled, cm[0]).astype(BF16)
    through = jnp.broadcast_to(from_start[:, rows - 1 :], (heads, 128))
    upper = through.astype(BF16).astype(F32)
    lower = through - upper
    spot = iota((EXTRA, 128), 0)
    for e in range(heads // 2):
        pay[e, : 2 * HEAD] = offset[e * 2 * HEAD : (e + 1) * 2 * HEAD]
        extra = jnp.where(spot == 0, upper[2 * e : 2 * e + 1], 0.0)
        extra = jnp.where(spot == 1, lower[2 * e : 2 * e + 1], extra)
        extra = jnp.where(spot == 2, upper[2 * e + 1 : 2 * e + 2], extra)
        extra = jnp.where(spot == 3, lower[2 * e + 1 : 2 * e + 2], extra)
        pay[e, 2 * HEAD :] = extra.astype(BF16)


def scan_kernel(pay, out):
    blocks = pay.shape[0]
    state = jnp.zeros((2 * HEAD, 128), F32)
    out[blocks - 1] = state.astype(BF16)
    for k in range(blocks - 2, -1, -1):
        extra = pay[k + 1, 2 * HEAD :].astype(F32)
        one = jnp.broadcast_to(extra[0:1] + extra[1:2], (HEAD, 128))
        two = jnp.broadcast_to(extra[2:3] + extra[3:4], (HEAD, 128))
        through = jnp.concatenate([one, two], axis=0)
        state = through * state + pay[k + 1, : 2 * HEAD].astype(F32)
        out[k] = state.astype(BF16)


def intra_kernel(
    first, lengths, skip, x, halo, gy, gyt, bm, cm, step, rows_in, state, taps,
    lagged, conv, upd, slope, part, heads_out, gc, gb, acc, statec,
):
    g = pl.program_id(0)
    heads = step.shape[1]
    rows = step.shape[2]
    start = first[0]
    low, high = doc_bounds(start, lengths, rows)
    sub = iota((rows, rows), 0)
    lane = iota((rows, rows), 1)
    xt = jnp.transpose(x[0].astype(F32)).astype(BF16)
    lagged[0, 0] = xt
    hsub = iota((HALO, rows), 0)
    hlane = iota((HALO, rows), 1)
    for j in range(1, 4):
        here = ((sub + j == lane) & (sub + start >= low)).astype(BF16)
        away = ((hsub - HALO + j == hlane) & (hsub - HALO + start >= low)).astype(BF16)
        lagged[0, j] = (dot(xt, here) + dot(halo[0], away, TN)).astype(BF16)
    statec[...] = dot(state[0], cm[0], NT)
    gram = dot(cm[0], bm[0], NT)
    bias = jnp.where((sub >= lane) & (sub + start <= high), 0.0, -1e30)
    cum = rows_in[0, 0]
    cum_col = jnp.transpose(cum)
    acc[...] = jnp.zeros((rows, rows), F32)
    zero = jnp.zeros((HEAD, rows), BF16)
    spot = iota((heads, rows), 0)
    cum_out = jnp.zeros((heads, rows), F32)
    step_out = jnp.zeros((heads, rows), F32)
    skip_out = jnp.zeros((heads, rows), F32)
    for h in range(heads):
        at = slice(h * HEAD, (h + 1) * HEAD)
        w = taps[0, at]
        pre = w[:, 4:5] + w[:, 0:1] * lagged[0, 0, at].astype(F32)
        for j in range(1, 4):
            pre = pre + w[:, j : j + 1] * lagged[0, j, at].astype(F32)
        sig = 1.0 / (1.0 + jnp.exp(-pre))
        co = (pre * sig).astype(BF16)
        conv[0, at] = co
        slope[0, at] = sig * (1.0 + pre * (1.0 - sig))
        co = co.astype(F32)
        st = step[0, h : h + 1]
        u = (st * co).astype(BF16)
        upd[0, at] = u
        pair = gy[0, :, (h // 2) * 128 : (h // 2 + 1) * 128]
        both = jnp.concatenate([u, zero] if h % 2 == 0 else [zero, u], axis=0)
        score_grad = dot(pair, both)
        decay = jnp.exp2(cum_col[:, h : h + 1] - cum[h : h + 1] + bias)
        acc[...] += decay * score_grad
        score = (decay * gram).astype(BF16)
        gt = gyt[0, at]
        grad_u = dot(gt, score)
        y = dot(u, score, NT)
        gt = gt.astype(F32)
        row_sum = jnp.sum(gt * (y + rows_in[0, 1, h : h + 1] * statec[at]), axis=0, keepdims=True)
        col_sum = jnp.sum(u.astype(F32) * grad_u, axis=0, keepdims=True)
        cum_out = jnp.where(spot == h, row_sum - col_sum, cum_out)
        step_out = jnp.where(spot == h, jnp.sum(grad_u * co, axis=0, keepdims=True), step_out)
        skip_out = jnp.where(spot == h, jnp.sum(gt * co, axis=0, keepdims=True), skip_out)
        part[0, at] = st * grad_u + skip[g, h] * gt
    heads_out[0, 0] = cum_out
    heads_out[0, 1] = step_out
    heads_out[0, 2] = skip_out
    grad_gram = acc[...].astype(BF16)
    scaled = jnp.concatenate(
        [
            (gyt[0, h * HEAD : (h + 1) * HEAD].astype(F32) * rows_in[0, 1, h : h + 1]).astype(BF16)
            for h in range(heads)
        ],
        axis=0,
    )
    gc[0] = (dot(grad_gram, bm[0]) + dot(scaled, state[0], TN)).astype(BF16)
    gb[0] = dot(grad_gram, cm[0], TN)


def carry_kernel(
    rate, grad, bm, step, rows_in, heads_in, state, lagged, conv, slope, part,
    pay, grad_step, pre_out, edge, cols,
):
    g = pl.program_id(0)
    heads = step.shape[1]
    rows = step.shape[2]
    carry = dot(grad[0], bm[0], NT)
    spot = iota((heads, rows), 0)
    lane = iota((HEAD, 128), 1)
    to_end = rows_in[0, 2]
    along = jnp.zeros((heads, rows), F32)
    inner = jnp.zeros((heads, 128), F32)
    for h in range(heads):
        at = slice(h * HEAD, (h + 1) * HEAD)
        cb = carry[at]
        st = step[0, h : h + 1]
        along = jnp.where(spot == h, jnp.sum(cb * conv[0, at].astype(F32), axis=0, keepdims=True), along)
        prod = grad[0, at].astype(F32) * state[0, at].astype(F32)
        inner = jnp.where(
            iota((heads, 128), 0) == h, jnp.sum(prod, axis=0, keepdims=True), inner
        )
        gp = (part[0, at] + (st * to_end[h : h + 1]) * cb) * slope[0, at]
        pre_out[0, at] = gp.astype(BF16)
        out = jnp.where(lane == 12, jnp.sum(gp, axis=1, keepdims=True), gp[:, :128])
        for j in range(4):
            s = jnp.sum(gp * lagged[0, j, at].astype(F32), axis=1, keepdims=True)
            out = jnp.where(lane == 8 + j, s, out)
        cols[at] = out
    along = along * to_end
    step_two = along
    along = along * step[0]
    through = rows_in[0, 1][:, rows - 1 :]
    last = jnp.sum(along, axis=1, keepdims=True) + through * jnp.sum(inner, axis=1, keepdims=True)
    grad_cum = heads_in[0, 0] - along + jnp.where(iota((heads, rows), 1) == rows - 1, last, 0.0)
    back = (iota((rows, rows), 0) >= iota((rows, rows), 1)).astype(F32)
    grad_log = dot(grad_cum, back, precision=FULL)
    grad_step[0] = heads_in[0, 1] + step_two - per_head(rate, g, (heads, rows)) * grad_log
    lane = iota((heads, 128), 1)
    rate_grad = -jnp.sum(step[0] * grad_log, axis=1, keepdims=True)
    skip_grad = jnp.sum(heads_in[0, 2], axis=1, keepdims=True)
    top = cols[:heads]
    top = jnp.where(lane == 13, rate_grad, top)
    cols[:heads] = jnp.where(lane == 14, skip_grad, top)
    turned = jnp.transpose(cols[...])
    edge[0] = turned[:HALO].astype(BF16)
    pay[0] = turned[8:16]


def grad_b_kernel(rows_in, upd, grad, gb, out):
    heads = rows_in.shape[2]
    scaled = jnp.concatenate(
        [
            (upd[0, h * HEAD : (h + 1) * HEAD].astype(F32) * rows_in[0, 2, h : h + 1]).astype(BF16)
            for h in range(heads)
        ],
        axis=0,
    )
    out[0] = (gb[0] + dot(scaled, grad[0], TN)).astype(BF16)


def input_kernel(first, lengths, pre, right, taps, out):
    rows = pre.shape[2]
    start = first[0]
    _, high = doc_bounds(start, lengths, rows)
    sub = iota((rows, rows), 0)
    lane = iota((rows, rows), 1)
    hsub = iota((HALO, rows), 0)
    hlane = iota((HALO, rows), 1)
    w = taps[0]
    total = w[:, 0:1] * pre[0].astype(F32)
    for j in range(1, 4):
        here = ((sub == lane + j) & (sub + start <= high)).astype(BF16)
        away = ((hsub + rows == hlane + j) & (hsub + rows + start <= high)).astype(BF16)
        total = total + w[:, j : j + 1] * (dot(pre[0], here) + dot(right[0], away, TN))
    out[0] = jnp.transpose(total).astype(BF16)


def sum_kernel(parts, out):
    total = parts[0].astype(F32)
    for i in range(1, parts.shape[0]):
        total = total + parts[i].astype(F32)
    out[...] = total.astype(out.dtype)


def call(kernel, grid, ins, outs, args, flops=0, nbytes=0, scratch=()):
    smem = pl.BlockSpec(memory_space=pltpu.SMEM)

    def spec(shape, blocked):
        if blocked is None:
            return smem
        if not blocked or not grid:
            return pl.BlockSpec(shape, lambda *i: (0,) * len(shape))
        return pl.BlockSpec(
            (shape[0] // grid[0],) + tuple(shape[1:]), lambda g: (g,) + (0,) * (len(shape) - 1)
        )

    return pl.pallas_call(
        kernel,
        grid=grid,
        in_specs=[spec(a.shape, b) for a, b in zip(args, ins)],
        out_specs=[spec(s, True) for s, _ in outs],
        out_shape=[jax.ShapeDtypeStruct(s, t) for s, t in outs],
        scratch_shapes=list(scratch),
        cost_estimate=pl.CostEstimate(flops=flops, bytes_accessed=nbytes, transcendentals=0),
        compiler_params=pltpu.CompilerParams(vmem_limit_bytes=48 * 1024 * 1024),
    )(*args)


def shifted(block, axis, distance):
    size = lax.axis_size(axis)
    route = [(i, i + distance) for i in range(size) if 0 <= i + distance < size]
    return lax.ppermute(block, axis, route)


def body(
    conv_input,
    output_grad,
    b_matrix,
    c_matrix,
    step_size,
    decay_rate,
    skip_gain,
    conv_weight,
    conv_bias,
    saved_state,
    doc_lengths,
):
    _, rows, groups, features = conv_input.shape
    heads = step_size.shape[3]
    blocks = lax.axis_size("context")
    first = (lax.axis_index("context") * rows).astype(jnp.int32).reshape(1)
    x = jnp.transpose(conv_input[0], (1, 0, 2))
    gy = jnp.transpose(output_grad[0], (1, 0, 2))
    bm = jnp.transpose(b_matrix[0], (1, 0, 2))
    cm = jnp.transpose(c_matrix[0], (1, 0, 2))
    step = jnp.transpose(step_size[0], (1, 2, 0))
    state = saved_state.reshape(groups, features, 128)
    taps = jnp.concatenate(
        [
            jnp.transpose(conv_weight, (1, 2, 0)),
            conv_bias[:, :, None],
            jnp.zeros((groups, features, 3), F32),
        ],
        axis=2,
    )
    halo = shifted(conv_input[0, rows - HALO :], "context", 1)
    halo = jnp.transpose(halo, (1, 0, 2))

    wide = (groups, features, rows)
    pay, gyt, rows_in = call(
        offset_kernel,
        (groups,),
        [None, None, None, True, True, True],
        [
            ((groups * heads // 2, 2 * HEAD + EXTRA, 128), BF16),
            (wide, BF16),
            ((groups, 3, heads, rows), F32),
        ],
        (first, doc_lengths, decay_rate, step, gy, cm),
        flops=10**9,
        nbytes=4 * 10**6,
    )
    own = groups * heads // 2 // blocks
    gathered = lax.all_to_all(pay, "context", 0, 0, tiled=True)
    lagged, conv, upd, slope, part, heads_in, gc, gb = call(
        intra_kernel,
        (groups,),
        [None, None, None] + [True] * 10,
        [
            ((groups, 4, features, rows), BF16),
            (wide, BF16),
            (wide, BF16),
            (wide, F32),
            (wide, F32),
            ((groups, 3, heads, rows), F32),
            ((groups, rows, 128), BF16),
            ((groups, rows, 128), F32),
        ],
        (first, doc_lengths, skip_gain, x, halo, gy, gyt, bm, cm, step, rows_in, state, taps),
        flops=20 * 10**9,
        nbytes=20 * 10**6,
        scratch=(pltpu.VMEM((rows, rows), F32), pltpu.VMEM((features, rows), F32)),
    )
    (scanned,) = call(
        scan_kernel,
        (),
        [True],
        [((blocks * own, 2 * HEAD, 128), BF16)],
        (gathered,),
        flops=10**7,
        nbytes=10**6,
    )
    grad = lax.all_to_all(scanned, "context", 0, 0, tiled=True).reshape(groups, features, 128)
    grad_c = lax.psum_scatter(gc, "tensor", scatter_dimension=0, tiled=True).astype(F32)
    sums, grad_step, pre, edge = call(
        carry_kernel,
        (groups,),
        [None] + [True] * 10,
        [
            ((groups, 8, features), F32),
            ((groups, heads, rows), F32),
            (wide, BF16),
            ((groups, HALO, features), BF16),
        ],
        (decay_rate, grad, bm, step, rows_in, heads_in, state, lagged, conv, slope, part),
        flops=10**9,
        nbytes=20 * 10**6,
        scratch=(pltpu.VMEM((features, 128), F32),),
    )
    copies = lax.axis_size("dp")
    shares = jnp.broadcast_to(sums.astype(BF16)[None], (copies,) + sums.shape)
    shares = lax.all_to_all(shares, "dp", 0, 0, tiled=True)
    (sums,) = call(sum_kernel, (), [True], [(sums.shape, BF16)], (shares,))
    shares = jnp.broadcast_to(sums[None], (blocks,) + sums.shape)
    shares = lax.all_to_all(shares, "context", 0, 0, tiled=True)
    (sums,) = call(sum_kernel, (), [True], [(sums.shape, F32)], (shares,))

    (gb,) = call(
        grad_b_kernel,
        (groups,),
        [True] * 4,
        [((groups, rows, 128), BF16)],
        (rows_in, upd, grad, gb),
        flops=10**8,
        nbytes=2 * 10**6,
    )
    parts = lax.axis_size("tensor")
    here = groups // parts
    gb = lax.all_to_all(gb, "tensor", 0, 0, tiled=True).reshape(parts, here * rows, 128)
    (grad_b,) = call(sum_kernel, (), [True], [((here * rows, 128), F32)], (gb,))

    right = shifted(edge, "context", -1)
    (grad_input,) = call(
        input_kernel,
        (groups,),
        [None, None] + [True] * 3,
        [((groups, rows, features), BF16)],
        (first, doc_lengths, pre, right, taps),
        flops=10**9,
        nbytes=4 * 10**6,
    )
    return (
        jnp.transpose(grad_input, (1, 0, 2))[None],
        jnp.transpose(grad_b.reshape(1, here, rows, 128), (0, 2, 1, 3)),
        jnp.transpose(grad_c.reshape(1, here, rows, 128), (0, 2, 1, 3)),
        jnp.transpose(grad_step, (2, 0, 1))[None],
        jnp.transpose(sums[:, :4], (1, 0, 2)),
        sums[:, 4],
        sums[:, 5, :heads],
        sums[:, 6, :heads],
    )


def solution(mesh):
    return jax.shard_map(
        body,
        mesh=mesh,
        in_specs=(
            P("dp", "context", None, "tensor"),
            P("dp", "context", None, "tensor"),
            P("dp", "context", None, None),
            P("dp", "context", None, None),
            P("dp", "context", None, "tensor"),
            P(None, "tensor"),
            P(None, "tensor"),
            P(None, None, "tensor"),
            P(None, "tensor"),
            P("dp", "context", None, "tensor", None, None),
            P("dp", None),
        ),
        out_specs=(
            P("dp", "context", None, "tensor"),
            P("dp", "context", "tensor", None),
            P("dp", "context", "tensor", None),
            P("dp", "context", None, "tensor"),
            P(None, None, "tensor"),
            P(None, "tensor"),
            P(None, "tensor"),
            P(None, "tensor"),
        ),
        check_vma=False,
    )
```

time: 906 us -> 188 us (0.21)
  blocking collectives: 504 us -> 0 us
  waiting for transfers between devices: 185 us -> 62.2 us
  other arithmetic: 85.8 us -> 4.13 us
  matrix products: 55.5 us -> 0 us
  starting transfers between devices: 25.7 us -> 55.1 us
  Pallas kernels: 0 us -> 28.3 us
    psum x1 -> x0, blocking collectives: 504 us -> none  [body(): lax.psum((grad_weight, grad_bias, grad_rate, grad_skip), ('context', 'dp'))]
    ppermute x17 -> x2, waiting for transfers between devices: 185 us -> 0.01 us  [shifted(): return lax.ppermute(block, axis, route)]
    dot_general x42 -> x0, matrix products: 55.5 us -> none  [the longest x40 52.9 us: mixed(): return jnp.einsum(form, left, right, preferred_element_type=jnp.float32)]
    all_to_all x0 -> x5, starting transfers between devices: none -> 50.5 us  [the longest x1 15.9 us: body(): gathered = lax.all_to_all(pay, 'context', 0, 0, tiled=True)]
    convert_element_type x34 -> x1, other arithmetic: 42 us -> 0.01 us  [body(): shares = jnp.broadcast_to(sums.astype(BF16)[None], (copies,) + sums.shape)]
    all_to_all x0 -> x5, waiting for transfers between devices: none -> 33.7 us  [the longest x1 19.4 us: body(): gathered = lax.all_to_all(pay, 'context', 0, 0, tiled=True)]
    pallas_call x0 -> x9, Pallas kernels: none -> 28.3 us  [call(): pl.pallas_call(kernel, grid=grid, in_specs=[spec(a.shape, b) for a, b in...]
    reduce_scatter x2 -> x1, waiting for transfers between devices: 0.01 us -> 27.8 us  [body(): lax.psum_scatter(gc, 'tensor', scatter_dimension=0, tiled=True).astype(F32)]
  transfers between devices with their start and end apart: 19 -> 8, of which waited for: 15 -> 5; matrix products, arithmetic and copies ran while one was open for 4% -> 5% of each run, Pallas kernels for 0% -> 10%
where the time goes in v1:
time: 188 us; the launch traced here: 186 us
  waiting for transfers between devices  62.2 us (33%)
  starting transfers between devices  55.1 us (29%)
  Pallas kernels  28.3 us (15%)
  local copies, waits for them, and re-layouts  21.9 us (12%)
  between operations  14.3 us (8%)
  other arithmetic  4.13 us (2%)
    pallas_call x9, Pallas kernels, call(): pl.pallas_call(kernel, grid=grid, in_specs=[spec(a.shape, b) for a, b in...  28.3 us
    reduce_scatter x1, waiting for transfers between devices, body(): lax.psum_scatter(gc, 'tensor', scatter_dimension=0, tiled=True).astype(F32)  27.8 us
    all_to_all x1, waiting for transfers between devices, body(): gathered = lax.all_to_all(pay, 'context', 0, 0, tiled=True)  19.4 us
    unnamed x62, local copies, waits for them, and re-layouts  17.7 us
    all_to_all x1, starting transfers between devices, body(): gathered = lax.all_to_all(pay, 'context', 0, 0, tiled=True)  15.9 us
    all_to_all x1, starting transfers between devices, body(): lax.all_to_all(scanned, 'context', 0, 0, tiled=True)  13 us
    all_to_all x1, starting transfers between devices, body(): shares = lax.all_to_all(shares, 'dp', 0, 0, tiled=True)  11.4 us
    all_to_all x1, waiting for transfers between devices, body(): lax.all_to_all(scanned, 'context', 0, 0, tiled=True)  6.37 us
  transfers between devices with their start and end apart: 8, of which 5 were waited for; matrix products, arithmetic and copies ran while one was open for 5% of the time, Pallas kernels for 10%

profile of v1, /device:TPU:1, one launch (start us, length us, event | category | flops | bytes accessed | tf_op | source)
XLA Modules:
  0.0 186.0 jit_solution(6430404576580002292)
XLA Ops:
  7.2 1.0 copy.73
  8.2 1.5 copy.71
  9.8 3.6 %shard_map.170 = (bf16[16,144,128]{2,1,0:T(8,128)(2,1)}, bf16[4,512,256]{2,1,0:T(8,128)(2,1)S(1)}, f32[4,3,8,256]{3,2,1,0:T(8,128)S(1)}) custom-call(s32[1]{0:T(128)} %bitcast.first, s32[1,6]{1,0:T(1,128)S(1)} %copy-done.21, f32[4,8]{1,0:T(4,128)S(1)} %copy-done.17, f32[4,8,256]{2,1,0:T(8,128)S(1)} %bitcast.62, bf16[4,256,512]{2,1,0:T(8,128)(2,1)S(1)} %bitcast.55, ...), custom_call_target="tpu_custom_call" | custom-call | flops 1000000000 | bytes 4000000 | tf_op jit(solution)/shard_map/pallas_call | solution.py:271
  13.4 0.6 copy-done.8
  14.0 1.0 copy-done.22
  15.0 15.9 %all-to-all-start = ((bf16[16,144,128]{2,1,0:T(8,128)(2,1)}), bf16[16,144,128]{2,1,0:T(8,128)(2,1)S(1)}, u32[]{:S(2)}, u32[]{:S(2)}) async-start(bf16[16,144,128]{2,1,0:T(8,128)(2,1)} %get-tuple-element.23), calls=%async_computation | async-start | bytes 1179648 | tf_op jit(solution)/shard_map/all_to_all | solution.py:338
  30.9 0.2 copy.75
  31.1 0.6 slice_bitcast_fusion.1
  31.7 3.3 %collective-permute-start = (bf16[8,4,512]{2,0,1:T(8,128)(2,1)}, bf16[8,4,512]{2,0,1:T(8,128)(2,1)S(1)}, u32[]{:S(2)}, u32[]{:S(2)}) collective-permute-start(bf16[8,4,512]{2,0,1:T(8,128)(2,1)} %slice_bitcast_fusion.1), channel_id=1, source_target_pairs={{0,32},{32,64},{64,96},{96,128},{128,160},{160,192},{192,224},{224... | collective-permute-start | bytes 98312 | tf_op jit(solution)/shard_map/ppermute | solution.py:286
  35.0 0.4 copy.58
  35.4 1.4 copy.59
  36.8 0.1 pad.2.clone
  36.8 19.4 %all-to-all-done.pay = bf16[16,144,128]{2,1,0:T(8,128)(2,1)S(1)} async-done(((bf16[16,144,128]{2,1,0:T(8,128)(2,1)}), bf16[16,144,128]{2,1,0:T(8,128)(2,1)S(1)}, u32[]{:S(2)}, u32[]{:S(2)}) %all-to-all-start) | async-done | bytes 589856 | tf_op jit(solution)/shard_map/all_to_all | solution.py:338
  56.2 0.9 shard_map.171
  57.1 13.0 %all-to-all-start.1 = ((bf16[16,128,128]{2,1,0:T(8,128)(2,1)}), bf16[16,128,128]{2,1,0:T(8,128)(2,1)S(1)}, u32[]{:S(2)}, u32[]{:S(2)}) async-start(bf16[16,128,128]{2,1,0:T(8,128)(2,1)} %shard_map.171), calls=%async_computation.1 | async-start | bytes 1048576 | tf_op jit(solution)/shard_map/all_to_all | solution.py:367
  70.2 2.6 %maximum_maximum_fusion.taps = f32[4,512,8]{2,1,0:T(8,128)} fusion(f32[4,512,1]{2,1,0:T(8,128)} %copy.59, f32[4,512,4]{2,1,0:T(8,128)S(1)} %bitcast.66, f32[8]{0:T(128)S(1)} %pad.2.clone), kind=kLoop, calls=%fused_computation | loop fusion | flops 32768 | bytes 106528 | tf_op jit(solution)/shard_map/concatenate | solution.py:312
  72.9 11.3 %shard_map.172 = (bf16[4,4,512,256]{3,2,1,0:T(8,128)(2,1)}, bf16[4,512,256]{2,1,0:T(8,128)(2,1)S(1)}, bf16[4,512,256]{2,1,0:T(8,128)(2,1)S(1)}, f32[4,512,256]{2...) custom-call(s32[1]{0:T(128)} %bitcast.first, ...), custom_call_target="tpu_custom_call" | custom-call | flops 20000000000 | bytes 20000000 | tf_op jit(solution)/shard_map/pallas_call | solution.py:271
  84.2 1.0 copy-done.1
  85.1 0.8 copy-done.6
  85.9 0.6 copy-done.14
  86.6 6.4 %all-to-all-done.1 = bf16[16,128,128]{2,1,0:T(8,128)(2,1)S(1)} async-done(((bf16[16,128,128]{2,1,0:T(8,128)(2,1)}), bf16[16,128,128]{2,1,0:T(8,128)(2,1)S(1)}, u32[]{:S(2)}, u32[]{:S(2)}) %all-to-all-start.1) | async-done | bytes 524320 | tf_op jit(solution)/shard_map/all_to_all | solution.py:367
  93.0 1.6 copy-done
  94.5 0.9 copy-done.10
  95.4 0.9 copy-done.15
  96.3 6.2 %shard_map.173 = (f32[4,8,512]{2,1,0:T(8,128)S(1)}, f32[4,8,256]{2,1,0:T(8,128)}, bf16[4,512,256]{2,1,0:T(8,128)(2,1)S(1)}, bf16[4,8,512]{2,1,0:T(8,128)(2,1)S(1)}) custom-call(f32[4,8]{1,0:T(4,128)S(1)} %copy-done.17, bf16[4,512,128]{2,1,0:T(8,128)(2,1)S(1)} %bitcast.50, bf16[4,256,128]{2,1,0:T(8,128)(2,1)S(1)} %bitcast.54, f32[4,8,256]{2,1,0:T(8,128)S(1)} %bitcast.64, ...), custom_call_target="tpu_custom_call" | custom-call | flops 1000000000 | bytes 20000000 | tf_op jit(solution)/shard_map/pallas_call | solution.py:271
  102.6 1.0 copy-done.18
  103.5 0.7 broadcast_in_dim.28
  104.3 11.4 %all-to-all-start.3 = ((bf16[8,4,8,512]{3,2,1,0:T(8,128)(2,1)}), bf16[8,4,8,512]{3,2,1,0:T(8,128)(2,1)S(1)}, u32[]{:S(2)}, u32[]{:S(2)}) async-start(bf16[8,4,8,512]{3,2,1,0:T(8,128)(2,1)} %broadcast_in_dim.28), calls=%async_computation.4 | async-start | bytes 524288 | tf_op jit(solution)/shard_map/all_to_all | solution.py:386
  115.7 1.0 copy-done.7
  116.7 0.9 copy-done.11
  117.6 2.1 %shard_map.175 = bf16[4,256,128]{2,1,0:T(8,128)(2,1)} custom-call(f32[4,3,8,256]{3,2,1,0:T(8,128)S(1)} %copy-done.11, bf16[4,512,256]{2,1,0:T(8,128)(2,1)S(1)} %copy-done.2, bf16[4,512,128]{2,1,0:T(8,128)(2,1)S(1)} %bitcast.51, f32[4,256,128]{2,1,0:T(8,128)S(1)} %copy-done.7), custom_call_target="tpu_custom_call" | custom-call | flops 100000000 | bytes 2000000 | tf_op jit(solution)/shard_map/pallas_call | solution.py:271
  119.7 2.5 %all-to-all-done.3.parts = bf16[8,4,8,512]{3,2,1,0:T(8,128)(2,1)S(1)} async-done(((bf16[8,4,8,512]{3,2,1,0:T(8,128)(2,1)}), bf16[8,4,8,512]{3,2,1,0:T(8,128)(2,1)S(1)}, u32[]{:S(2)}, u32[]{:S(2)}) %all-to-all-start.3) | async-done | bytes 262176 | tf_op jit(solution)/shard_map/all_to_all | solution.py:386
  122.2 4.2 %all-to-all-start.2 = ((bf16[4,256,128]{2,1,0:T(8,128)(2,1)}), bf16[4,256,128]{2,1,0:T(8,128)(2,1)S(1)}, u32[]{:S(2)}, u32[]{:S(2)}) async-start(bf16[4,256,128]{2,1,0:T(8,128)(2,1)} %shard_map.175), calls=%async_computation.2 | async-start | bytes 524288 | tf_op jit(solution)/shard_map/all_to_all | solution.py:403
  126.4 5.5 %all-to-all-done.2.parts = bf16[4,256,128]{2,1,0:T(8,128)(2,1)S(1)} async-done(((bf16[4,256,128]{2,1,0:T(8,128)(2,1)}), bf16[4,256,128]{2,1,0:T(8,128)(2,1)S(1)}, u32[]{:S(2)}, u32[]{:S(2)}) %all-to-all-start.2) | async-done | bytes 262176 | tf_op jit(solution)/shard_map/all_to_all | solution.py:403
  131.9 0.8 broadcast_in_dim.29
  132.7 6.1 %all-to-all-start.4 = ((bf16[16,4,8,512]{3,2,1,0:T(8,128)(2,1)}), bf16[16,4,8,512]{3,2,1,0:T(8,128)(2,1)S(1)}, u32[]{:S(2)}, u32[]{:S(2)}) async-start(bf16[16,4,8,512]{3,2,1,0:T(8,128)(2,1)} %broadcast_in_dim.29), calls=%async_computation.5 | async-start | bytes 1048576 | tf_op jit(solution)/shard_map/all_to_all | solution.py:389
  138.9 0.7 reduce-scatter.2.cloned.1.call-update
  139.6 1.3 collective-permute-start.1
  140.9 27.8 %reduce-scatter.2.cloned.1.call-done = bf16[1,256,128]{2,1,0:T(8,128)(2,1)} async-done(((bf16[4,256,128]{2,1,0:T(8,128)(2,1)}), bf16[1,256,128]{2,1,0:T(8,128)(2,1)}) %reduce-scatter.2.cloned.1.call-update) | async-done | bytes 65552 | tf_op jit(solution)/shard_map/reduce_scatter | solution.py:368
  168.6 1.5 bitcast_convert_fusion
  170.2 1.2 copy-done.19
  171.4 3.4 %shard_map.174 = bf16[4,256,512]{2,1,0:T(8,128)(2,1)S(1)} custom-call(s32[1]{0:T(128)} %bitcast.first, s32[1,6]{1,0:T(1,128)S(1)} %copy-done.21, bf16[4,512,256]{2,1,0:T(8,128)(2,1)S(1)} %copy-done.19, bf16[4,8,512]{2,1,0:T(8,128)(2,1)S(1)} %collective-permute-done.1.right, f32[4,512,8]{2,1,0:T(8,128)S(1)} %copy-done.3), custom_call_target="tpu_custom_call" | custom-call | flops 1000000000 | bytes 4000000 | tf_op jit(solution)/shard_map/pallas_call | solution.py:271
  174.8 1.8 copy.60
  176.5 0.7 shard_map.176
  177.2 0.1 shard_map.178
  177.3 0.6 fusion.1
  177.9 0.6 copy.63
  178.6 0.6 copy.74
  (52 shorter events, 0.2 us)
Async XLA Ops:
  7.2 2.6 %copy-start.21 = (s32[1,6]{1,0:T(1,128)S(1)}, s32[1,6]{1,0:T(1,128)}, u32[]{:S(2)}) copy-start(s32[1,6]{1,0:T(1,128)} %lengths.5) | copy-start | bytes 76
  7.2 2.6 %copy-start.17 = (f32[4,8]{1,0:T(4,128)S(1)}, f32[4,8]{1,0:T(4,128)}, u32[]{:S(2)}) copy-start(f32[4,8]{1,0:T(4,128)} %rate.3) | copy-start | bytes 388
  7.2 2.6 %copy-start.16 = (f32[1,256,4,8]{1,3,2,0:T(8,128)S(1)}, f32[1,256,4,8]{1,3,2,0:T(8,128)}, u32[]{:S(2)}) copy-start(f32[1,256,4,8]{1,3,2,0:T(8,128)} %param.15) | copy-start | bytes 98308
  8.2 5.2 %copy-start.12 = (bf16[1,256,4,128]{3,1,2,0:T(8,128)(2,1)}, bf16[1,256,4,128]{3,1,2,0:T(8,128)(2,1)S(1)}, u32[]{:S(2)}) copy-start(bf16[1,256,4,128]{3,1,2,0:T(8,128)(2,1)S(1)} %copy.73) | copy-start | bytes 786436
  9.7 5.3 %copy-start.4 = (bf16[1,256,4,512]{3,1,2,0:T(8,128)(2,1)}, bf16[1,256,4,512]{3,1,2,0:T(8,128)(2,1)S(1)}, u32[]{:S(2)}) copy-start(bf16[1,256,4,512]{3,1,2,0:T(8,128)(2,1)S(1)} %copy.71) | copy-start | bytes 3145732
  9.8 21.1 %copy-start.23 = (bf16[1,256,4,512]{3,2,1,0:T(4,128)(2,1)S(1)}, bf16[1,256,4,512]{3,2,1,0:T(4,128)(2,1)}, u32[]{:S(2)}) copy-start(bf16[1,256,4,512]{3,2,1,0:T(4,128)(2,1)} %param.11) | copy-start | bytes 3145732
  13.4 0.6 copy-start.8
  14.0 1.0 copy-start.22
  15.0 20.0 %copy-start.25 = (f32[4,4,512]{2,1,0:T(4,128)S(1)}, f32[4,4,512]{2,1,0:T(4,128)}, u32[]{:S(2)}) copy-start(f32[4,4,512]{2,1,0:T(4,128)} %param.18) | copy-start | bytes 98308
  15.0 20.4 %copy-start.26 = (f32[4,512]{1,0:T(4,128)S(1)}, f32[4,512]{1,0:T(4,128)}, u32[]{:S(2)}) copy-start(f32[4,512]{1,0:T(4,128)} %param.19) | copy-start | bytes 24580
  15.0 41.2 %all-to-all-start = ((bf16[16,144,128]{2,1,0:T(8,128)(2,1)}), bf16[16,144,128]{2,1,0:T(8,128)(2,1)S(1)}, u32[]{:S(2)}, u32[]{:S(2)}) async-start(bf16[16,144,128]{2,1,0:T(8,128)(2,1)} %get-tuple-element.23), calls=%async_computation | async-start | bytes 1179648 | tf_op jit(solution)/shard_map/all_to_all | solution.py:338
  31.7 41.1 %collective-permute-start = (bf16[8,4,512]{2,0,1:T(8,128)(2,1)}, bf16[8,4,512]{2,0,1:T(8,128)(2,1)S(1)}, u32[]{:S(2)}, u32[]{:S(2)}) collective-permute-start(bf16[8,4,512]{2,0,1:T(8,128)(2,1)} %slice_bitcast_fusion.1), channel_id=1, source_target_pairs={{0,32},{32,64},{64,96},{96,128},{128,160},{160,192},{192,224},{224... | collective-permute-start | bytes 98312 | tf_op jit(solution)/shard_map/ppermute | solution.py:286
  57.1 35.8 %all-to-all-start.1 = ((bf16[16,128,128]{2,1,0:T(8,128)(2,1)}), bf16[16,128,128]{2,1,0:T(8,128)(2,1)S(1)}, u32[]{:S(2)}, u32[]{:S(2)}) async-start(bf16[16,128,128]{2,1,0:T(8,128)(2,1)} %shard_map.171), calls=%async_computation.1 | async-start | bytes 1048576 | tf_op jit(solution)/shard_map/all_to_all | solution.py:367
  70.1 2.7 %copy-start.24 = (bf16[1,256,4,128]{3,2,1,0:T(4,128)(2,1)S(1)}, bf16[1,256,4,128]{3,2,1,0:T(4,128)(2,1)}, u32[]{:S(2)}) copy-start(bf16[1,256,4,128]{3,2,1,0:T(4,128)(2,1)} %param.13) | copy-start | bytes 786436
  70.1 2.7 %copy-start.5 = (bf16[1,1,4,8,64,128]{5,4,3,2,1,0:T(8,128)(2,1)S(1)}, bf16[1,1,4,8,64,128]{5,4,3,2,1,0:T(8,128)(2,1)}, u32[]{:S(2)}) copy-start(bf16[1,1,4,8,64,128]{5,4,3,2,1,0:T(8,128)(2,1)} %param.20) | copy-start | bytes 1572868
  70.1 2.7 %copy-start.9 = (f32[4,3,8,256]{3,2,1,0:T(8,128)S(1)}, f32[4,3,8,256]{3,2,1,0:T(8,128)}, u32[]{:S(2)}) copy-start(f32[4,3,8,256]{3,2,1,0:T(8,128)} %copy-done.8) | copy-start | bytes 294916
  70.1 2.7 %copy-start.13 = (bf16[1,256,4,128]{3,1,2,0:T(8,128)(2,1)S(1)}, bf16[1,256,4,128]{3,1,2,0:T(8,128)(2,1)}, u32[]{:S(2)}) copy-start(bf16[1,256,4,128]{3,1,2,0:T(8,128)(2,1)} %copy-done.12) | copy-start | bytes 786436
  70.2 2.7 %copy-start.20 = (f32[4,8]{1,0:T(4,128)S(1)}, f32[4,8]{1,0:T(4,128)}, u32[]{:S(2)}) copy-start(f32[4,8]{1,0:T(4,128)} %skip.1) | copy-start | bytes 388
  84.2 1.0 copy-start.1
  85.1 0.8 copy-start.6
  85.9 0.6 copy-start.14
  93.0 1.6 copy-start
  94.5 0.9 copy-start.10
  95.4 0.9 copy-start.15
  96.3 19.3 %copy-start.2 = (bf16[4,512,256]{2,1,0:T(8,128)(2,1)S(1)}, bf16[4,512,256]{2,1,0:T(8,128)(2,1)}, u32[]{:S(2)}) copy-start(bf16[4,512,256]{2,1,0:T(8,128)(2,1)} %copy-done.1) | copy-start | bytes 3145732
  102.6 1.0 copy-start.18
  104.3 17.9 %all-to-all-start.3 = ((bf16[8,4,8,512]{3,2,1,0:T(8,128)(2,1)}), bf16[8,4,8,512]{3,2,1,0:T(8,128)(2,1)S(1)}, u32[]{:S(2)}, u32[]{:S(2)}) async-start(bf16[8,4,8,512]{3,2,1,0:T(8,128)(2,1)} %broadcast_in_dim.28), calls=%async_computation.4 | async-start | bytes 524288 | tf_op jit(solution)/shard_map/all_to_all | solution.py:386
  115.7 1.0 copy-start.7
  116.7 0.9 copy-start.11
  117.6 52.6 %copy-start.3 = (f32[4,512,8]{2,1,0:T(8,128)S(1)}, f32[4,512,8]{2,1,0:T(8,128)}, u32[]{:S(2)}) copy-start(f32[4,512,8]{2,1,0:T(8,128)} %maximum_maximum_fusion.taps) | copy-start | bytes 196612
  122.2 9.7 %all-to-all-start.2 = ((bf16[4,256,128]{2,1,0:T(8,128)(2,1)}), bf16[4,256,128]{2,1,0:T(8,128)(2,1)S(1)}, u32[]{:S(2)}, u32[]{:S(2)}) async-start(bf16[4,256,128]{2,1,0:T(8,128)(2,1)} %shard_map.175), calls=%async_computation.2 | async-start | bytes 524288 | tf_op jit(solution)/shard_map/all_to_all | solution.py:403
  132.7 44.5 %all-to-all-start.4 = ((bf16[16,4,8,512]{3,2,1,0:T(8,128)(2,1)}), bf16[16,4,8,512]{3,2,1,0:T(8,128)(2,1)S(1)}, u32[]{:S(2)}, u32[]{:S(2)}) async-start(bf16[16,4,8,512]{3,2,1,0:T(8,128)(2,1)} %broadcast_in_dim.29), calls=%async_computation.5 | async-start | bytes 1048576 | tf_op jit(solution)/shard_map/all_to_all | solution.py:389
  138.8 29.8 %reduce-scatter.2.cloned.1.call-start = ((), (), s32[]{:S(2)}) async-start(), calls=%async_computation.6 | async-start | bytes 327680 | tf_op jit(solution)/shard_map/reduce_scatter | solution.py:368
  139.6 30.6 %collective-permute-start.1 = (bf16[4,8,512]{2,1,0:T(8,128)(2,1)S(1)}, bf16[4,8,512]{2,1,0:T(8,128)(2,1)S(1)}, u32[]{:S(2)}, u32[]{:S(2)}) collective-permute-start(bf16[4,8,512]{2,1,0:T(8,128)(2,1)S(1)} %get-tuple-element.32), channel_id=1, source_target_pairs={{32,0},{64,32},{96,64},{128,96},{160,128},{192,160},{224,192},{256... | collective-permute-start | bytes 98312 | tf_op jit(solution)/shard_map/ppermute | solution.py:286
  170.2 1.2 copy-start.19
Sparse Core Ops, SparseCore 0:
  142.5 26.1 reduce-scatter.1

commit v2 on v1

--- a/solution.py
+++ b/solution.py
@@ -83,7 +83,7 @@
         pay[e, 2 * HEAD :] = extra.astype(BF16)
 
 
-def scan_kernel(pay, out):
+def scan_kernel(pay, after, out):
     blocks = pay.shape[0]
     state = jnp.zeros((2 * HEAD, 128), F32)
     out[blocks - 1] = state.astype(BF16)
@@ -96,15 +96,11 @@
         out[k] = state.astype(BF16)
 
 
-def intra_kernel(
-    first, lengths, skip, x, halo, gy, gyt, bm, cm, step, rows_in, state, taps,
-    lagged, conv, upd, slope, part, heads_out, gc, gb, acc, statec,
-):
-    g = pl.program_id(0)
+def conv_kernel(first, lengths, x, halo, step, taps, lagged, conv, upd, slope):
     heads = step.shape[1]
     rows = step.shape[2]
     start = first[0]
-    low, high = doc_bounds(start, lengths, rows)
+    low, _ = doc_bounds(start, lengths, rows)
     sub = iota((rows, rows), 0)
     lane = iota((rows, rows), 1)
     xt = jnp.transpose(x[0].astype(F32)).astype(BF16)
@@ -115,6 +111,30 @@
         here = ((sub + j == lane) & (sub + start >= low)).astype(BF16)
         away = ((hsub - HALO + j == hlane) & (hsub - HALO + start >= low)).astype(BF16)
         lagged[0, j] = (dot(xt, here) + dot(halo[0], away, TN)).astype(BF16)
+    for h in range(heads):
+        at = slice(h * HEAD, (h + 1) * HEAD)
+        w = taps[0, at]
+        pre = w[:, 4:5] + w[:, 0:1] * lagged[0, 0, at].astype(F32)
+        for j in range(1, 4):
+            pre = pre + w[:, j : j + 1] * lagged[0, j, at].astype(F32)
+        sig = 1.0 / (1.0 + jnp.exp(-pre))
+        co = (pre * sig).astype(BF16)
+        conv[0, at] = co
+        slope[0, at] = sig * (1.0 + pre * (1.0 - sig))
+        upd[0, at] = (step[0, h : h + 1] * co.astype(F32)).astype(BF16)
+
+
+def intra_kernel(
+    first, lengths, skip, conv, upd, gy, gyt, bm, cm, step, rows_in, state, after,
+    part, heads_out, gc, gb, acc, statec,
+):
+    g = pl.program_id(0)
+    heads = step.shape[1]
+    rows = step.shape[2]
+    start = first[0]
+    _, high = doc_bounds(start, lengths, rows)
+    sub = iota((rows, rows), 0)
+    lane = iota((rows, rows), 1)
     statec[...] = dot(state[0], cm[0], NT)
     gram = dot(cm[0], bm[0], NT)
     bias = jnp.where((sub >= lane) & (sub + start <= high), 0.0, -1e30)
@@ -128,18 +148,9 @@
     skip_out = jnp.zeros((heads, rows), F32)
     for h in range(heads):
         at = slice(h * HEAD, (h + 1) * HEAD)
-        w = taps[0, at]
-        pre = w[:, 4:5] + w[:, 0:1] * lagged[0, 0, at].astype(F32)
-        for j in range(1, 4):
-            pre = pre + w[:, j : j + 1] * lagged[0, j, at].astype(F32)
-        sig = 1.0 / (1.0 + jnp.exp(-pre))
-        co = (pre * sig).astype(BF16)
-        conv[0, at] = co
-        slope[0, at] = sig * (1.0 + pre * (1.0 - sig))
-        co = co.astype(F32)
+        co = conv[0, at].astype(F32)
+        u = upd[0, at]
         st = step[0, h : h + 1]
-        u = (st * co).astype(BF16)
-        upd[0, at] = u
         pair = gy[0, :, (h // 2) * 128 : (h // 2 + 1) * 128]
         both = jnp.concatenate([u, zero] if h % 2 == 0 else [zero, u], axis=0)
         score_grad = dot(pair, both)
@@ -217,10 +228,12 @@
     cols[:heads] = jnp.where(lane == 14, skip_grad, top)
     turned = jnp.transpose(cols[...])
     edge[0] = turned[:HALO].astype(BF16)
-    pay[0] = turned[8:16]
-
-
-def grad_b_kernel(rows_in, upd, grad, gb, out):
+    pay[:, 0, 0] = jnp.broadcast_to(turned[8:16].astype(BF16), (pay.shape[0], 8, turned.shape[1]))
+
+
+def grad_b_kernel(rows_in, upd, grad, gb, gc, edge, after, out, edge_out):
+    edge_out[...] = edge[...]
+    out[0, 1] = gc[0]
     heads = rows_in.shape[2]
     scaled = jnp.concatenate(
         [
@@ -229,7 +242,7 @@
         ],
         axis=0,
     )
-    out[0] = (gb[0] + dot(scaled, grad[0], TN)).astype(BF16)
+    out[0, 0] = (gb[0] + dot(scaled, grad[0], TN)).astype(BF16)
 
 
 def input_kernel(first, lengths, pre, right, taps, out):
@@ -249,6 +262,34 @@
     out[0] = jnp.transpose(total).astype(BF16)
 
 
+def spread_kernel(parts, out):
+    total = parts[0].astype(F32)
+    for i in range(1, parts.shape[0]):
+        total = total + parts[i].astype(F32)
+    out[...] = jnp.broadcast_to(total.astype(out.dtype), out.shape)
+
+
+def final_kernel(core, mine, other, weight, bias, rate, skip):
+    each = mine.shape[0]
+    heads = rate.shape[1]
+    for g in range(bias.shape[0]):
+        ours = core[0] == g // each
+        rows = jnp.where(ours, mine[g % each], other[g % each])
+        for j in range(4):
+            weight[j, g : g + 1] = rows[j : j + 1]
+        bias[g : g + 1] = rows[4:5]
+        rate[g : g + 1] = rows[5:6, :heads]
+        skip[g : g + 1] = rows[6:7, :heads]
+
+
+def pair_sum_kernel(parts, one, two):
+    for out, i in ((one, 0), (two, 1)):
+        total = parts[0, :, i].astype(F32)
+        for p in range(1, parts.shape[0]):
+            total = total + parts[p, :, i].astype(F32)
+        out[...] = total
+
+
 def sum_kernel(parts, out):
     total = parts[0].astype(F32)
     for i in range(1, parts.shape[0]):
@@ -256,12 +297,19 @@
     out[...] = total.astype(out.dtype)
 
 
-def call(kernel, grid, ins, outs, args, flops=0, nbytes=0, scratch=()):
+ANY = "any"
+
+
+def call(kernel, grid, ins, outs, args, flops=0, nbytes=0, scratch=(), mib=60, specs=None):
     smem = pl.BlockSpec(memory_space=pltpu.SMEM)
 
     def spec(shape, blocked):
         if blocked is None:
             return smem
+        if blocked is ANY:
+            return pl.BlockSpec(memory_space=pl.ANY)
+        if isinstance(blocked, pl.BlockSpec):
+            return blocked
         if not blocked or not grid:
             return pl.BlockSpec(shape, lambda *i: (0,) * len(shape))
         return pl.BlockSpec(
@@ -272,11 +320,11 @@
         kernel,
         grid=grid,
         in_specs=[spec(a.shape, b) for a, b in zip(args, ins)],
-        out_specs=[spec(s, True) for s, _ in outs],
+        out_specs=specs or [spec(s, True) for s, _ in outs],
         out_shape=[jax.ShapeDtypeStruct(s, t) for s, t in outs],
         scratch_shapes=list(scratch),
         cost_estimate=pl.CostEstimate(flops=flops, bytes_accessed=nbytes, transcendentals=0),
-        compiler_params=pltpu.CompilerParams(vmem_limit_bytes=48 * 1024 * 1024),
+        compiler_params=pltpu.CompilerParams(vmem_limit_bytes=mib * 1024 * 1024),
     )(*args)
 
 
@@ -336,42 +384,57 @@
     )
     own = groups * heads // 2 // blocks
     gathered = lax.all_to_all(pay, "context", 0, 0, tiled=True)
-    lagged, conv, upd, slope, part, heads_in, gc, gb = call(
-        intra_kernel,
+    lagged, conv, upd, slope = call(
+        conv_kernel,
         (groups,),
-        [None, None, None] + [True] * 10,
+        [None, None] + [True] * 4,
         [
             ((groups, 4, features, rows), BF16),
             (wide, BF16),
             (wide, BF16),
             (wide, F32),
+        ],
+        (first, doc_lengths, x, halo, step, taps),
+        flops=4 * 10**9,
+        nbytes=10 * 10**6,
+    )
+    (scanned,) = call(
+        scan_kernel,
+        (),
+        [True, ANY],
+        [((blocks * own, 2 * HEAD, 128), BF16)],
+        (gathered, upd),
+        flops=10**7,
+        nbytes=10**6,
+    )
+    part, heads_in, gc, gb = call(
+        intra_kernel,
+        (groups,),
+        [None, None, None] + [True] * 9 + [ANY],
+        [
             (wide, F32),
             ((groups, 3, heads, rows), F32),
             ((groups, rows, 128), BF16),
             ((groups, rows, 128), F32),
         ],
-        (first, doc_lengths, skip_gain, x, halo, gy, gyt, bm, cm, step, rows_in, state, taps),
-        flops=20 * 10**9,
-        nbytes=20 * 10**6,
+        (first, doc_lengths, skip_gain, conv, upd, gy, gyt, bm, cm, step, rows_in, state, scanned),
+        flops=16 * 10**9,
+        nbytes=10 * 10**6,
         scratch=(pltpu.VMEM((rows, rows), F32), pltpu.VMEM((features, rows), F32)),
     )
-    (scanned,) = call(
-        scan_kernel,
-        (),
-        [True],
-        [((blocks * own, 2 * HEAD, 128), BF16)],
-        (gathered,),
-        flops=10**7,
-        nbytes=10**6,
-    )
     grad = lax.all_to_all(scanned, "context", 0, 0, tiled=True).reshape(groups, features, 128)
-    grad_c = lax.psum_scatter(gc, "tensor", scatter_dimension=0, tiled=True).astype(F32)
-    sums, grad_step, pre, edge = call(
+    parts = lax.axis_size("tensor")
+    here = groups // parts
+    copies = lax.axis_size("dp")
+    halves = 2 if copies % 2 == 0 else 1
+    each = groups // halves
+    wide_spec = pl.BlockSpec((1, features, rows), lambda g: (g, 0, 0))
+    shares, grad_step, pre, edge = call(
         carry_kernel,
         (groups,),
         [None] + [True] * 10,
         [
-            ((groups, 8, features), F32),
+            ((copies // halves, halves, each, 8, features), BF16),
             ((groups, heads, rows), F32),
             (wide, BF16),
             ((groups, HALO, features), BF16),
@@ -380,28 +443,49 @@
         flops=10**9,
         nbytes=20 * 10**6,
         scratch=(pltpu.VMEM((features, 128), F32),),
-    )
-    copies = lax.axis_size("dp")
-    shares = jnp.broadcast_to(sums.astype(BF16)[None], (copies,) + sums.shape)
-    shares = lax.all_to_all(shares, "dp", 0, 0, tiled=True)
-    (sums,) = call(sum_kernel, (), [True], [(sums.shape, BF16)], (shares,))
-    shares = jnp.broadcast_to(sums[None], (blocks,) + sums.shape)
-    shares = lax.all_to_all(shares, "context", 0, 0, tiled=True)
-    (sums,) = call(sum_kernel, (), [True], [(sums.shape, F32)], (shares,))
-
-    (gb,) = call(
+        specs=[
+            pl.BlockSpec(
+                (copies // halves, 1, 1, 8, features), lambda g: (0, g // each, g % each, 0, 0)
+            ),
+            pl.BlockSpec((1, heads, rows), lambda g: (g, 0, 0)),
+            wide_spec,
+            pl.BlockSpec((1, HALO, features), lambda g: (g, 0, 0)),
+        ],
+    )
+    small = (each, 8, features)
+    shares = lax.all_to_all(shares.reshape((copies,) + small), "dp", 0, 0, tiled=True)
+    (shares,) = call(spread_kernel, (), [True], [((blocks,) + small, BF16)], (shares,))
+    gb, edge = call(
         grad_b_kernel,
         (groups,),
-        [True] * 4,
-        [((groups, rows, 128), BF16)],
-        (rows_in, upd, grad, gb),
+        [True] * 6 + [ANY],
+        [((groups, 2, rows, 128), BF16), ((groups, HALO, features), BF16)],
+        (rows_in, upd, grad, gb, gc, edge, shares),
         flops=10**8,
         nbytes=2 * 10**6,
     )
-    parts = lax.axis_size("tensor")
-    here = groups // parts
-    gb = lax.all_to_all(gb, "tensor", 0, 0, tiled=True).reshape(parts, here * rows, 128)
-    (grad_b,) = call(sum_kernel, (), [True], [((here * rows, 128), F32)], (gb,))
+    shares = lax.all_to_all(shares, "context", 0, 0, tiled=True)
+    (mine,) = call(sum_kernel, (), [True], [(small, F32)], (shares,))
+    core = lax.axis_index("dp") % halves
+    other = mine
+    if halves == 2:
+        other = lax.ppermute(mine, "dp", [(i, i ^ 1) for i in range(copies)])
+    weight, bias, rate, skip = call(
+        final_kernel,
+        (),
+        [None, True, True],
+        [
+            ((4, groups, features), F32),
+            ((groups, features), F32),
+            ((groups, heads), F32),
+            ((groups, heads), F32),
+        ],
+        (core.astype(jnp.int32).reshape(1), mine, other),
+    )
+    both = lax.all_to_all(gb, "tensor", 0, 0, tiled=True).reshape(parts, here, 2, rows, 128)
+    grad_b, grad_c = call(
+        pair_sum_kernel, (), [True], [((here, rows, 128), F32)] * 2, (both,)
+    )
 
     right = shifted(edge, "context", -1)
     (grad_input,) = call(
@@ -418,10 +502,10 @@
         jnp.transpose(grad_b.reshape(1, here, rows, 128), (0, 2, 1, 3)),
         jnp.transpose(grad_c.reshape(1, here, rows, 128), (0, 2, 1, 3)),
         jnp.transpose(grad_step, (2, 0, 1))[None],
-        jnp.transpose(sums[:, :4], (1, 0, 2)),
-        sums[:, 4],
-        sums[:, 5, :heads],
-        sums[:, 6, :heads],
+        weight,
+        bias,
+        rate,
+        skip,
     )
 
 

time: 188 us -> 173 us (0.920)
  waiting for transfers between devices: 62.2 us -> 34.5 us
  blocking collectives: 0 us -> 16.8 us
  Pallas kernels: 28.3 us -> 43.7 us
  between operations: 14.3 us -> 0.85 us
  local copies, waits for them, and re-layouts: 21.9 us -> 13.2 us
  starting transfers between devices: 55.1 us -> 60.7 us
  other arithmetic: 4.13 us -> 1.39 us
    reduce_scatter x1 -> x0, waiting for transfers between devices: 27.8 us -> none  [body(): lax.psum_scatter(gc, 'tensor', scatter_dimension=0, tiled=True).astype(F32)]
    all_to_all x1, waiting for transfers between devices: 19.4 us -> 0.47 us  [body(): gathered = lax.all_to_all(pay, 'context', 0, 0, tiled=True)]
    all_to_all x0 -> x1, blocking collectives: none -> 16.8 us  [body(): lax.all_to_all(shares.reshape((copies,) + small), 'dp', 0, 0, tiled=True)]
    pallas_call x9 -> x11, Pallas kernels: 28.3 us -> 43.7 us  [call(): pl.pallas_call(kernel, grid=grid, in_specs=[spec(a.shape, b) for a, b in...]
    all_to_all x1 -> x0, starting transfers between devices: 11.4 us -> none  [body(): shares = lax.all_to_all(shares, 'dp', 0, 0, tiled=True)]
    ppermute x2, waiting for transfers between devices: 0.01 us -> 10.6 us  [shifted(): return lax.ppermute(block, axis, route)]
    all_to_all x1, waiting for transfers between devices: 0.01 us -> 8.94 us  [body(): shares = lax.all_to_all(shares, 'context', 0, 0, tiled=True)]
    ppermute x0 -> x1, starting transfers between devices: none -> 8.67 us  [body(): other = lax.ppermute(mine, 'dp', [(i, i ^ 1) for i in range(copies)])]
  transfers between devices with their start and end apart: 8 -> 7, of which waited for: 5 -> 4; matrix products, arithmetic and copies ran while one was open for 5% -> 4% of each run, Pallas kernels for 10% -> 16%
where the time goes in v2:
time: 173 us; the launch traced here: 171 us
  starting transfers between devices  60.7 us (35%)
  Pallas kernels  43.7 us (25%)
  waiting for transfers between devices  34.5 us (20%)
  blocking collectives  16.8 us (10%)
  local copies, waits for them, and re-layouts  13.2 us (8%)
    pallas_call x11, Pallas kernels, call(): pl.pallas_call(kernel, grid=grid, in_specs=[spec(a.shape, b) for a, b in...  43.7 us
    all_to_all x1, starting transfers between devices, body(): lax.all_to_all(scanned, 'context', 0, 0, tiled=True)  21.3 us
    all_to_all x1, blocking collectives, body(): lax.all_to_all(shares.reshape((copies,) + small), 'dp', 0, 0, tiled=True)  16.8 us
    all_to_all x1, starting transfers between devices, body(): gathered = lax.all_to_all(pay, 'context', 0, 0, tiled=True)  15.9 us
    all_to_all x1, waiting for transfers between devices, body(): lax.all_to_all(scanned, 'context', 0, 0, tiled=True)  14.4 us
    unnamed x32, local copies, waits for them, and re-layouts  12.7 us
    ppermute x2, waiting for transfers between devices, shifted(): return lax.ppermute(block, axis, route)  10.6 us
    all_to_all x1, waiting for transfers between devices, body(): shares = lax.all_to_all(shares, 'context', 0, 0, tiled=True)  8.94 us
  transfers between devices with their start and end apart: 7, of which 4 were waited for; matrix products, arithmetic and copies ran while one was open for 4% of the time, Pallas kernels for 16%

profile of v2, /device:TPU:1, one launch (start us, length us, event | category | flops | bytes accessed | tf_op | source)
XLA Modules:
  0.0 171.1 jit_solution(1260465228450480510)
XLA Ops:
  0.6 0.0 copy-start.6
  0.6 2.4 %copy.65 = bf16[1,256,4,512]{3,1,2,0:T(8,128)(2,1)} copy(bf16[1,256,4,512]{3,2,1,0:T(4,128)(2,1)} %param.12) | data formatting | bytes 2097152 | tf_op args[1]
  3.1 0.0 copy-done.6
  3.1 0.7 copy.67
  3.8 4.5 %shard_map.170 = (bf16[16,144,128]{2,1,0:T(8,128)(2,1)}, bf16[4,512,256]{2,1,0:T(8,128)(2,1)}, f32[4,3,8,256]{3,2,1,0:T(8,128)}) custom-call(s32[1]{0:T(128)} %bitcast.first, s32[1,6]{1,0:T(1,128)} %lengths.7, f32[4,8]{1,0:T(4,128)} %rate.3, f32[4,8,256]{2,1,0:T(8,128)} %bitcast.60, bf16[4,256,512]{2,1,0:T(8,128)(2,1)} %bitcast.52, bf16[4,256,128]{2,1,0:T(8,128)(2,1)} %bitcast.57), custom_call_target="tpu_custom_call" | custom-call | flops 1000000000 | bytes 4000000 | tf_op jit(solution)/shard_map/pallas_call | solution.py:319
  8.3 0.0 copy-start.10
  8.3 15.9 %all-to-all-start = ((bf16[16,144,128]{2,1,0:T(8,128)(2,1)}), bf16[16,144,128]{2,1,0:T(8,128)(2,1)S(1)}, u32[]{:S(2)}, u32[]{:S(2)}) async-start(bf16[16,144,128]{2,1,0:T(8,128)(2,1)} %get-tuple-element.31), calls=%async_computation | async-start | bytes 1179648 | tf_op jit(solution)/shard_map/all_to_all | solution.py:386
  24.2 0.0 copy-done.4
  24.2 0.2 copy.68
  24.4 0.9 copy-done.3
  25.4 3.3 %collective-permute-start = (bf16[8,4,512]{2,0,1:T(8,128)(2,1)S(1)}, bf16[8,4,512]{2,0,1:T(8,128)(2,1)S(1)}, u32[]{:S(2)}, u32[]{:S(2)}) collective-permute-start(bf16[8,4,512]{2,0,1:T(8,128)(2,1)S(1)} %slice_bitcast_fusion), channel_id=1, source_target_pairs={{0,32},{32,64},{64,96},{96,128},{128,160},{160,192},{192,224},{224... | collective-permute-start | bytes 98312 | tf_op jit(solution)/shard_map/ppermute | solution.py:334
  28.6 0.0 copy-done.8
  28.7 0.4 copy.54
  29.0 0.4 copy.55
  29.4 0.1 pad.2.clone
  29.5 1.4 maximum_maximum_fusion.taps
  30.9 10.6 %collective-permute-done = bf16[8,4,512]{2,0,1:T(8,128)(2,1)S(1)} collective-permute-done((bf16[8,4,512]{2,0,1:T(8,128)(2,1)S(1)}, bf16[8,4,512]{2,0,1:T(8,128)(2,1)S(1)}, u32[]{:S(2)}, u32[]{:S(2)}) %collective-permute-start) | collective-permute-done | bytes 32800 | tf_op jit(solution)/shard_map/ppermute | solution.py:334
  41.5 0.6 copy-done.12
  42.1 6.9 %shard_map.171 = (bf16[4,4,512,256]{3,2,1,0:T(8,128)(2,1)}, bf16[4,512,256]{2,1,0:T(8,128)(2,1)}, bf16[4,512,256]{2,1,0:T(8,128)(2,1)}, f32[4,512,256]{2,1,0:T(8,128)}) custom-call(s32[1]{0:T(128)} %bitcast.first, s32[1,6]{1,0:T(1,128)} %lengths.7, bf16[4,256,512]{2,1,0:T(8,128)(2,1)} %bitcast.49, bf16[4,8,512]{2,1,0:T(8,128)(2,1)} %bitcast.68, ...), custom_call_target="tpu_custom_call" | custom-call | flops 4000000000 | bytes 10000000 | tf_op jit(solution)/shard_map/pallas_call | solution.py:319
  49.1 0.5 all-to-all-done.pay
  49.5 0.8 copy-done.1
  50.4 2.0 %shard_map.172.after = bf16[16,128,128]{2,1,0:T(8,128)(2,1)} custom-call(bf16[16,144,128]{2,1,0:T(8,128)(2,1)} %copy-done.1, bf16[4,512,256]{2,1,0:T(8,128)(2,1)} %get-tuple-element.32.after.upd), custom_call_target="tpu_custom_call" | custom-call | flops 10000000 | bytes 1000000 | tf_op jit(solution)/shard_map/pallas_call | solution.py:319
  52.3 21.3 %all-to-all-start.1 = ((bf16[16,128,128]{2,1,0:T(8,128)(2,1)}), bf16[16,128,128]{2,1,0:T(8,128)(2,1)S(1)}, u32[]{:S(2)}, u32[]{:S(2)}) async-start(bf16[16,128,128]{2,1,0:T(8,128)(2,1)} %shard_map.172.after), calls=%async_computation.1 | async-start | bytes 1048576 | tf_op jit(solution)/shard_map/all_to_all | solution.py:425
  73.7 0.7 copy.66
  74.4 7.7 %shard_map.173 = (f32[4,512,256]{2,1,0:T(8,128)}, f32[4,3,8,256]{3,2,1,0:T(8,128)}, bf16[4,256,128]{2,1,0:T(8,128)(2,1)}, f32[4,256,128]{2,1,0:T(8,128)}) custom-call(s32[1]{0:T(128)} %bitcast.first, s32[1,6]{1,0:T(1,128)} %lengths.7, f32[4,8]{1,0:T(4,128)} %skip.1, bf16[4,512,256]{2,1,0:T(8,128)(2,1)} %get-tuple-element.34.conv, ...), custom_call_target="tpu_custom_call" | custom-call | flops 16000000000 | bytes 10000000 | tf_op jit(solution)/shard_map/pallas_call | solution.py:319
  82.1 14.4 %all-to-all-done.1 = bf16[16,128,128]{2,1,0:T(8,128)(2,1)S(1)} async-done(((bf16[16,128,128]{2,1,0:T(8,128)(2,1)}), bf16[16,128,128]{2,1,0:T(8,128)(2,1)S(1)}, u32[]{:S(2)}, u32[]{:S(2)}) %all-to-all-start.1) | async-done | bytes 524320 | tf_op jit(solution)/shard_map/all_to_all | solution.py:425
  96.5 0.8 copy-done
  97.3 7.1 %shard_map.174 = (bf16[4,2,2,8,512]{4,3,2,1,0:T(8,128)(2,1)}, f32[4,8,256]{2,1,0:T(8,128)}, bf16[4,512,256]{2,1,0:T(8,128)(2,1)}, bf16[4,8,512]{2,1,0:T(8,128)(2,1)}) custom-call(f32[4,8]{1,0:T(4,128)} %rate.3, bf16[4,512,128]{2,1,0:T(8,128)(2,1)} %bitcast.45, bf16[4,256,128]{2,1,0:T(8,128)(2,1)} %bitcast.51, f32[4,8,256]{2,1,0:T(8,128)} %bitcast.63, ...), custom_call_target="tpu_custom_call" | custom-call | flops 1000000000 | bytes 20000000 | tf_op jit(solution)/shard_map/pallas_call | solution.py:319
  104.5 16.8 %all_to_all.25.parts = bf16[8,2,8,512]{3,2,1,0:T(8,128)(2,1)} all-to-all(bf16[8,2,8,512]{3,2,1,0:T(8,128)(2,1)} %bitcast.59), channel_id=1, replica_groups=mesh['context'=16,'dp'=8,'tensor'=4] {'dp'}, dimensions={0} | all-to-all | bytes 262144 | tf_op jit(solution)/shard_map/all_to_all | solution.py:456
  121.3 1.6 shard_map.175.after
  122.9 6.1 %all-to-all-start.4 = ((bf16[16,2,8,512]{3,2,1,0:T(8,128)(2,1)}), bf16[16,2,8,512]{3,2,1,0:T(8,128)(2,1)S(1)}, u32[]{:S(2)}, u32[]{:S(2)}) async-start(bf16[16,2,8,512]{3,2,1,0:T(8,128)(2,1)} %shard_map.175.after), calls=%async_computation.4 | async-start | bytes 524288 | tf_op jit(solution)/shard_map/all_to_all | solution.py:467
  129.0 4.1 %shard_map.176 = (bf16[4,2,256,128]{3,2,1,0:T(8,128)(2,1)}, bf16[4,8,512]{2,1,0:T(8,128)(2,1)}) custom-call(f32[4,3,8,256]{3,2,1,0:T(8,128)} %get-tuple-element.33.rows_in, bf16[4,512,256]{2,1,0:T(8,128)(2,1)} %get-tuple-element.32.after.upd, bf16[4,512,128]{2,1,0:T(8,128)(2,1)} %bitcast.46, f32[4,256,128]{2,1,0:T(8,128)} %get-tuple-element.41.gb, ...), custom_call_target="tpu_custom_call" | custom-call | flops 100000000 | bytes 2000000 | tf_op jit(solution)/shard_map/pallas_call | solution.py:319
  133.1 8.9 %all-to-all-done.4.parts = bf16[16,2,8,512]{3,2,1,0:T(8,128)(2,1)S(1)} async-done(((bf16[16,2,8,512]{3,2,1,0:T(8,128)(2,1)}), bf16[16,2,8,512]{3,2,1,0:T(8,128)(2,1)S(1)}, u32[]{:S(2)}, u32[]{:S(2)}) %all-to-all-start.4) | async-done | bytes 262176 | tf_op jit(solution)/shard_map/all_to_all | solution.py:467
  142.0 4.2 %all-to-all-start.3 = ((bf16[4,2,256,128]{3,2,1,0:T(8,128)(2,1)}), bf16[4,2,256,128]{3,2,1,0:T(8,128)(2,1)S(1)}, u32[]{:S(2)}, u32[]{:S(2)}) async-start(bf16[4,2,256,128]{3,2,1,0:T(8,128)(2,1)} %get-tuple-element.46), calls=%async_computation.3 | async-start | bytes 1048576 | tf_op jit(solution)/shard_map/all_to_all | solution.py:485
  146.2 1.3 collective-permute-start.1
  147.5 1.6 shard_map.179.mine
  149.1 8.7 %collective-permute-start.2 = (f32[2,8,512]{2,1,0:T(8,128)}, f32[2,8,512]{2,1,0:T(8,128)S(1)}, u32[]{:S(2)}, u32[]{:S(2)}) collective-permute-start(f32[2,8,512]{2,1,0:T(8,128)} %shard_map.179.mine), channel_id=1, source_target_pairs={{0,4},{4,0},{8,12},{12,8},{16,20},{20,16},{24,28},{28,24},{1,5},{5... | collective-permute-start | bytes 98312 | tf_op jit(solution)/shard_map/ppermute | solution.py:472
  157.8 0.0 collective-permute-done.1.right
  157.8 0.0 copy-start.11
  157.8 0.6 copy-done.11
  158.4 5.1 %shard_map.177 = bf16[4,256,512]{2,1,0:T(8,128)(2,1)} custom-call(s32[1]{0:T(128)} %bitcast.first, s32[1,6]{1,0:T(1,128)} %lengths.7, bf16[4,512,256]{2,1,0:T(8,128)(2,1)} %get-tuple-element.40.pre, bf16[4,8,512]{2,1,0:T(8,128)(2,1)} %copy-done.11, f32[4,512,8]{2,1,0:T(8,128)} %maximum_maximum_fusion.taps), custom_call_target="tpu_custom_call" | custom-call | flops 1000000000 | bytes 4000000 | tf_op jit(solution)/shard_map/pallas_call | solution.py:319
  163.5 3.0 %copy.57 = bf16[1,256,4,512]{3,2,1,0:T(4,128)(2,1)} copy(bf16[1,256,4,512]{3,1,2,0:T(8,128)(2,1)} %bitcast.54) | data formatting | bytes 2097152
  166.5 0.0 all-to-all-done.3
  166.5 0.8 copy-done.2
  167.3 1.8 %shard_map.178 = (f32[1,256,128]{2,1,0:T(8,128)}, f32[1,256,128]{2,1,0:T(8,128)}) custom-call(bf16[4,1,2,256,128]{4,3,2,1,0:T(8,128)(2,1)} %bitcast.48), custom_call_target="tpu_custom_call" | custom-call | tf_op jit(solution)/shard_map/pallas_call | solution.py:319
  169.1 0.0 collective-permute-done.2.other
  169.1 0.6 copy-done.9
  169.7 1.4 shard_map.180
  (15 shorter events, 0.0 us)
Async XLA Ops:
  0.6 2.5 %copy-start.6 = (bf16[1,256,4,128]{3,2,1,0:T(4,128)(2,1)S(1)}, bf16[1,256,4,128]{3,2,1,0:T(4,128)(2,1)}, u32[]{:S(2)}) copy-start(bf16[1,256,4,128]{3,2,1,0:T(4,128)(2,1)} %param.14) | copy-start | bytes 786436
  3.8 20.4 %copy-start.4 = (bf16[1,256,4,512]{3,2,1,0:T(4,128)(2,1)S(1)}, bf16[1,256,4,512]{3,2,1,0:T(4,128)(2,1)}, u32[]{:S(2)}) copy-start(bf16[1,256,4,512]{3,2,1,0:T(4,128)(2,1)} %param.11) | copy-start | bytes 3145732
  8.3 20.3 %copy-start.8 = (f32[4,4,512]{2,1,0:T(4,128)S(1)}, f32[4,4,512]{2,1,0:T(4,128)}, u32[]{:S(2)}) copy-start(f32[4,4,512]{2,1,0:T(4,128)} %param.18) | copy-start | bytes 98308
  8.3 20.7 %copy-start.10 = (f32[4,512]{1,0:T(4,128)S(1)}, f32[4,512]{1,0:T(4,128)}, u32[]{:S(2)}) copy-start(f32[4,512]{1,0:T(4,128)} %param.19) | copy-start | bytes 24580
  8.3 41.2 %all-to-all-start = ((bf16[16,144,128]{2,1,0:T(8,128)(2,1)}), bf16[16,144,128]{2,1,0:T(8,128)(2,1)S(1)}, u32[]{:S(2)}, u32[]{:S(2)}) async-start(bf16[16,144,128]{2,1,0:T(8,128)(2,1)} %get-tuple-element.31), calls=%async_computation | async-start | bytes 1179648 | tf_op jit(solution)/shard_map/all_to_all | solution.py:386
  24.4 1.0 copy-start.3
  25.4 16.1 %collective-permute-start = (bf16[8,4,512]{2,0,1:T(8,128)(2,1)S(1)}, bf16[8,4,512]{2,0,1:T(8,128)(2,1)S(1)}, u32[]{:S(2)}, u32[]{:S(2)}) collective-permute-start(bf16[8,4,512]{2,0,1:T(8,128)(2,1)S(1)} %slice_bitcast_fusion), channel_id=1, source_target_pairs={{0,32},{32,64},{64,96},{96,128},{128,160},{160,192},{192,224},{224... | collective-permute-start | bytes 98312 | tf_op jit(solution)/shard_map/ppermute | solution.py:334
  41.5 0.6 copy-start.12
  49.1 24.6 %copy-start.7 = (bf16[1,256,4,128]{3,2,1,0:T(4,128)(2,1)S(1)}, bf16[1,256,4,128]{3,2,1,0:T(4,128)(2,1)}, u32[]{:S(2)}) copy-start(bf16[1,256,4,128]{3,2,1,0:T(4,128)(2,1)} %param.13) | copy-start | bytes 786436
  49.5 0.8 copy-start.1
  52.3 44.2 %all-to-all-start.1 = ((bf16[16,128,128]{2,1,0:T(8,128)(2,1)}), bf16[16,128,128]{2,1,0:T(8,128)(2,1)S(1)}, u32[]{:S(2)}, u32[]{:S(2)}) async-start(bf16[16,128,128]{2,1,0:T(8,128)(2,1)} %shard_map.172.after), calls=%async_computation.1 | async-start | bytes 1048576 | tf_op jit(solution)/shard_map/all_to_all | solution.py:425
  96.5 0.8 copy-start
  122.9 19.1 %all-to-all-start.4 = ((bf16[16,2,8,512]{3,2,1,0:T(8,128)(2,1)}), bf16[16,2,8,512]{3,2,1,0:T(8,128)(2,1)S(1)}, u32[]{:S(2)}, u32[]{:S(2)}) async-start(bf16[16,2,8,512]{3,2,1,0:T(8,128)(2,1)} %shard_map.175.after), calls=%async_computation.4 | async-start | bytes 524288 | tf_op jit(solution)/shard_map/all_to_all | solution.py:467
  142.0 5.5 %copy-start.5 = (bf16[16,2,8,512]{3,2,1,0:T(8,128)(2,1)}, bf16[16,2,8,512]{3,2,1,0:T(8,128)(2,1)S(1)}, u32[]{:S(2)}) copy-start(bf16[16,2,8,512]{3,2,1,0:T(8,128)(2,1)S(1)} %all-to-all-done.4.parts) | copy-start | bytes 786436
  142.0 24.5 %all-to-all-start.3 = ((bf16[4,2,256,128]{3,2,1,0:T(8,128)(2,1)}), bf16[4,2,256,128]{3,2,1,0:T(8,128)(2,1)S(1)}, u32[]{:S(2)}, u32[]{:S(2)}) async-start(bf16[4,2,256,128]{3,2,1,0:T(8,128)(2,1)} %get-tuple-element.46), calls=%async_computation.3 | async-start | bytes 1048576 | tf_op jit(solution)/shard_map/all_to_all | solution.py:485
  146.2 11.6 %collective-permute-start.1 = (bf16[4,8,512]{2,1,0:T(8,128)(2,1)}, bf16[4,8,512]{2,1,0:T(8,128)(2,1)S(1)}, u32[]{:S(2)}, u32[]{:S(2)}) collective-permute-start(bf16[4,8,512]{2,1,0:T(8,128)(2,1)} %get-tuple-element.45), channel_id=1, source_target_pairs={{32,0},{64,32},{96,64},{128,96},{160,128},{192,160},{224,192},{256... | collective-permute-start | bytes 98312 | tf_op jit(solution)/shard_map/ppermute | solution.py:334
  149.1 20.0 %collective-permute-start.2 = (f32[2,8,512]{2,1,0:T(8,128)}, f32[2,8,512]{2,1,0:T(8,128)S(1)}, u32[]{:S(2)}, u32[]{:S(2)}) collective-permute-start(f32[2,8,512]{2,1,0:T(8,128)} %shard_map.179.mine), channel_id=1, source_target_pairs={{0,4},{4,0},{8,12},{12,8},{16,20},{20,16},{24,28},{28,24},{1,5},{5... | collective-permute-start | bytes 98312 | tf_op jit(solution)/shard_map/ppermute | solution.py:472
  157.8 0.6 copy-start.11
  166.5 0.8 copy-start.2
  169.1 0.6 copy-start.9

commit v3 on v2

v3 whole, which is shorter than its diff:
```python
import functools

import jax
import jax.numpy as jnp
from jax import lax
from jax.experimental import pallas as pl
from jax.experimental.pallas import tpu as pltpu
from jax.sharding import PartitionSpec as P

F32 = jnp.float32
BF16 = jnp.bfloat16
LOG2E = 1.4426950408889634
FULL = lax.Precision.HIGHEST
HEAD = 64
HALO = 8
EXTRA = 16
ROWS = 24
FAR = 1 << 28


def dot(a, b, dims=((1,), (0,)), precision=None):
    return lax.dot_general(a, b, (dims, ((), ())), precision=precision, preferred_element_type=F32)


NT = ((1,), (1,))
TN = ((0,), (0,))


def iota(shape, axis):
    return lax.broadcasted_iota(jnp.int32, shape, axis)


def doc_bounds(first, lengths, rows):
    pos = first + iota((1, rows), 1)
    low = jnp.zeros((1, rows), jnp.int32)
    high = jnp.full((1, rows), FAR, jnp.int32)
    start = jnp.int32(0)
    for d in range(lengths.shape[1]):
        low = jnp.where(pos >= start, start, low)
        start = start + lengths[0, d]
        high = jnp.minimum(high, jnp.where(start > pos, start - 1, FAR))
    return low, high


def per_head(values, group, shape):
    column = jnp.zeros(shape, F32)
    for h in range(shape[0]):
        column = jnp.where(iota(shape, 0) == h, values[group, h], column)
    return column


def summed(values, chosen):
    count = values.shape[0]
    upper = values.astype(BF16).astype(F32)
    rest = values - upper
    middle = rest.astype(BF16).astype(F32)
    parts = jnp.concatenate([upper, middle, rest - middle], axis=0).astype(BF16)
    out = dot(parts, chosen)
    return out[:count] + out[count : 2 * count] + out[2 * count :]


def offset_kernel(first, lengths, rate, step, gy, cm, pay, gyt, rows_out, tri):
    g = pl.program_id(0)

    @pl.when(g == 0)
    def _():
        size = tri.shape
        tri[...] = (iota(size, 0) <= iota(size, 1)).astype(BF16)

    rows = step.shape[2]
    heads = step.shape[1]
    low, high = doc_bounds(first[0], lengths, rows)
    cum = summed(step[0] * (per_head(rate, g, (heads, rows)) * (-LOG2E)), tri[...])
    from_start = jnp.where(low < first[0], jnp.exp2(cum), 0.0)
    last = jnp.broadcast_to(cum[:, rows - 1 :], (heads, rows))
    to_end = jnp.where(high >= first[0] + rows - 1, jnp.exp2(jnp.minimum(last - cum, 0.0)), 0.0)
    rows_out[0, 0] = cum
    rows_out[0, 1] = from_start
    rows_out[0, 2] = to_end
    gt = jnp.transpose(gy[0].astype(F32))
    gyt[0] = gt.astype(BF16)
    scaled = jnp.concatenate(
        [gt[h * HEAD : (h + 1) * HEAD] * from_start[h : h + 1] for h in range(heads)], axis=0
    ).astype(BF16)
    pay[0, : heads * HEAD] = dot(scaled, cm[0]).astype(BF16)
    pay[0, heads * HEAD :] = factors_out(jnp.broadcast_to(from_start[:, rows - 1 :], (heads, 128)))


def factors_out(values):
    upper = values.astype(BF16).astype(F32)
    return jnp.concatenate([upper, values - upper], axis=0).astype(BF16)


def factors_in(rows):
    rows = rows.astype(F32)
    half = rows.shape[0] // 2
    return rows[:half] + rows[half:]


def quad_kernel(got, out):
    count = got.shape[0]
    size = got.shape[1] - EXTRA
    through = [factors_in(got[r, size:]) for r in range(count)]
    total = through[0]
    for r in range(1, count):
        total = total * through[r]
    for h in range(size // HEAD):
        at = slice(h * HEAD, (h + 1) * HEAD)
        state = got[count - 1, at].astype(F32)
        for r in range(count - 2, -1, -1):
            state = through[r][h : h + 1] * state + got[r, at].astype(F32)
        out[at] = state.astype(BF16)
    out[size:] = factors_out(total)


def scan_kernel(got, near, far, after, out):
    count = got.shape[0]
    size = got.shape[1] - EXTRA
    through = [factors_in(got[r, size:]) for r in range(count)]
    total = factors_in(near[size:])
    for h in range(size // HEAD):
        at = slice(h * HEAD, (h + 1) * HEAD)
        state = near[at].astype(F32) + total[h : h + 1] * far[at].astype(F32)
        out[count - 1, at] = state.astype(BF16)
        for r in range(count - 2, -1, -1):
            state = through[r + 1][h : h + 1] * state + got[r + 1, at].astype(F32)
            out[r, at] = state.astype(BF16)


def conv_kernel(first, lengths, x, halo, step, taps, after, lagged, conv, upd, slope):
    heads = step.shape[1]
    rows = step.shape[2]
    start = first[0]
    low, _ = doc_bounds(start, lengths, rows)
    sub = iota((rows, rows), 0)
    lane = iota((rows, rows), 1)
    xt = jnp.transpose(x[0].astype(F32)).astype(BF16)
    lagged[0, 0] = xt
    hsub = iota((HALO, rows), 0)
    hlane = iota((HALO, rows), 1)
    for j in range(1, 4):
        here = ((sub + j == lane) & (sub + start >= low)).astype(BF16)
        away = ((hsub - HALO + j == hlane) & (hsub - HALO + start >= low)).astype(BF16)
        lagged[0, j] = (dot(xt, here) + dot(halo[0], away, TN)).astype(BF16)
    for h in range(heads):
        at = slice(h * HEAD, (h + 1) * HEAD)
        w = taps[0, at]
        pre = w[:, 4:5] + w[:, 0:1] * lagged[0, 0, at].astype(F32)
        for j in range(1, 4):
            pre = pre + w[:, j : j + 1] * lagged[0, j, at].astype(F32)
        sig = 1.0 / (1.0 + jnp.exp(-pre))
        co = (pre * sig).astype(BF16)
        conv[0, at] = co
        slope[0, at] = (sig * (1.0 + pre * (1.0 - sig))).astype(BF16)
        upd[0, at] = (step[0, h : h + 1] * co.astype(F32)).astype(BF16)


def intra_kernel(
    first, lengths, skip, conv, upd, gy, gyt, bm, cm, step, rows_in, state, after,
    part, heads_out, gc, gb, acc, statec,
):
    g = pl.program_id(0)
    heads = step.shape[1]
    rows = step.shape[2]
    start = first[0]
    _, high = doc_bounds(start, lengths, rows)
    sub = iota((rows, rows), 0)
    lane = iota((rows, rows), 1)
    statec[...] = dot(state[0], cm[0], NT)
    gram = dot(cm[0], bm[0], NT)
    bias = jnp.where((sub >= lane) & (sub + start <= high), 0.0, -1e30)
    cum = rows_in[0, 0]
    cum_col = jnp.transpose(cum)
    acc[...] = jnp.zeros((rows, rows), F32)
    zero = jnp.zeros((HEAD, rows), BF16)
    spot = iota((heads, rows), 0)
    cum_out = jnp.zeros((heads, rows), F32)
    step_out = jnp.zeros((heads, rows), F32)
    skip_out = jnp.zeros((heads, rows), F32)
    for h in range(heads):
        at = slice(h * HEAD, (h + 1) * HEAD)
        co = conv[0, at].astype(F32)
        u = upd[0, at]
        st = step[0, h : h + 1]
        pair = gy[0, :, (h // 2) * 128 : (h // 2 + 1) * 128]
        both = jnp.concatenate([u, zero] if h % 2 == 0 else [zero, u], axis=0)
        score_grad = dot(pair, both)
        decay = jnp.exp2(cum_col[:, h : h + 1] - cum[h : h + 1] + bias)
        acc[...] += decay * score_grad
        score = (decay * gram).astype(BF16)
        gt = gyt[0, at]
        grad_u = dot(gt, score)
        y = dot(u, score, NT)
        gt = gt.astype(F32)
        row_sum = jnp.sum(gt * (y + rows_in[0, 1, h : h + 1] * statec[at]), axis=0, keepdims=True)
        col_sum = jnp.sum(u.astype(F32) * grad_u, axis=0, keepdims=True)
        cum_out = jnp.where(spot == h, row_sum - col_sum, cum_out)
        step_out = jnp.where(spot == h, jnp.sum(grad_u * co, axis=0, keepdims=True), step_out)
        skip_out = jnp.where(spot == h, jnp.sum(gt * co, axis=0, keepdims=True), skip_out)
        part[0, at] = (st * grad_u + skip[g, h] * gt).astype(BF16)
    heads_out[0, 0] = cum_out
    heads_out[0, 1] = step_out
    heads_out[0, 2] = skip_out
    grad_gram = acc[...].astype(BF16)
    scaled = jnp.concatenate(
        [
            (gyt[0, h * HEAD : (h + 1) * HEAD].astype(F32) * rows_in[0, 1, h : h + 1]).astype(BF16)
            for h in range(heads)
        ],
        axis=0,
    )
    gc[0] = (dot(grad_gram, bm[0]) + dot(scaled, state[0], TN)).astype(BF16)
    gb[0] = dot(grad_gram, cm[0], TN)


def carry_kernel(
    rate, grad, bm, step, rows_in, heads_in, state, lagged, conv, slope, part,
    after, pay, grad_step, pre_out, edge, prods, tri,
):
    group = pl.program_id(0)

    @pl.when(group == 0)
    def _():
        size = tri.shape
        tri[...] = (iota(size, 0) >= iota(size, 1)).astype(BF16)

    heads = step.shape[1]
    rows = step.shape[2]
    carry = dot(grad[0], bm[0], NT)
    spot = iota((heads, rows), 0)
    to_end = rows_in[0, 2]
    along = jnp.zeros((heads, rows), F32)
    inner = jnp.zeros((heads, 128), F32)
    for h in range(heads):
        at = slice(h * HEAD, (h + 1) * HEAD)
        cb = carry[at]
        st = step[0, h : h + 1]
        along = jnp.where(spot == h, jnp.sum(cb * conv[0, at].astype(F32), axis=0, keepdims=True), along)
        prod = grad[0, at].astype(F32) * state[0, at].astype(F32)
        inner = jnp.where(
            iota((heads, 128), 0) == h, jnp.sum(prod, axis=0, keepdims=True), inner
        )
        gp = part[0, at].astype(F32) + (st * to_end[h : h + 1]) * cb
        gp = gp * slope[0, at].astype(F32)
        pre_out[0, at] = gp.astype(BF16)
        terms = [gp * lagged[0, j, at].astype(F32) for j in range(4)] + [gp]
        for j, term in enumerate(terms):
            lanes = slice(j % 2 * 128, j % 2 * 128 + 128)
            prods[j // 2, at, lanes] = (term[:, :128] + term[:, 128:]).astype(BF16)
        prods[2, at, 128:] = gp[:, :128].astype(BF16)
    along = along * to_end
    step_two = along
    along = along * step[0]
    through = rows_in[0, 1][:, rows - 1 :]
    last = jnp.sum(along, axis=1, keepdims=True) + through * jnp.sum(inner, axis=1, keepdims=True)
    grad_cum = heads_in[0, 0] - along + jnp.where(iota((heads, rows), 1) == rows - 1, last, 0.0)
    grad_log = summed(grad_cum, tri[...])
    grad_step[0] = heads_in[0, 1] + step_two - per_head(rate, group, (heads, rows)) * grad_log
    spot = iota((ROWS + HALO, rows), 0)
    lane = iota((ROWS + HALO, rows), 1)
    total = jnp.zeros((ROWS, 128), F32)
    for i in range(prods.shape[1] // 128):
        at = slice(i * 128, (i + 1) * 128)
        for k in range(3):
            if k < 2:
                chosen = spot == i * 5 + 2 * k + (lane >= 128).astype(jnp.int32)
            else:
                chosen = spot == jnp.where(lane < 128, i * 5 + 4, ROWS + lane - 128)
            out = dot(chosen.astype(BF16), prods[k, at], NT)
            total = total + out[:ROWS]
        edge[0, :, at] = out[ROWS:].astype(BF16)
    few = jnp.concatenate([-step[0] * grad_log, heads_in[0, 2]], axis=0)
    upper = few.astype(BF16).astype(F32)
    few = jnp.concatenate([upper, few - upper], axis=1)
    few = jnp.concatenate([few, jnp.zeros((128 - 2 * heads, 2 * rows), F32)], axis=0).astype(BF16)
    total = total + dot((iota((ROWS, 2 * rows), 0) == 20).astype(BF16), few, NT)
    pay[:, 0, 0] = jnp.broadcast_to(total.astype(BF16), (pay.shape[0], ROWS, 128))


def grad_b_kernel(index, rows_in, upd, grad, gb, gc, after, *outs):
    heads = rows_in.shape[2]
    scaled = jnp.concatenate(
        [
            (upd[0, h * HEAD : (h + 1) * HEAD].astype(F32) * rows_in[0, 2, h : h + 1]).astype(BF16)
            for h in range(heads)
        ],
        axis=0,
    )
    total = (gb[0] + dot(scaled, grad[0], TN)).astype(BF16)
    for r, out in enumerate(outs):

        @pl.when(pl.program_id(0) == r)
        def _():
            out[0] = total
            out[1] = gc[0]


def input_kernel(first, lengths, pre, right, taps, out, here, away):
    rows = pre.shape[2]

    @pl.when(pl.program_id(0) == 0)
    def _():
        start = first[0]
        _, high = doc_bounds(start, lengths, rows)
        for j in range(1, 4):
            sub = iota((rows, rows), 0)
            lane = iota((rows, rows), 1)
            here[j - 1] = ((sub == lane + j) & (sub + start <= high)).astype(BF16)
            sub = iota((HALO, rows), 0) + rows
            lane = iota((HALO, rows), 1)
            away[j - 1] = ((sub == lane + j) & (sub + start <= high)).astype(F32)

    w = taps[0]
    total = w[:, 0:1] * pre[0].astype(F32)
    for j in range(1, 4):
        far = dot(right[0], away[j - 1].astype(BF16), TN)
        total = total + w[:, j : j + 1] * (dot(pre[0], here[j - 1]) + far)
    out[0] = jnp.transpose(total).astype(BF16)


def spread_kernel(parts, *refs, groups):
    out = refs[groups + 1]
    total = parts[0].astype(F32)
    for i in range(1, parts.shape[0]):
        total = total + parts[i].astype(F32)
    out[...] = jnp.broadcast_to(total.astype(out.dtype), out.shape)


def final_kernel(core, mine, other, weight, bias, rate, skip):
    each = mine.shape[0]
    heads = rate.shape[1]
    for g in range(bias.shape[0]):
        ours = core[0] == g // each
        rows = jnp.where(ours, mine[g % each], other[g % each])
        for i in range(bias.shape[1] // 128):
            at = slice(i * 128, (i + 1) * 128)
            for j in range(4):
                weight[j, g : g + 1, at] = rows[i * 5 + j : i * 5 + j + 1]
            bias[g : g + 1, at] = rows[i * 5 + 4 : i * 5 + 5]
        rate[g : g + 1] = rows[20:21, :heads]
        skip[g : g + 1] = rows[20:21, heads : 2 * heads]


def pair_sum_kernel(*refs):
    parts, outs = refs[:-2], refs[-2:]
    for i, out in enumerate(outs):
        total = parts[0][i].astype(F32)
        for part in parts[1:]:
            total = total + part[i].astype(F32)
        out[...] = total


def sum_kernel(parts, *refs):
    out = refs[-1]
    total = parts[0].astype(F32)
    for i in range(1, parts.shape[0]):
        total = total + parts[i].astype(F32)
    out[...] = total.astype(out.dtype)


ANY = pl.BlockSpec(memory_space=pl.ANY)
SMEM = pl.BlockSpec(memory_space=pltpu.SMEM)


def whole(shape):
    return pl.BlockSpec(shape, lambda *i: (0,) * len(shape))


def by_group(array, at=0):
    tail = tuple(array.shape[1:])
    return pl.BlockSpec((1,) + tail, lambda g: (g + at,) + (0,) * len(tail))


def array(shape, dtype):
    return jax.ShapeDtypeStruct(shape, dtype)


def call(kernel, grid, ins, outs, flops=0, nbytes=0, scratch=(), alias=None, mib=24):
    return pl.pallas_call(
        kernel,
        grid=grid,
        in_specs=[s for s, _ in ins],
        out_specs=[s for s, _ in outs],
        out_shape=[o for _, o in outs],
        scratch_shapes=list(scratch),
        input_output_aliases=alias or {},
        cost_estimate=pl.CostEstimate(flops=flops, bytes_accessed=nbytes, transcendentals=0),
        compiler_params=pltpu.CompilerParams(vmem_limit_bytes=mib * 1024 * 1024),
    )(*[a for _, a in ins])


def shifted(block, axis, distance):
    size = lax.axis_size(axis)
    route = [(i, i + distance) for i in range(size) if 0 <= i + distance < size]
    return lax.ppermute(block, axis, route)


def body(
    conv_input,
    output_grad,
    b_matrix,
    c_matrix,
    step_size,
    decay_rate,
    skip_gain,
    conv_weight,
    conv_bias,
    saved_state,
    doc_lengths,
):
    _, rows, groups, features = conv_input.shape
    heads = step_size.shape[3]
    blocks = lax.axis_size("context")
    first = (lax.axis_index("context") * rows).astype(jnp.int32).reshape(1)
    x = jnp.transpose(conv_input[0], (1, 0, 2))
    gy = jnp.transpose(output_grad[0], (1, 0, 2))
    bm = jnp.transpose(b_matrix[0], (1, 0, 2))
    cm = jnp.transpose(c_matrix[0], (1, 0, 2))
    step = jnp.transpose(step_size[0], (1, 2, 0))
    state = saved_state.reshape(groups, features, 128)
    taps = jnp.concatenate(
        [
            jnp.transpose(conv_weight, (1, 2, 0)),
            conv_bias[:, :, None],
            jnp.zeros((groups, features, 3), F32),
        ],
        axis=2,
    )
    sent = shifted(conv_input[0, rows - HALO :], "context", 1)
    halo = jnp.transpose(sent, (1, 0, 2))

    wide = array((groups, features, rows), BF16)
    per_row = array((groups, 3, heads, rows), F32)
    quads = [[q * groups + r for r in range(groups)] for q in range(blocks // groups)]
    size = features + EXTRA
    pay = array((groups, size, 128), BF16)
    pay, gyt, rows_in = call(
        offset_kernel,
        (groups,),
        [(SMEM, a) for a in (first, doc_lengths, decay_rate)]
        + [(by_group(a), a) for a in (step, gy, cm)],
        [(by_group(a), a) for a in (pay, wide, per_row)],
        flops=10**9,
        nbytes=4 * 10**6,
        mib=60,
        scratch=(pltpu.VMEM((rows, rows), BF16),),
    )

    def across(block, axis, among=None):
        return lax.all_to_all(block, axis, 0, 0, axis_index_groups=among, tiled=True)

    got = across(pay, "context", quads)
    quad = array((size, 128), BF16)
    (quad,) = call(
        quad_kernel,
        (),
        [(whole(got.shape), got)],
        [(whole(quad.shape), quad)],
        flops=10**7,
        nbytes=10**6,
    )
    near = shifted(quad, "context", -groups)
    far = shifted(quad, "context", -2 * groups)
    lags = array((groups, 4, features, rows), BF16)
    lagged, conv, upd, slope = call(
        conv_kernel,
        (groups,),
        [(SMEM, first), (SMEM, doc_lengths)]
        + [(by_group(a), a) for a in (x, halo, step, taps)]
        + [(ANY, quad)],
        [(by_group(a), a) for a in (lags, wide, wide, wide)],
        flops=4 * 10**9,
        nbytes=10 * 10**6,
        mib=60,
    )
    states = array((groups, features, 128), BF16)
    (states,) = call(
        scan_kernel,
        (),
        [(whole(a.shape), a) for a in (got, near, far)] + [(ANY, upd)],
        [(whole(states.shape), states)],
        flops=10**7,
        nbytes=10**6,
    )
    gram_out = array((groups, rows, 128), BF16)
    gram_out32 = array((groups, rows, 128), F32)
    part, heads_in, gc, gb = call(
        intra_kernel,
        (groups,),
        [(SMEM, first), (SMEM, doc_lengths), (SMEM, skip_gain)]
        + [(by_group(a), a) for a in (conv, upd, gy, gyt, bm, cm, step, rows_in, state)]
        + [(ANY, states)],
        [(by_group(a), a) for a in (wide, per_row, gram_out, gram_out32)],
        flops=16 * 10**9,
        nbytes=10 * 10**6,
        mib=60,
        scratch=(pltpu.VMEM((rows, rows), F32), pltpu.VMEM((features, rows), F32)),
    )
    grad = across(states, "context", quads)

    copies = lax.axis_size("dp")
    halves = 2 if copies % 2 == 0 else 1
    each = groups // halves
    parts = lax.axis_size("tensor")
    shares = array((copies // halves, halves, each, ROWS, 128), BF16)
    step_out = array((groups, heads, rows), F32)
    edges = array((groups, HALO, features), BF16)
    shared, grad_step, pre, edge = call(
        carry_kernel,
        (groups,),
        [(SMEM, decay_rate)]
        + [
            (by_group(a), a)
            for a in (grad, bm, step, rows_in, heads_in, state, lagged, conv, slope, part)
        ]
        + [(ANY, gc)],
        [
            (
                pl.BlockSpec(
                    (copies // halves, 1, 1, ROWS, 128),
                    lambda g: (0, g // each, g % each, 0, 0),
                ),
                shares,
            ),
        ]
        + [(by_group(a), a) for a in (step_out, wide, edges)],
        flops=10**9,
        nbytes=8 * 10**6,
        mib=60,
        scratch=(pltpu.VMEM((3, features, rows), BF16), pltpu.VMEM((rows, rows), BF16)),
    )
    assert parts in (1, groups)
    index = lax.axis_index("tensor").astype(jnp.int32).reshape(1)

    def turned(a):
        tail = tuple(a.shape[1:])
        return pl.BlockSpec(
            (1,) + tail, lambda r, i: ((i[0] + r) % groups,) + (0,) * len(tail)
        )

    pair = (2, rows, 128)
    held = pl.pallas_call(
        grad_b_kernel,
        grid_spec=pltpu.PrefetchScalarGridSpec(
            num_scalar_prefetch=1,
            grid=(groups,),
            in_specs=[turned(a) for a in (rows_in, upd, grad, gb, gc)] + [ANY],
            out_specs=[pl.BlockSpec(pair, lambda r, i: (0, 0, 0))] * groups,
        ),
        out_shape=[array(pair, BF16)] * groups,
        cost_estimate=pl.CostEstimate(flops=10**8, bytes_accessed=2 * 10**6, transcendentals=0),
        compiler_params=pltpu.CompilerParams(vmem_limit_bytes=24 * 1024 * 1024),
    )(index, rows_in, upd, grad, gb, gc, shared)

    small = (each, ROWS, 128)
    shared = across(shared.reshape((copies,) + small), "dp")
    spread = array((blocks,) + small, BF16)
    right = shifted(edge, "context", -1)
    shared, *held = call(
        functools.partial(spread_kernel, groups=groups),
        (),
        [(whole(shared.shape), shared)] + [(ANY, h) for h in held] + [(ANY, right)],
        [(whole(spread.shape), spread)] + [(ANY, array(pair, BF16))] * groups,
        alias={1 + i: 1 + i for i in range(groups)},
    )
    shared = across(shared, "context")
    part_out = array((rows, 128), F32)

    def pair_sum(held):
        return call(
            pair_sum_kernel,
            (),
            [(whole(pair), h) for h in held],
            [(whole(part_out.shape), part_out)] * 2,
        )

    if parts == groups:
        held = [
            lax.ppermute(h, "tensor", [(i, (i + r) % parts) for i in range(parts)]) if r else h
            for r, h in enumerate(held)
        ]
        grad_b, grad_c = [p[None] for p in pair_sum(held)]
    else:
        grad_b, grad_c = [jnp.stack(p) for p in zip(*[pair_sum([h]) for h in held])]
    natural = array((groups, rows, features), BF16)
    (grad_input,) = call(
        input_kernel,
        (groups,),
        [(SMEM, first), (SMEM, doc_lengths)] + [(by_group(a), a) for a in (pre, right, taps)],
        [(by_group(natural), natural)],
        flops=10**9,
        nbytes=4 * 10**6,
        mib=60,
        scratch=(pltpu.VMEM((3, rows, rows), BF16), pltpu.VMEM((3, HALO, rows), F32)),
    )
    (mine,) = call(
        sum_kernel,
        (),
        [(whole(shared.shape), shared), (ANY, grad_input)],
        [(whole(small), array(small, F32))],
    )
    core = lax.axis_index("dp") % halves
    other = mine
    if halves == 2:
        other = lax.ppermute(mine, "dp", [(i, i ^ 1) for i in range(copies)])
    outs = [(4, groups, features), (groups, features), (groups, heads), (groups, heads)]
    weight, bias, rate, skip = call(
        final_kernel,
        (),
        [(SMEM, core.astype(jnp.int32).reshape(1)), (whole(small), mine), (whole(small), other)],
        [(whole(o), array(o, F32)) for o in outs],
    )
    return (
        jnp.transpose(grad_input, (1, 0, 2))[None],
        jnp.transpose(grad_b[None], (0, 2, 1, 3)),
        jnp.transpose(grad_c[None], (0, 2, 1, 3)),
        jnp.transpose(grad_step, (2, 0, 1))[None],
        weight,
        bias,
        rate,
        skip,
    )


def solution(mesh):
    return jax.shard_map(
        body,
        mesh=mesh,
        in_specs=(
            P("dp", "context", None, "tensor"),
            P("dp", "context", None, "tensor"),
            P("dp", "context", None, None),
            P("dp", "context", None, None),
            P("dp", "context", None, "tensor"),
            P(None, "tensor"),
            P(None, "tensor"),
            P(None, None, "tensor"),
            P(None, "tensor"),
            P("dp", "context", None, "tensor", None, None),
            P("dp", None),
        ),
        out_specs=(
            P("dp", "context", None, "tensor"),
            P("dp", "context", "tensor", None),
            P("dp", "context", "tensor", None),
            P("dp", "context", None, "tensor"),
            P(None, None, "tensor"),
            P(None, "tensor"),
            P(None, "tensor"),
            P(None, "tensor"),
        ),
        check_vma=False,
    )
```

time: 173 us -> 136 us (0.79)
  blocking collectives: 16.8 us -> 0 us
  waiting for transfers between devices: 34.5 us -> 20.4 us
  Pallas kernels: 43.7 us -> 35.6 us
  local copies, waits for them, and re-layouts: 13.2 us -> 15.7 us
    all_to_all x4, waiting for transfers between devices: 23.8 us -> 5.47 us  [across(): lax.all_to_all(block, axis, 0, 0, axis_index_groups=among, tiled=True)]
    all_to_all x1 -> x0, blocking collectives: 16.8 us -> none  [body(): lax.all_to_all(shares.reshape((copies,) + small), 'dp', 0, 0, tiled=True)]
    ppermute x0 -> x3, starting transfers between devices: none -> 10.7 us  [body(): lax.ppermute(h, 'tensor', [(i, (i + r) % parts) for i in range(parts)])]
    all_to_all x4, starting transfers between devices: 47.5 us -> 39.2 us  [across(): lax.all_to_all(block, axis, 0, 0, axis_index_groups=among, tiled=True)]
    pallas_call x11 -> x12, Pallas kernels: 43.7 us -> 35.6 us  [the longest x11 34.4 us: call(): pl.pallas_call(kernel, grid=grid, in_specs=[s for s, _ in ins], out_specs...]
    ppermute x1, starting transfers between devices: 8.67 us -> 3.31 us  [body(): other = lax.ppermute(mine, 'dp', [(i, i ^ 1) for i in range(copies)])]
    ppermute x2 -> x4, waiting for transfers between devices: 10.6 us -> 14.9 us  [shifted(): return lax.ppermute(block, axis, route)]
    ppermute x2 -> x4, starting transfers between devices: 4.53 us -> 7.22 us  [shifted(): return lax.ppermute(block, axis, route)]
  transfers between devices with their start and end apart: 7 -> 12, of which waited for: 4 -> 4; matrix products, arithmetic and copies ran while one was open for 4% -> 5% of each run, Pallas kernels for 16% -> 16%
where the time goes in v3:
time: 136 us; the launch traced here: 134 us
  starting transfers between devices  60.4 us (44%)
  Pallas kernels  35.6 us (26%)
  waiting for transfers between devices  20.4 us (15%)
  local copies, waits for them, and re-layouts  15.7 us (12%)
    all_to_all x4, starting transfers between devices, across(): lax.all_to_all(block, axis, 0, 0, axis_index_groups=among, tiled=True)  39.2 us
    pallas_call x11, Pallas kernels, call(): pl.pallas_call(kernel, grid=grid, in_specs=[s for s, _ in ins], out_specs...  34.4 us
    unnamed x40, local copies, waits for them, and re-layouts  15.3 us
    ppermute x4, waiting for transfers between devices, shifted(): return lax.ppermute(block, axis, route)  14.9 us
    ppermute x3, starting transfers between devices, body(): lax.ppermute(h, 'tensor', [(i, (i + r) % parts) for i in range(parts)])  10.7 us
    ppermute x4, starting transfers between devices, shifted(): return lax.ppermute(block, axis, route)  7.22 us
    all_to_all x4, waiting for transfers between devices, across(): lax.all_to_all(block, axis, 0, 0, axis_index_groups=among, tiled=True)  5.47 us
    ppermute x1, starting transfers between devices, body(): other = lax.ppermute(mine, 'dp', [(i, i ^ 1) for i in range(copies)])  3.31 us
  transfers between devices with their start and end apart: 12, of which 4 were waited for; matrix products, arithmetic and copies ran while one was open for 5% of the time, Pallas kernels for 16%

profile of v3, /device:TPU:1, one launch (start us, length us, event | category | flops | bytes accessed | tf_op | source)
XLA Modules:
  0.0 134.4 jit_solution(2810263093856279469)
XLA Ops:
  0.6 2.5 %copy.69 = bf16[1,256,4,512]{3,1,2,0:T(8,128)(2,1)} copy(bf16[1,256,4,512]{3,2,1,0:T(4,128)(2,1)} %param.12) | data formatting | bytes 2097152 | tf_op args[1]
  3.1 1.7 %copy.71 = bf16[1,256,4,128]{3,1,2,0:T(8,128)(2,1)} copy(bf16[1,256,4,128]{3,2,1,0:T(4,128)(2,1)} %param.14) | data formatting | bytes 524288 | tf_op args[3]
  4.8 4.1 %shard_map.170 = (bf16[4,528,128]{2,1,0:T(8,128)(2,1)}, bf16[4,512,256]{2,1,0:T(8,128)(2,1)}, f32[4,3,8,256]{3,2,1,0:T(8,128)}) custom-call(s32[1]{0:T(128)} %bitcast.first, s32[1,6]{1,0:T(1,128)} %lengths.7, f32[4,8]{1,0:T(4,128)} %rate.3, f32[4,8,256]{2,1,0:T(8,128)} %bitcast.56, bf16[4,256,512]{2,1,0:T(8,128)(2,1)} %bitcast.50, bf16[4,256,128]{2,1,0:T(8,128)(2,1)} %bitcast.54), custom_call_target="tpu_custom_call" | custom-call | flops 1000000000 | bytes 4000000 | tf_op jit(solution)/shard_map/pallas_call | solution.py:379
  8.9 6.4 %all-to-all-start = ((bf16[4,528,128]{2,1,0:T(8,128)(2,1)}), bf16[4,528,128]{2,1,0:T(8,128)(2,1)S(1)}, u32[]{:S(2)}, u32[]{:S(2)}) async-start(bf16[4,528,128]{2,1,0:T(8,128)(2,1)} %get-tuple-element.38), calls=%async_computation | async-start | bytes 1081344 | tf_op jit(solution)/shard_map/all_to_all | solution.py:450
  15.3 0.2 copy.72
  15.5 1.0 copy-done.11
  16.5 3.4 %collective-permute-start.2 = (bf16[8,4,512]{2,0,1:T(8,128)(2,1)S(1)}, bf16[8,4,512]{2,0,1:T(8,128)(2,1)S(1)}, u32[]{:S(2)}, u32[]{:S(2)}) collective-permute-start(bf16[8,4,512]{2,0,1:T(8,128)(2,1)S(1)} %slice_bitcast_fusion), channel_id=1, source_target_pairs={{0,32},{32,64},{64,96},{96,128},{128,160},{160,192},{192,224},{224... | collective-permute-start | bytes 98312 | tf_op jit(solution)/shard_map/ppermute | solution.py:395
  19.9 0.4 copy.58
  20.3 0.4 copy.59
  20.7 0.1 pad.2.clone
  20.7 1.4 %maximum_maximum_fusion.taps = f32[4,512,8]{2,1,0:T(8,128)} fusion(f32[4,512,1]{2,1,0:T(8,128)S(1)} %copy.59, f32[4,512,4]{2,1,0:T(8,128)S(1)} %bitcast.46, f32[8]{0:T(128)S(1)} %pad.2.clone), kind=kLoop, calls=%fused_computation | loop fusion | flops 32768 | bytes 106528 | tf_op jit(solution)/shard_map/concatenate | solution.py:421
  22.1 4.3 %all-to-all-done.got = bf16[4,528,128]{2,1,0:T(8,128)(2,1)S(1)} async-done(((bf16[4,528,128]{2,1,0:T(8,128)(2,1)}), bf16[4,528,128]{2,1,0:T(8,128)(2,1)S(1)}, u32[]{:S(2)}, u32[]{:S(2)}) %all-to-all-start) | async-done | bytes 540704 | tf_op jit(solution)/shard_map/all_to_all | solution.py:450
  26.4 0.1 shard_map.171.after
  26.5 1.3 collective-permute-start
  27.8 1.3 collective-permute-start.1
  29.1 0.0 collective-permute-done.2
  29.1 0.0 copy-start.16
  29.2 0.6 copy-done.16
  29.8 6.9 %shard_map.172 = (bf16[4,4,512,256]{3,2,1,0:T(8,128)(2,1)}, bf16[4,512,256]{2,1,0:T(8,128)(2,1)}, bf16[4,512,256]{2,1,0:T(8,128)(2,1)}, bf16[4,512,256]{2,1,0:T(8,128)(2,1)}) custom-call(s32[1]{0:T(128)} %bitcast.first, s32[1,6]{1,0:T(1,128)} %lengths.7, bf16[4,256,512]{2,1,0:T(8,128)(2,1)} %bitcast.47, bf16[4,8,512]{2,1,0:T(8,128)(2,1)} %bitcast.64, ...), custom_call_target="tpu_custom_call" | custom-call | flops 4000000000 | bytes 10000000 | tf_op jit(solution)/shard_map/pallas_call | solution.py:379
  36.7 14.3 %collective-permute-done.near = bf16[528,128]{1,0:T(8,128)(2,1)S(1)} collective-permute-done((bf16[528,128]{1,0:T(8,128)(2,1)S(1)}, bf16[528,128]{1,0:T(8,128)(2,1)S(1)}, u32[]{:S(2)}, u32[]{:S(2)}) %collective-permute-start) | collective-permute-done | bytes 135200 | tf_op jit(solution)/shard_map/ppermute | solution.py:395
  51.0 0.0 collective-permute-done.1.far
  51.0 1.2 copy-done.2
  52.2 0.9 shard_map.173.after
  53.1 8.7 %all-to-all-start.1 = ((bf16[4,512,128]{2,1,0:T(8,128)(2,1)}), bf16[4,512,128]{2,1,0:T(8,128)(2,1)S(1)}, u32[]{:S(2)}, u32[]{:S(2)}) async-start(bf16[4,512,128]{2,1,0:T(8,128)(2,1)} %shard_map.173.after), calls=%async_computation.1 | async-start | bytes 1048576 | tf_op jit(solution)/shard_map/all_to_all | solution.py:450
  61.9 0.7 copy.70
  62.6 7.5 %shard_map.174 = (bf16[4,512,256]{2,1,0:T(8,128)(2,1)}, f32[4,3,8,256]{3,2,1,0:T(8,128)}, bf16[4,256,128]{2,1,0:T(8,128)(2,1)}, f32[4,256,128]{2,1,0:T(8,128)}) custom-call(s32[1]{0:T(128)} %bitcast.first, s32[1,6]{1,0:T(1,128)} %lengths.7, f32[4,8]{1,0:T(4,128)} %skip.1, bf16[4,512,256]{2,1,0:T(8,128)(2,1)} %get-tuple-element.41.conv, ...), custom_call_target="tpu_custom_call" | custom-call | flops 16000000000 | bytes 10000000 | tf_op jit(solution)/shard_map/pallas_call | solution.py:379
  70.1 1.1 all-to-all-done.1.grad
  71.2 0.8 copy-done
  72.0 7.6 %shard_map.175 = (bf16[4,2,2,24,128]{4,3,2,1,0:T(8,128)(2,1)}, f32[4,8,256]{2,1,0:T(8,128)}, bf16[4,512,256]{2,1,0:T(8,128)(2,1)}, bf16[4,8,512]{2,1,0:T(8,128)(2,1)}) custom-call(f32[4,8]{1,0:T(4,128)} %rate.3, bf16[4,512,128]{2,1,0:T(8,128)(2,1)} %copy-done, bf16[4,256,128]{2,1,0:T(8,128)(2,1)} %bitcast.49, f32[4,8,256]{2,1,0:T(8,128)} %bitcast.59, ...), custom_call_target="tpu_custom_call" | custom-call | flops 1000000000 | bytes 8000000 | tf_op jit(solution)/shard_map/pallas_call | solution.py:379
  79.6 13.7 %all-to-all-start.2 = ((bf16[8,2,24,128]{3,2,1,0:T(8,128)(2,1)}), bf16[8,2,24,128]{3,2,1,0:T(8,128)(2,1)S(1)}, u32[]{:S(2)}, u32[]{:S(2)}) async-start(bf16[8,2,24,128]{3,2,1,0:T(8,128)(2,1)} %bitcast.45), calls=%async_computation.2 | async-start | bytes 196608 | tf_op jit(solution)/shard_map/all_to_all | solution.py:450
  93.3 1.3 collective-permute-start.3
  94.6 1.0 copy-done.1
  95.7 0.9 copy-done.8
  96.6 1.2 shard_map.177
  97.8 0.6 collective-permute-done.3.right.refs_4_
  98.5 0.7 shard_map.178
  99.2 10.4 %all-to-all-start.3 = ((bf16[16,2,24,128]{3,2,1,0:T(8,128)(2,1)}), bf16[16,2,24,128]{3,2,1,0:T(8,128)(2,1)S(1)}, u32[]{:S(2)}, u32[]{:S(2)}) async-start(bf16[16,2,24,128]{3,2,1,0:T(8,128)(2,1)} %get-tuple-element.63), calls=%async_computation.3 | async-start | bytes 393216 | tf_op jit(solution)/shard_map/all_to_all | solution.py:450
  109.5 3.2 %collective-permute-start.4 = (bf16[2,256,128]{2,1,0:T(8,128)(2,1)S(1)}, bf16[2,256,128]{2,1,0:T(8,128)(2,1)S(1)}, u32[]{:S(2)}, u32[]{:S(2)}) collective-permute-start(bf16[2,256,128]{2,1,0:T(8,128)(2,1)S(1)} %get-tuple-element.57), channel_id=1, source_target_pairs={{0,1},{1,2},{2,3},{3,0},{4,5},{5,6},{6,7},{7,4},{8,9},{9,10},{10,1... | collective-permute-start | bytes 393224 | tf_op jit(solution)/shard_map/ppermute | solution.py:579
  112.7 4.5 %collective-permute-start.5 = (bf16[2,256,128]{2,1,0:T(8,128)(2,1)S(1)}, bf16[2,256,128]{2,1,0:T(8,128)(2,1)S(1)}, u32[]{:S(2)}, u32[]{:S(2)}) collective-permute-start(bf16[2,256,128]{2,1,0:T(8,128)(2,1)S(1)} %get-tuple-element.58), channel_id=1, source_target_pairs={{0,2},{1,3},{2,0},{3,1},{4,6},{5,7},{6,4},{7,5},{8,10},{9,11},{10,... | collective-permute-start | bytes 393224 | tf_op jit(solution)/shard_map/ppermute | solution.py:579
  117.3 3.0 %collective-permute-start.6 = (bf16[2,256,128]{2,1,0:T(8,128)(2,1)S(1)}, bf16[2,256,128]{2,1,0:T(8,128)(2,1)S(1)}, u32[]{:S(2)}, u32[]{:S(2)}) collective-permute-start(bf16[2,256,128]{2,1,0:T(8,128)(2,1)S(1)} %get-tuple-element.59), channel_id=1, source_target_pairs={{0,3},{1,0},{2,1},{3,2},{4,7},{5,4},{6,5},{7,6},{8,11},{9,8},{10,9... | collective-permute-start | bytes 393224 | tf_op jit(solution)/shard_map/ppermute | solution.py:579
  120.3 5.2 %shard_map.176.refs_0_ = bf16[4,256,512]{2,1,0:T(8,128)(2,1)} custom-call(s32[1]{0:T(128)} %bitcast.first, s32[1,6]{1,0:T(1,128)} %lengths.7, bf16[4,512,256]{2,1,0:T(8,128)(2,1)} %get-tuple-element.48.pre, bf16[4,8,512]{2,1,0:T(8,128)(2,1)} %copy-done.10, f32[4,512,8]{2,1,0:T(8,128)} %maximum_maximum_fusion.taps), custom_call_target="tpu_custom_call" | custom-call | flops 1000000000 | bytes 4000000 | tf_op jit(solution)/shard_map/pallas_call | solution.py:379
  125.4 1.2 copy-done.4
  126.7 3.3 %collective-permute-start.7 = (f32[2,24,128]{2,1,0:T(8,128)S(1)}, f32[2,24,128]{2,1,0:T(8,128)S(1)}, u32[]{:S(2)}, u32[]{:S(2)}) collective-permute-start(f32[2,24,128]{2,1,0:T(8,128)S(1)} %shard_map.180.mine), channel_id=1, source_target_pairs={{0,4},{4,0},{8,12},{12,8},{16,20},{20,16},{24,28},{28,24},{1,5},{5... | collective-permute-start | bytes 73736 | tf_op jit(solution)/shard_map/ppermute | solution.py:605
  130.0 3.0 %copy.61 = bf16[1,256,4,512]{3,2,1,0:T(4,128)(2,1)} copy(bf16[1,256,4,512]{3,1,2,0:T(8,128)(2,1)} %bitcast.44) | data formatting | bytes 2097152
  133.0 0.0 collective-permute-done.4.refs_1_
  133.0 0.0 collective-permute-done.5.refs_2_
  133.1 0.7 shard_map.179
  133.8 0.7 shard_map.181
  (33 shorter events, 0.1 us)
Async XLA Ops:
  0.6 14.7 %copy-start.12 = (bf16[1,256,4,512]{3,2,1,0:T(4,128)(2,1)S(1)}, bf16[1,256,4,512]{3,2,1,0:T(4,128)(2,1)}, u32[]{:S(2)}) copy-start(bf16[1,256,4,512]{3,2,1,0:T(4,128)(2,1)} %param.11) | copy-start | bytes 3145732
  3.1 16.8 %copy-start.14 = (f32[4,4,512]{2,1,0:T(4,128)S(1)}, f32[4,4,512]{2,1,0:T(4,128)}, u32[]{:S(2)}) copy-start(f32[4,4,512]{2,1,0:T(4,128)} %param.18) | copy-start | bytes 98308
  3.1 17.1 %copy-start.15 = (f32[4,512]{1,0:T(4,128)S(1)}, f32[4,512]{1,0:T(4,128)}, u32[]{:S(2)}) copy-start(f32[4,512]{1,0:T(4,128)} %param.19) | copy-start | bytes 24580
  8.9 17.5 %all-to-all-start = ((bf16[4,528,128]{2,1,0:T(8,128)(2,1)}), bf16[4,528,128]{2,1,0:T(8,128)(2,1)S(1)}, u32[]{:S(2)}, u32[]{:S(2)}) async-start(bf16[4,528,128]{2,1,0:T(8,128)(2,1)} %get-tuple-element.38), calls=%async_computation | async-start | bytes 1081344 | tf_op jit(solution)/shard_map/all_to_all | solution.py:450
  15.5 1.0 copy-start.11
  16.5 12.6 %collective-permute-start.2 = (bf16[8,4,512]{2,0,1:T(8,128)(2,1)S(1)}, bf16[8,4,512]{2,0,1:T(8,128)(2,1)S(1)}, u32[]{:S(2)}, u32[]{:S(2)}) collective-permute-start(bf16[8,4,512]{2,0,1:T(8,128)(2,1)S(1)} %slice_bitcast_fusion), channel_id=1, source_target_pairs={{0,32},{32,64},{64,96},{96,128},{128,160},{160,192},{192,224},{224... | collective-permute-start | bytes 98312 | tf_op jit(solution)/shard_map/ppermute | solution.py:395
  26.5 2.6 %copy-start.9 = (bf16[528,128]{1,0:T(8,128)(2,1)}, bf16[528,128]{1,0:T(8,128)(2,1)S(1)}, u32[]{:S(2)}) copy-start(bf16[528,128]{1,0:T(8,128)(2,1)S(1)} %shard_map.171.after) | copy-start | bytes 405508
  26.5 24.4 %collective-permute-start = (bf16[528,128]{1,0:T(8,128)(2,1)S(1)}, bf16[528,128]{1,0:T(8,128)(2,1)S(1)}, u32[]{:S(2)}, u32[]{:S(2)}) collective-permute-start(bf16[528,128]{1,0:T(8,128)(2,1)S(1)} %shard_map.171.after), channel_id=1, source_target_pairs={{128,0},{160,32},{192,64},{224,96},{256,128},{288,160},{320,192},{... | collective-permute-start | bytes 405512 | tf_op jit(solution)/shard_map/ppermute | solution.py:395
  27.8 23.1 %collective-permute-start.1 = (bf16[528,128]{1,0:T(8,128)(2,1)S(1)}, bf16[528,128]{1,0:T(8,128)(2,1)S(1)}, u32[]{:S(2)}, u32[]{:S(2)}) collective-permute-start(bf16[528,128]{1,0:T(8,128)(2,1)S(1)} %shard_map.171.after), channel_id=1, source_target_pairs={{256,0},{288,32},{320,64},{352,96},{384,128},{416,160},{448,192},{... | collective-permute-start | bytes 405512 | tf_op jit(solution)/shard_map/ppermute | solution.py:395
  29.1 0.6 copy-start.16
  29.8 32.1 %copy-start.13 = (bf16[1,256,4,128]{3,2,1,0:T(4,128)(2,1)S(1)}, bf16[1,256,4,128]{3,2,1,0:T(4,128)(2,1)}, u32[]{:S(2)}) copy-start(bf16[1,256,4,128]{3,2,1,0:T(4,128)(2,1)} %param.13) | copy-start | bytes 786436
  51.0 1.2 copy-start.2
  53.1 18.1 %all-to-all-start.1 = ((bf16[4,512,128]{2,1,0:T(8,128)(2,1)}), bf16[4,512,128]{2,1,0:T(8,128)(2,1)S(1)}, u32[]{:S(2)}, u32[]{:S(2)}) async-start(bf16[4,512,128]{2,1,0:T(8,128)(2,1)} %shard_map.173.after), calls=%async_computation.1 | async-start | bytes 1048576 | tf_op jit(solution)/shard_map/all_to_all | solution.py:450
  71.2 0.8 copy-start
  72.0 22.6 %copy-start.3 = (bf16[4,512,256]{2,1,0:T(8,128)(2,1)S(1)}, bf16[4,512,256]{2,1,0:T(8,128)(2,1)}, u32[]{:S(2)}) copy-start(bf16[4,512,256]{2,1,0:T(8,128)(2,1)} %get-tuple-element.39.after.upd) | copy-start | bytes 3145732
  72.0 22.6 %copy-start.5 = (bf16[4,256,128]{2,1,0:T(8,128)(2,1)S(1)}, bf16[4,256,128]{2,1,0:T(8,128)(2,1)}, u32[]{:S(2)}) copy-start(bf16[4,256,128]{2,1,0:T(8,128)(2,1)} %get-tuple-element.47.after.gc) | copy-start | bytes 786436
  72.0 22.6 %copy-start.6 = (f32[4,256,128]{2,1,0:T(8,128)S(1)}, f32[4,256,128]{2,1,0:T(8,128)}, u32[]{:S(2)}) copy-start(f32[4,256,128]{2,1,0:T(8,128)} %get-tuple-element.51.gb) | copy-start | bytes 1572868
  72.0 22.6 %copy-start.7 = (f32[4,3,8,256]{3,2,1,0:T(8,128)S(1)}, f32[4,3,8,256]{3,2,1,0:T(8,128)}, u32[]{:S(2)}) copy-start(f32[4,3,8,256]{3,2,1,0:T(8,128)} %get-tuple-element.40.rows_in) | copy-start | bytes 294916
  79.6 18.8 %all-to-all-start.2 = ((bf16[8,2,24,128]{3,2,1,0:T(8,128)(2,1)}), bf16[8,2,24,128]{3,2,1,0:T(8,128)(2,1)S(1)}, u32[]{:S(2)}, u32[]{:S(2)}) async-start(bf16[8,2,24,128]{3,2,1,0:T(8,128)(2,1)} %bitcast.45), calls=%async_computation.2 | async-start | bytes 196608 | tf_op jit(solution)/shard_map/all_to_all | solution.py:450
  93.3 5.2 %collective-permute-start.3 = (bf16[4,8,512]{2,1,0:T(8,128)(2,1)}, bf16[4,8,512]{2,1,0:T(8,128)(2,1)S(1)}, u32[]{:S(2)}, u32[]{:S(2)}) collective-permute-start(bf16[4,8,512]{2,1,0:T(8,128)(2,1)} %get-tuple-element.49), channel_id=1, source_target_pairs={{32,0},{64,32},{96,64},{128,96},{160,128},{192,160},{224,192},{256... | collective-permute-start | bytes 98312 | tf_op jit(solution)/shard_map/ppermute | solution.py:395
  94.6 1.0 copy-start.1
  95.7 0.9 copy-start.8
  98.4 21.8 %copy-start.10 = (bf16[4,8,512]{2,1,0:T(8,128)(2,1)}, bf16[4,8,512]{2,1,0:T(8,128)(2,1)S(1)}, u32[]{:S(2)}) copy-start(bf16[4,8,512]{2,1,0:T(8,128)(2,1)S(1)} %collective-permute-done.3.right.refs_4_) | copy-start | bytes 98308
  99.2 26.3 %all-to-all-start.3 = ((bf16[16,2,24,128]{3,2,1,0:T(8,128)(2,1)}), bf16[16,2,24,128]{3,2,1,0:T(8,128)(2,1)S(1)}, u32[]{:S(2)}, u32[]{:S(2)}) async-start(bf16[16,2,24,128]{3,2,1,0:T(8,128)(2,1)} %get-tuple-element.63), calls=%async_computation.3 | async-start | bytes 393216 | tf_op jit(solution)/shard_map/all_to_all | solution.py:450
  109.5 23.5 %collective-permute-start.4 = (bf16[2,256,128]{2,1,0:T(8,128)(2,1)S(1)}, bf16[2,256,128]{2,1,0:T(8,128)(2,1)S(1)}, u32[]{:S(2)}, u32[]{:S(2)}) collective-permute-start(bf16[2,256,128]{2,1,0:T(8,128)(2,1)S(1)} %get-tuple-element.57), channel_id=1, source_target_pairs={{0,1},{1,2},{2,3},{3,0},{4,5},{5,6},{6,7},{7,4},{8,9},{9,10},{10,1... | collective-permute-start | bytes 393224 | tf_op jit(solution)/shard_map/ppermute | solution.py:579
  112.7 20.3 %collective-permute-start.5 = (bf16[2,256,128]{2,1,0:T(8,128)(2,1)S(1)}, bf16[2,256,128]{2,1,0:T(8,128)(2,1)S(1)}, u32[]{:S(2)}, u32[]{:S(2)}) collective-permute-start(bf16[2,256,128]{2,1,0:T(8,128)(2,1)S(1)} %get-tuple-element.58), channel_id=1, source_target_pairs={{0,2},{1,3},{2,0},{3,1},{4,6},{5,7},{6,4},{7,5},{8,10},{9,11},{10,... | collective-permute-start | bytes 393224 | tf_op jit(solution)/shard_map/ppermute | solution.py:579
  117.3 15.8 %collective-permute-start.6 = (bf16[2,256,128]{2,1,0:T(8,128)(2,1)S(1)}, bf16[2,256,128]{2,1,0:T(8,128)(2,1)S(1)}, u32[]{:S(2)}, u32[]{:S(2)}) collective-permute-start(bf16[2,256,128]{2,1,0:T(8,128)(2,1)S(1)} %get-tuple-element.59), channel_id=1, source_target_pairs={{0,3},{1,0},{2,1},{3,2},{4,7},{5,4},{6,5},{7,6},{8,11},{9,8},{10,9... | collective-permute-start | bytes 393224 | tf_op jit(solution)/shard_map/ppermute | solution.py:579
  125.4 1.2 copy-start.4
  126.7 7.1 %collective-permute-start.7 = (f32[2,24,128]{2,1,0:T(8,128)S(1)}, f32[2,24,128]{2,1,0:T(8,128)S(1)}, u32[]{:S(2)}, u32[]{:S(2)}) collective-permute-start(f32[2,24,128]{2,1,0:T(8,128)S(1)} %shard_map.180.mine), channel_id=1, source_target_pairs={{0,4},{4,0},{8,12},{12,8},{16,20},{20,16},{24,28},{28,24},{1,5},{5... | collective-permute-start | bytes 73736 | tf_op jit(solution)/shard_map/ppermute | solution.py:605

commit v4 on v3

--- a/solution.py
+++ b/solution.py
@@ -59,7 +59,7 @@
     return out[:count] + out[count : 2 * count] + out[2 * count :]
 
 
-def offset_kernel(first, lengths, rate, step, gy, cm, pay, gyt, rows_out, tri):
+def offset_kernel(shift, first, lengths, rate, step, gy, cm, pay, gyt, rows_out, tri):
     g = pl.program_id(0)
 
     @pl.when(g == 0)
@@ -127,21 +127,36 @@
             out[r, at] = state.astype(BF16)
 
 
-def conv_kernel(first, lengths, x, halo, step, taps, after, lagged, conv, upd, slope):
-    heads = step.shape[1]
-    rows = step.shape[2]
+def lag_masks(first, lengths, here, away):
+    rows = here.shape[2]
     start = first[0]
     low, _ = doc_bounds(start, lengths, rows)
-    sub = iota((rows, rows), 0)
-    lane = iota((rows, rows), 1)
+    for j in range(1, 4):
+        sub = iota((rows, rows), 0)
+        lane = iota((rows, rows), 1)
+        here[j - 1] = ((sub + j == lane) & (sub + start >= low)).astype(BF16)
+        sub = iota((HALO, rows), 0) - HALO
+        lane = iota((HALO, rows), 1)
+        away[j - 1] = ((sub + j == lane) & (sub + start >= low)).astype(F32)
+
+
+def lag(xt, halo, here, away, j):
+    return dot(xt, here[j - 1]) + dot(halo, away[j - 1].astype(BF16), TN)
+
+
+def conv_kernel(
+    first, lengths, x, halo, step, taps, after, lagged, conv, upd, slope, here, away
+):
+    heads = step.shape[1]
+
+    @pl.when(pl.program_id(0) == 0)
+    def _():
+        lag_masks(first, lengths, here, away)
+
     xt = jnp.transpose(x[0].astype(F32)).astype(BF16)
     lagged[0, 0] = xt
-    hsub = iota((HALO, rows), 0)
-    hlane = iota((HALO, rows), 1)
     for j in range(1, 4):
-        here = ((sub + j == lane) & (sub + start >= low)).astype(BF16)
-        away = ((hsub - HALO + j == hlane) & (hsub - HALO + start >= low)).astype(BF16)
-        lagged[0, j] = (dot(xt, here) + dot(halo[0], away, TN)).astype(BF16)
+        lagged[0, j] = lag(xt, halo[0], here, away, j).astype(BF16)
     for h in range(heads):
         at = slice(h * HEAD, (h + 1) * HEAD)
         w = taps[0, at]
@@ -210,20 +225,20 @@
         axis=0,
     )
     gc[0] = (dot(grad_gram, bm[0]) + dot(scaled, state[0], TN)).astype(BF16)
-    gb[0] = dot(grad_gram, cm[0], TN)
+    gb[0] = dot(grad_gram, cm[0], TN).astype(BF16)
 
 
 def carry_kernel(
-    rate, grad, bm, step, rows_in, heads_in, state, lagged, conv, slope, part,
-    after, pay, grad_step, pre_out, edge, prods, tri,
+    index, rate, grad, bm, step, rows_in, heads_in, state, lagged, conv, slope, part, gb, gc,
+    pay, grad_step, pre_out, edge, kept, sent, prods, scaled, tri,
 ):
-    group = pl.program_id(0)
-
-    @pl.when(group == 0)
+    turn = pl.program_id(0)
+    group = index[0] ^ turn
+
+    @pl.when(turn == 0)
     def _():
         size = tri.shape
         tri[...] = (iota(size, 0) >= iota(size, 1)).astype(BF16)
-
     heads = step.shape[1]
     rows = step.shape[2]
     carry = dot(grad[0], bm[0], NT)
@@ -235,12 +250,15 @@
         at = slice(h * HEAD, (h + 1) * HEAD)
         cb = carry[at]
         st = step[0, h : h + 1]
-        along = jnp.where(spot == h, jnp.sum(cb * conv[0, at].astype(F32), axis=0, keepdims=True), along)
+        co = conv[0, at].astype(F32)
+        along = jnp.where(spot == h, jnp.sum(cb * co, axis=0, keepdims=True), along)
+        weight = st * to_end[h : h + 1]
+        scaled[at] = (weight * co).astype(BF16)
         prod = grad[0, at].astype(F32) * state[0, at].astype(F32)
         inner = jnp.where(
             iota((heads, 128), 0) == h, jnp.sum(prod, axis=0, keepdims=True), inner
         )
-        gp = part[0, at].astype(F32) + (st * to_end[h : h + 1]) * cb
+        gp = part[0, at].astype(F32) + weight * cb
         gp = gp * slope[0, at].astype(F32)
         pre_out[0, at] = gp.astype(BF16)
         terms = [gp * lagged[0, j, at].astype(F32) for j in range(4)] + [gp]
@@ -248,6 +266,14 @@
             lanes = slice(j % 2 * 128, j % 2 * 128 + 128)
             prods[j // 2, at, lanes] = (term[:, :128] + term[:, 128:]).astype(BF16)
         prods[2, at, 128:] = gp[:, :128].astype(BF16)
+    total_b = (gb[0].astype(F32) + dot(scaled[...], grad[0], TN)).astype(BF16)
+    for out, here in ((kept, turn < 2), (sent, turn >= 2)):
+
+        @pl.when(here)
+        def _():
+            out[0, 0] = total_b
+            out[0, 1] = gc[0]
+
     along = along * to_end
     step_two = along
     along = along * step[0]
@@ -277,24 +303,6 @@
     pay[:, 0, 0] = jnp.broadcast_to(total.astype(BF16), (pay.shape[0], ROWS, 128))
 
 
-def grad_b_kernel(index, rows_in, upd, grad, gb, gc, after, *outs):
-    heads = rows_in.shape[2]
-    scaled = jnp.concatenate(
-        [
-            (upd[0, h * HEAD : (h + 1) * HEAD].astype(F32) * rows_in[0, 2, h : h + 1]).astype(BF16)
-            for h in range(heads)
-        ],
-        axis=0,
-    )
-    total = (gb[0] + dot(scaled, grad[0], TN)).astype(BF16)
-    for r, out in enumerate(outs):
-
-        @pl.when(pl.program_id(0) == r)
-        def _():
-            out[0] = total
-            out[1] = gc[0]
-
-
 def input_kernel(first, lengths, pre, right, taps, out, here, away):
     rows = pre.shape[2]
 
@@ -318,8 +326,7 @@
     out[0] = jnp.transpose(total).astype(BF16)
 
 
-def spread_kernel(parts, *refs, groups):
-    out = refs[groups + 1]
+def spread_kernel(parts, after, out):
     total = parts[0].astype(F32)
     for i in range(1, parts.shape[0]):
         total = total + parts[i].astype(F32)
@@ -341,13 +348,14 @@
         skip[g : g + 1] = rows[20:21, heads : 2 * heads]
 
 
-def pair_sum_kernel(*refs):
-    parts, outs = refs[:-2], refs[-2:]
-    for i, out in enumerate(outs):
-        total = parts[0][i].astype(F32)
-        for part in parts[1:]:
-            total = total + part[i].astype(F32)
-        out[...] = total
+def meet_kernel(kept, got, after, mine, passed):
+    mine[...] = kept[0].astype(F32) + got[0].astype(F32)
+    passed[...] = (kept[1].astype(F32) + got[1].astype(F32)).astype(BF16)
+
+
+def pair_sum_kernel(mine, got, one, two):
+    one[...] = mine[0] + got[0].astype(F32)
+    two[...] = mine[1] + got[1].astype(F32)
 
 
 def sum_kernel(parts, *refs):
@@ -373,6 +381,10 @@
 
 def array(shape, dtype):
     return jax.ShapeDtypeStruct(shape, dtype)
+
+
+def in_hbm(a):
+    return pltpu.with_memory_space_constraint(a, pltpu.HBM)
 
 
 def call(kernel, grid, ins, outs, flops=0, nbytes=0, scratch=(), alias=None, mib=24):
@@ -434,17 +446,42 @@
     quads = [[q * groups + r for r in range(groups)] for q in range(blocks // groups)]
     size = features + EXTRA
     pay = array((groups, size, 128), BF16)
-    pay, gyt, rows_in = call(
+    count = len(quads)
+
+    def owner(q, e):
+        return q * groups + (e + (2 * q >= count)) % groups
+
+    def to_earlier(block, distance):
+        route = [
+            (owner(q, e), owner(q - distance, e))
+            for q in range(distance, count)
+            for e in range(groups)
+        ]
+        return lax.ppermute(block, "context", route)
+
+    shift = (lax.axis_index("context") * 2 >= blocks).astype(jnp.int32).reshape(1)
+
+    def plain(a):
+        tail = tuple(a.shape[1:])
+        return pl.BlockSpec((1,) + tail, lambda g, i: (g,) + (0,) * len(tail))
+
+    pay, gyt, rows_in = pl.pallas_call(
         offset_kernel,
-        (groups,),
-        [(SMEM, a) for a in (first, doc_lengths, decay_rate)]
-        + [(by_group(a), a) for a in (step, gy, cm)],
-        [(by_group(a), a) for a in (pay, wide, per_row)],
-        flops=10**9,
-        nbytes=4 * 10**6,
-        mib=60,
-        scratch=(pltpu.VMEM((rows, rows), BF16),),
-    )
+        grid_spec=pltpu.PrefetchScalarGridSpec(
+            num_scalar_prefetch=1,
+            grid=(groups,),
+            in_specs=[SMEM] * 3 + [plain(a) for a in (step, gy, cm)],
+            out_specs=[
+                pl.BlockSpec((1, size, 128), lambda g, i: ((g + i[0]) % groups, 0, 0)),
+                plain(wide),
+                plain(per_row),
+            ],
+            scratch_shapes=[pltpu.VMEM((rows, rows), BF16)],
+        ),
+        out_shape=[pay, wide, per_row],
+        cost_estimate=pl.CostEstimate(flops=10**9, bytes_accessed=4 * 10**6, transcendentals=0),
+        compiler_params=pltpu.CompilerParams(vmem_limit_bytes=60 * 1024 * 1024),
+    )(shift, first, doc_lengths, decay_rate, step, gy, cm)
 
     def across(block, axis, among=None):
         return lax.all_to_all(block, axis, 0, 0, axis_index_groups=among, tiled=True)
@@ -459,8 +496,9 @@
         flops=10**7,
         nbytes=10**6,
     )
-    near = shifted(quad, "context", -groups)
-    far = shifted(quad, "context", -2 * groups)
+    near = to_earlier(quad, 1)
+    far = to_earlier(quad, 2)
+    masks = (pltpu.VMEM((3, rows, rows), BF16), pltpu.VMEM((3, HALO, rows), F32))
     lags = array((groups, 4, features, rows), BF16)
     lagged, conv, upd, slope = call(
         conv_kernel,
@@ -472,6 +510,7 @@
         flops=4 * 10**9,
         nbytes=10 * 10**6,
         mib=60,
+        scratch=masks,
     )
     states = array((groups, features, 128), BF16)
     (states,) = call(
@@ -483,14 +522,13 @@
         nbytes=10**6,
     )
     gram_out = array((groups, rows, 128), BF16)
-    gram_out32 = array((groups, rows, 128), F32)
     part, heads_in, gc, gb = call(
         intra_kernel,
         (groups,),
         [(SMEM, first), (SMEM, doc_lengths), (SMEM, skip_gain)]
         + [(by_group(a), a) for a in (conv, upd, gy, gyt, bm, cm, step, rows_in, state)]
         + [(ANY, states)],
-        [(by_group(a), a) for a in (wide, per_row, gram_out, gram_out32)],
+        [(by_group(a), a) for a in (wide, per_row, gram_out, gram_out)],
         flops=16 * 10**9,
         nbytes=10 * 10**6,
         mib=60,
@@ -505,93 +543,87 @@
     shares = array((copies // halves, halves, each, ROWS, 128), BF16)
     step_out = array((groups, heads, rows), F32)
     edges = array((groups, HALO, features), BF16)
-    shared, grad_step, pre, edge = call(
-        carry_kernel,
-        (groups,),
-        [(SMEM, decay_rate)]
-        + [
-            (by_group(a), a)
-            for a in (grad, bm, step, rows_in, heads_in, state, lagged, conv, slope, part)
-        ]
-        + [(ANY, gc)],
-        [
-            (
-                pl.BlockSpec(
-                    (copies // halves, 1, 1, ROWS, 128),
-                    lambda g: (0, g // each, g % each, 0, 0),
-                ),
-                shares,
-            ),
-        ]
-        + [(by_group(a), a) for a in (step_out, wide, edges)],
-        flops=10**9,
-        nbytes=8 * 10**6,
-        mib=60,
-        scratch=(pltpu.VMEM((3, features, rows), BF16), pltpu.VMEM((rows, rows), BF16)),
-    )
-    assert parts in (1, groups)
-    index = lax.axis_index("tensor").astype(jnp.int32).reshape(1)
+    assert parts == groups == 4
+    index = jnp.concatenate([lax.axis_index("tensor").astype(jnp.int32).reshape(1), shift])
 
     def turned(a):
         tail = tuple(a.shape[1:])
-        return pl.BlockSpec(
-            (1,) + tail, lambda r, i: ((i[0] + r) % groups,) + (0,) * len(tail)
-        )
-
+        return pl.BlockSpec((1,) + tail, lambda r, i: (i[0] ^ r,) + (0,) * len(tail))
+
+    ins = (grad, bm, step, rows_in, heads_in, state, lagged, conv, slope, part, gb, gc)
     pair = (2, rows, 128)
-    held = pl.pallas_call(
-        grad_b_kernel,
+    twice = array((2,) + pair, BF16)
+    shared, grad_step, pre, edge, kept, sent = pl.pallas_call(
+        carry_kernel,
         grid_spec=pltpu.PrefetchScalarGridSpec(
             num_scalar_prefetch=1,
             grid=(groups,),
-            in_specs=[turned(a) for a in (rows_in, upd, grad, gb, gc)] + [ANY],
-            out_specs=[pl.BlockSpec(pair, lambda r, i: (0, 0, 0))] * groups,
+            in_specs=[
+                SMEM,
+                pl.BlockSpec(
+                    (1, features, 128), lambda r, i: (((i[0] ^ r) + i[1]) % groups, 0, 0)
+                ),
+            ]
+            + [turned(a) for a in ins[1:]],
+            out_specs=[
+                pl.BlockSpec(
+                    (copies // halves, 1, 1, ROWS, 128),
+                    lambda r, i: (0, (i[0] ^ r) // each, (i[0] ^ r) % each, 0, 0),
+                )
+            ]
+            + [turned(a) for a in (step_out, wide, edges)]
+            + [
+                pl.BlockSpec((1,) + pair, lambda r, i: (jnp.minimum(r, 1), 0, 0, 0)),
+                pl.BlockSpec((1,) + pair, lambda r, i: (jnp.maximum(r - 2, 0), 0, 0, 0)),
+            ],
+            scratch_shapes=[
+                pltpu.VMEM((3, features, rows), BF16),
+                pltpu.VMEM((features, rows), BF16),
+                pltpu.VMEM((rows, rows), BF16),
+            ],
         ),
-        out_shape=[array(pair, BF16)] * groups,
-        cost_estimate=pl.CostEstimate(flops=10**8, bytes_accessed=2 * 10**6, transcendentals=0),
-        compiler_params=pltpu.CompilerParams(vmem_limit_bytes=24 * 1024 * 1024),
-    )(index, rows_in, upd, grad, gb, gc, shared)
+        out_shape=[shares, step_out, wide, edges, twice, twice],
+        cost_estimate=pl.CostEstimate(flops=10**9, bytes_accessed=8 * 10**6, transcendentals=0),
+        compiler_params=pltpu.CompilerParams(vmem_limit_bytes=60 * 1024 * 1024),
+    )(index, decay_rate, *ins)
+
+    def exchanged(block, bit):
+        return lax.ppermute(block, "tensor", [(i, i ^ bit) for i in range(parts)])
 
     small = (each, ROWS, 128)
     shared = across(shared.reshape((copies,) + small), "dp")
     spread = array((blocks,) + small, BF16)
     right = shifted(edge, "context", -1)
-    shared, *held = call(
-        functools.partial(spread_kernel, groups=groups),
+    (shared,) = call(
+        spread_kernel,
         (),
-        [(whole(shared.shape), shared)] + [(ANY, h) for h in held] + [(ANY, right)],
-        [(whole(spread.shape), spread)] + [(ANY, array(pair, BF16))] * groups,
-        alias={1 + i: 1 + i for i in range(groups)},
-    )
-    shared = across(shared, "context")
-    part_out = array((rows, 128), F32)
-
-    def pair_sum(held):
-        return call(
-            pair_sum_kernel,
-            (),
-            [(whole(pair), h) for h in held],
-            [(whole(part_out.shape), part_out)] * 2,
-        )
-
-    if parts == groups:
-        held = [
-            lax.ppermute(h, "tensor", [(i, (i + r) % parts) for i in range(parts)]) if r else h
-            for r, h in enumerate(held)
-        ]
-        grad_b, grad_c = [p[None] for p in pair_sum(held)]
-    else:
-        grad_b, grad_c = [jnp.stack(p) for p in zip(*[pair_sum([h]) for h in held])]
+        [(whole(shared.shape), shared), (ANY, right)],
+        [(whole(spread.shape), spread)],
+    )
     natural = array((groups, rows, features), BF16)
     (grad_input,) = call(
         input_kernel,
         (groups,),
-        [(SMEM, first), (SMEM, doc_lengths)] + [(by_group(a), a) for a in (pre, right, taps)],
+        [(SMEM, first), (SMEM, doc_lengths)] + [(by_group(a), a) for a in (in_hbm(pre), right, taps)],
         [(by_group(natural), natural)],
         flops=10**9,
         nbytes=4 * 10**6,
-        mib=60,
         scratch=(pltpu.VMEM((3, rows, rows), BF16), pltpu.VMEM((3, HALO, rows), F32)),
+    )
+    got = exchanged(sent, 2)
+    part_out = array((rows, 128), F32)
+    mine_b, passed = call(
+        meet_kernel,
+        (),
+        [(whole(twice.shape), kept), (whole(twice.shape), got), (ANY, grad_input)],
+        [(whole(pair), array(pair, F32)), (whole(pair), array(pair, BF16))],
+    )
+    shared = across(shared, "context")
+    grad_b, grad_c = call(
+        pair_sum_kernel,
+        (),
+        [(whole(pair), mine_b), (whole(pair), exchanged(passed, 1))],
+        [(whole(part_out.shape), part_out)] * 2,
     )
     (mine,) = call(
         sum_kernel,
@@ -612,8 +644,8 @@
     )
     return (
         jnp.transpose(grad_input, (1, 0, 2))[None],
-        jnp.transpose(grad_b[None], (0, 2, 1, 3)),
-        jnp.transpose(grad_c[None], (0, 2, 1, 3)),
+        grad_b.reshape(1, rows, 1, 128),
+        grad_c.reshape(1, rows, 1, 128),
         jnp.transpose(grad_step, (2, 0, 1))[None],
         weight,
         bias,

time: 136 us -> 131 us (0.963)
  waiting for transfers between devices: 20.4 us -> 25.9 us
  starting transfers between devices: 60.4 us -> 55 us
  local copies, waits for them, and re-layouts: 15.7 us -> 11.4 us
    ppermute x3 -> x4, waiting for transfers between devices: 0.01 us -> 15.8 us  [the longest x2 14.9 us: to_earlier(): return lax.ppermute(block, 'context', route)]
    pallas_call x11 -> x10, Pallas kernels: 34.4 us -> 22.1 us  [call(): pl.pallas_call(kernel, grid=grid, in_specs=[s for s, _ in ins], out_specs...]
    pallas_call x1 -> x2, Pallas kernels: 1.24 us -> 13.2 us  [the longest x1 9.09 us: body(): pl.pallas_call(carry_kernel, grid_spec=pltpu.PrefetchScalarGridSpec(num_s...]
    ppermute x4 -> x2, waiting for transfers between devices: 14.9 us -> 3.87 us  [shifted(): return lax.ppermute(block, axis, route)]
    all_to_all x4, starting transfers between devices: 39.2 us -> 33.6 us  [across(): lax.all_to_all(block, axis, 0, 0, axis_index_groups=among, tiled=True)]
    unnamed x40 -> x30, local copies, waits for them, and re-layouts: 15.3 us -> 10.9 us
    ppermute x1, starting transfers between devices: 3.31 us -> 6.09 us  [body(): other = lax.ppermute(mine, 'dp', [(i, i ^ 1) for i in range(copies)])]
    ppermute x4 -> x2, starting transfers between devices: 7.22 us -> 4.64 us  [shifted(): return lax.ppermute(block, axis, route)]
  transfers between devices with their start and end apart: 12 -> 11, of which waited for: 4 -> 6; matrix products, arithmetic and copies ran while one was open for 5% -> 4% of each run, Pallas kernels for 16% -> 15%
where the time goes in v4:
time: 131 us; the launch traced here: 130 us
  starting transfers between devices  55 us (42%)
  Pallas kernels  35.2 us (27%)
  waiting for transfers between devices  25.9 us (20%)
  local copies, waits for them, and re-layouts  11.4 us (9%)
  other arithmetic  2.02 us (2%)
    all_to_all x4, starting transfers between devices, across(): lax.all_to_all(block, axis, 0, 0, axis_index_groups=among, tiled=True)  33.6 us
    pallas_call x10, Pallas kernels, call(): pl.pallas_call(kernel, grid=grid, in_specs=[s for s, _ in ins], out_specs...  22.1 us
    ppermute x2, waiting for transfers between devices, to_earlier(): return lax.ppermute(block, 'context', route)  14.9 us
    unnamed x30, local copies, waits for them, and re-layouts  10.9 us
    pallas_call x1, Pallas kernels, body(): pl.pallas_call(carry_kernel, grid_spec=pltpu.PrefetchScalarGridSpec(num_s...  9.09 us
    ppermute x2, starting transfers between devices, exchanged(): return lax.ppermute(block, 'tensor', [(i, i ^ bit) for i in range(parts)])  8.03 us
    all_to_all x4, waiting for transfers between devices, across(): lax.all_to_all(block, axis, 0, 0, axis_index_groups=among, tiled=True)  6.27 us
    ppermute x1, starting transfers between devices, body(): other = lax.ppermute(mine, 'dp', [(i, i ^ 1) for i in range(copies)])  6.09 us
  transfers between devices with their start and end apart: 11, of which 6 were waited for; matrix products, arithmetic and copies ran while one was open for 4% of the time, Pallas kernels for 15%

profile of v4, /device:TPU:1, one launch (start us, length us, event | category | flops | bytes accessed | tf_op | source)
XLA Modules:
  0.0 130.4 jit_solution(17447142535169709048)
XLA Ops:
  0.7 1.8 %copy.67 = bf16[1,256,4,128]{3,1,2,0:T(8,128)(2,1)} copy(bf16[1,256,4,128]{3,2,1,0:T(4,128)(2,1)} %param.14) | data formatting | bytes 524288 | tf_op args[3]
  2.4 2.4 %copy.65 = bf16[1,256,4,512]{3,1,2,0:T(8,128)(2,1)} copy(bf16[1,256,4,512]{3,2,1,0:T(4,128)(2,1)} %param.12) | data formatting | bytes 2097152 | tf_op args[1]
  4.8 4.1 %shard_map.170 = (bf16[4,528,128]{2,1,0:T(8,128)(2,1)}, bf16[4,512,256]{2,1,0:T(8,128)(2,1)}, f32[4,3,8,256]{3,2,1,0:T(8,128)}) custom-call(s32[1]{0:T(128)} %bitcast.2.shift, s32[1]{0:T(128)} %bitcast.first, s32[1,6]{1,0:T(1,128)} %lengths.7, f32[4,8]{1,0:T(4,128)} %rate.3, f32[4,8,256]{2,1,0:T(8,128)} %bitcast.57, bf16[4,256,512]{2,1,0:T(8,128)(2,1)} %bitcast.48, ...), custom_call_target="tpu_custom_call" | custom-call | flops 1000000000 | bytes 4000000 | tf_op jit(solution)/shard_map/pallas_call | solution.py:468
  8.9 6.6 %all-to-all-start = ((bf16[4,528,128]{2,1,0:T(8,128)(2,1)}), bf16[4,528,128]{2,1,0:T(8,128)(2,1)S(1)}, u32[]{:S(2)}, u32[]{:S(2)}) async-start(bf16[4,528,128]{2,1,0:T(8,128)(2,1)} %get-tuple-element.33), calls=%async_computation | async-start | bytes 1081344 | tf_op jit(solution)/shard_map/all_to_all | solution.py:487
  15.5 0.2 copy.68
  15.7 1.0 copy-done.6
  16.7 3.4 %collective-permute-start.2 = (bf16[8,4,512]{2,0,1:T(8,128)(2,1)S(1)}, bf16[8,4,512]{2,0,1:T(8,128)(2,1)S(1)}, u32[]{:S(2)}, u32[]{:S(2)}) collective-permute-start(bf16[8,4,512]{2,0,1:T(8,128)(2,1)S(1)} %slice_bitcast_fusion), channel_id=1, source_target_pairs={{0,32},{32,64},{64,96},{96,128},{128,160},{160,192},{192,224},{224... | collective-permute-start | bytes 98312 | tf_op jit(solution)/shard_map/ppermute | solution.py:407
  20.1 0.4 copy.54
  20.5 0.4 copy.55
  20.8 0.1 pad.2.clone
  20.9 1.4 %maximum_maximum_fusion.taps = f32[4,512,8]{2,1,0:T(8,128)} fusion(f32[4,512,1]{2,1,0:T(8,128)S(1)} %copy.55, f32[4,512,4]{2,1,0:T(8,128)S(1)} %bitcast.46, f32[8]{0:T(128)S(1)} %pad.2.clone), kind=kLoop, calls=%fused_computation | loop fusion | flops 32768 | bytes 106528 | tf_op jit(solution)/shard_map/concatenate | solution.py:433
  22.3 0.7 copy.66
  23.0 3.6 %all-to-all-done.got = bf16[4,528,128]{2,1,0:T(8,128)(2,1)S(1)} async-done(((bf16[4,528,128]{2,1,0:T(8,128)(2,1)}), bf16[4,528,128]{2,1,0:T(8,128)(2,1)S(1)}, u32[]{:S(2)}, u32[]{:S(2)}) %all-to-all-start) | async-done | bytes 540704 | tf_op jit(solution)/shard_map/all_to_all | solution.py:487
  26.6 0.1 shard_map.171.after
  26.7 1.3 collective-permute-start.1
  28.0 1.3 collective-permute-start
  29.3 0.0 collective-permute-done.2
  29.3 0.0 copy-start.11
  29.3 0.6 copy-done.11
  29.9 7.2 %shard_map.172 = (bf16[4,4,512,256]{3,2,1,0:T(8,128)(2,1)}, bf16[4,512,256]{2,1,0:T(8,128)(2,1)}, bf16[4,512,256]{2,1,0:T(8,128)(2,1)}, bf16[4,512,256]{2,1,0:T(8,128)(2,1)}) custom-call(s32[1]{0:T(128)} %bitcast.first, s32[1,6]{1,0:T(1,128)} %lengths.7, bf16[4,256,512]{2,1,0:T(8,128)(2,1)} %bitcast.47, bf16[4,8,512]{2,1,0:T(8,128)(2,1)} %bitcast.65, ...), custom_call_target="tpu_custom_call" | custom-call | flops 4000000000 | bytes 10000000 | tf_op jit(solution)/shard_map/pallas_call | solution.py:391
  37.1 5.4 %collective-permute-done.1.far = bf16[528,128]{1,0:T(8,128)(2,1)S(1)} collective-permute-done((bf16[528,128]{1,0:T(8,128)(2,1)S(1)}, bf16[528,128]{1,0:T(8,128)(2,1)S(1)}, u32[]{:S(2)}, u32[]{:S(2)}) %collective-permute-start.1) | collective-permute-done | bytes 135200 | tf_op jit(solution)/shard_map/ppermute | solution.py:460
  42.5 9.4 %collective-permute-done.near = bf16[528,128]{1,0:T(8,128)(2,1)S(1)} collective-permute-done((bf16[528,128]{1,0:T(8,128)(2,1)S(1)}, bf16[528,128]{1,0:T(8,128)(2,1)S(1)}, u32[]{:S(2)}, u32[]{:S(2)}) %collective-permute-start) | collective-permute-done | bytes 135200 | tf_op jit(solution)/shard_map/ppermute | solution.py:460
  52.0 1.2 copy-done
  53.2 0.9 shard_map.173.after
  54.1 5.2 %all-to-all-start.1 = ((bf16[4,512,128]{2,1,0:T(8,128)(2,1)}), bf16[4,512,128]{2,1,0:T(8,128)(2,1)S(1)}, u32[]{:S(2)}, u32[]{:S(2)}) async-start(bf16[4,512,128]{2,1,0:T(8,128)(2,1)} %shard_map.173.after), calls=%async_computation.1 | async-start | bytes 1048576 | tf_op jit(solution)/shard_map/all_to_all | solution.py:487
  59.3 0.6 pad_add_fusion.index
  60.0 7.5 %shard_map.174 = (bf16[4,512,256]{2,1,0:T(8,128)(2,1)}, f32[4,3,8,256]{3,2,1,0:T(8,128)}, bf16[4,256,128]{2,1,0:T(8,128)(2,1)}, bf16[4,256,128]{2,1,0:T(8,128)(2,1)}) custom-call(s32[1]{0:T(128)} %bitcast.first, s32[1,6]{1,0:T(1,128)} %lengths.7, f32[4,8]{1,0:T(4,128)} %skip.1, bf16[4,512,256]{2,1,0:T(8,128)(2,1)} %get-tuple-element.36.conv, ...), custom_call_target="tpu_custom_call" | custom-call | flops 16000000000 | bytes 10000000 | tf_op jit(solution)/shard_map/pallas_call | solution.py:391
  67.5 2.7 %all-to-all-done.1.grad = bf16[4,512,128]{2,1,0:T(8,128)(2,1)S(1)} async-done(((bf16[4,512,128]{2,1,0:T(8,128)(2,1)}), bf16[4,512,128]{2,1,0:T(8,128)(2,1)S(1)}, u32[]{:S(2)}, u32[]{:S(2)}) %all-to-all-start.1) | async-done | bytes 524320 | tf_op jit(solution)/shard_map/all_to_all | solution.py:487
  70.2 0.8 copy-done.5
  71.0 9.1 %shard_map.175 = (bf16[4,2,2,24,128]{4,3,2,1,0:T(8,128)(2,1)}, f32[4,8,256]{2,1,0:T(8,128)}, bf16[4,512,256]{2,1,0:T(8,128)(2,1)}, bf16[4,8,512]{2,1,0:T(8,128)(...) custom-call(s32[2]{0:T(128)} %pad_add_fusion.index, f32[4,8]{1,0:T(4,128)} %rate.3, ...), custom_call_target="tpu_custom_call" | custom-call | flops 1000000000 | bytes 8000000 | tf_op jit(solution)/shard_map/pallas_call | solution.py:556
  80.1 9.0 %all-to-all-start.2 = ((bf16[8,2,24,128]{3,2,1,0:T(8,128)(2,1)}), bf16[8,2,24,128]{3,2,1,0:T(8,128)(2,1)S(1)}, u32[]{:S(2)}, u32[]{:S(2)}) async-start(bf16[8,2,24,128]{3,2,1,0:T(8,128)(2,1)} %bitcast.56), calls=%async_computation.2 | async-start | bytes 196608 | tf_op jit(solution)/shard_map/all_to_all | solution.py:487
  89.1 1.3 collective-permute-start.3
  90.4 3.9 %collective-permute-done.3.right.after = bf16[4,8,512]{2,1,0:T(8,128)(2,1)S(1)} collective-permute-done((bf16[4,8,512]{2,1,0:T(8,128)(2,1)}, bf16[4,8,512]{2,1,0:T(8,128)(2,1)S(1)}, u32[]{:S(2)}, u32[]{:S(2)}) %collective-permute-start.3) | collective-permute-done | bytes 32800 | tf_op jit(solution)/shard_map/ppermute | solution.py:407
  94.3 0.0 all-to-all-done.2.parts
  94.3 0.7 shard_map.179
  95.0 12.8 %all-to-all-start.3 = ((bf16[16,2,24,128]{3,2,1,0:T(8,128)(2,1)}), bf16[16,2,24,128]{3,2,1,0:T(8,128)(2,1)S(1)}, u32[]{:S(2)}, u32[]{:S(2)}) async-start(bf16[16,2,24,128]{3,2,1,0:T(8,128)(2,1)} %shard_map.179), calls=%async_computation.3 | async-start | bytes 393216 | tf_op jit(solution)/shard_map/all_to_all | solution.py:487
  107.8 4.8 %collective-permute-start.4 = (bf16[2,2,256,128]{3,2,1,0:T(8,128)(2,1)}, bf16[2,2,256,128]{3,2,1,0:T(8,128)(2,1)S(1)}, u32[]{:S(2)}, u32[]{:S(2)}) collective-permute-start(bf16[2,2,256,128]{3,2,1,0:T(8,128)(2,1)} %get-tuple-element.47), channel_id=1, source_target_pairs={{0,2},{1,3},{2,0},{3,1},{4,6},{5,7},{6,4},{7,5},{8,10},{9,11},{10,... | collective-permute-start | bytes 786440 | tf_op jit(solution)/shard_map/ppermute | solution.py:591
  112.7 4.2 %shard_map.176.after.refs_0_ = bf16[4,256,512]{2,1,0:T(8,128)(2,1)S(1)} custom-call(s32[1]{0:T(128)} %bitcast.first, s32[1,6]{1,0:T(1,128)S(1)} %copy-done.4, bf16[4,512,256]{2,1,0:T(8,128)(2,1)} %get-tuple-element.44.pre, bf16[4,8,512]{2,1,0:T(8,128)(2,1)S(1)} %collective-permute-done.3.right.after, f32[4,512,8]{2,1,0:T(8,128)S(1)} %copy-done.1), custom_call_target="tpu_custom_call" | custom-call | flops 1000000000 | bytes 4000000 | tf_op jit(solution)/shard_map/pallas_call | solution.py:391
  116.9 0.9 collective-permute-done.4.got
  117.8 0.1 shard_map.177
  117.9 3.2 %collective-permute-start.5 = (bf16[2,256,128]{2,1,0:T(8,128)(2,1)S(1)}, bf16[2,256,128]{2,1,0:T(8,128)(2,1)S(1)}, u32[]{:S(2)}, u32[]{:S(2)}) collective-permute-start(bf16[2,256,128]{2,1,0:T(8,128)(2,1)S(1)} %get-tuple-element.49), channel_id=1, source_target_pairs={{0,1},{1,0},{2,3},{3,2},{4,5},{5,4},{6,7},{7,6},{8,9},{9,8},{10,11... | collective-permute-start | bytes 393224 | tf_op jit(solution)/shard_map/ppermute | solution.py:591
  121.1 0.0 all-to-all-done.3.parts
  121.1 6.1 %collective-permute-start.6 = (f32[2,24,128]{2,1,0:T(8,128)S(1)}, f32[2,24,128]{2,1,0:T(8,128)S(1)}, u32[]{:S(2)}, u32[]{:S(2)}) collective-permute-start(f32[2,24,128]{2,1,0:T(8,128)S(1)} %shard_map.180.mine), channel_id=1, source_target_pairs={{0,4},{4,0},{8,12},{12,8},{16,20},{20,16},{24,28},{28,24},{1,5},{5... | collective-permute-start | bytes 73736 | tf_op jit(solution)/shard_map/ppermute | solution.py:637
  127.2 1.8 %copy.57 = bf16[1,256,4,512]{3,2,1,0:T(4,128)(2,1)} copy(bf16[1,256,4,512]{3,1,2,0:T(8,128)(2,1)S(1)} %bitcast.45) | data formatting | bytes 2097152
  129.0 0.0 collective-permute-done.5.got
  129.0 0.7 shard_map.178
  129.7 0.0 collective-permute-done.6.other
  129.7 0.7 shard_map.181
  (22 shorter events, 0.1 us)
Async XLA Ops:
  0.6 14.8 %copy-start.7 = (bf16[1,256,4,512]{3,2,1,0:T(4,128)(2,1)S(1)}, bf16[1,256,4,512]{3,2,1,0:T(4,128)(2,1)}, u32[]{:S(2)}) copy-start(bf16[1,256,4,512]{3,2,1,0:T(4,128)(2,1)} %param.11) | copy-start | bytes 3145732
  2.4 17.7 %copy-start.9 = (f32[4,4,512]{2,1,0:T(4,128)S(1)}, f32[4,4,512]{2,1,0:T(4,128)}, u32[]{:S(2)}) copy-start(f32[4,4,512]{2,1,0:T(4,128)} %param.18) | copy-start | bytes 98308
  4.8 15.6 %copy-start.10 = (f32[4,512]{1,0:T(4,128)S(1)}, f32[4,512]{1,0:T(4,128)}, u32[]{:S(2)}) copy-start(f32[4,512]{1,0:T(4,128)} %param.19) | copy-start | bytes 24580
  8.9 13.4 %copy-start.8 = (bf16[1,256,4,128]{3,2,1,0:T(4,128)(2,1)S(1)}, bf16[1,256,4,128]{3,2,1,0:T(4,128)(2,1)}, u32[]{:S(2)}) copy-start(bf16[1,256,4,128]{3,2,1,0:T(4,128)(2,1)} %param.13) | copy-start | bytes 786436
  8.9 17.7 %all-to-all-start = ((bf16[4,528,128]{2,1,0:T(8,128)(2,1)}), bf16[4,528,128]{2,1,0:T(8,128)(2,1)S(1)}, u32[]{:S(2)}, u32[]{:S(2)}) async-start(bf16[4,528,128]{2,1,0:T(8,128)(2,1)} %get-tuple-element.33), calls=%async_computation | async-start | bytes 1081344 | tf_op jit(solution)/shard_map/all_to_all | solution.py:487
  15.7 1.0 copy-start.6
  16.7 12.6 %collective-permute-start.2 = (bf16[8,4,512]{2,0,1:T(8,128)(2,1)S(1)}, bf16[8,4,512]{2,0,1:T(8,128)(2,1)S(1)}, u32[]{:S(2)}, u32[]{:S(2)}) collective-permute-start(bf16[8,4,512]{2,0,1:T(8,128)(2,1)S(1)} %slice_bitcast_fusion), channel_id=1, source_target_pairs={{0,32},{32,64},{64,96},{96,128},{128,160},{160,192},{192,224},{224... | collective-permute-start | bytes 98312 | tf_op jit(solution)/shard_map/ppermute | solution.py:407
  26.7 2.6 %copy-start.3 = (bf16[528,128]{1,0:T(8,128)(2,1)}, bf16[528,128]{1,0:T(8,128)(2,1)S(1)}, u32[]{:S(2)}) copy-start(bf16[528,128]{1,0:T(8,128)(2,1)S(1)} %shard_map.171.after) | copy-start | bytes 405508
  26.7 15.8 %collective-permute-start.1 = (bf16[528,128]{1,0:T(8,128)(2,1)S(1)}, bf16[528,128]{1,0:T(8,128)(2,1)S(1)}, u32[]{:S(2)}, u32[]{:S(2)}) collective-permute-start(bf16[528,128]{1,0:T(8,128)(2,1)S(1)} %shard_map.171.after), channel_id=1, source_target_pairs={{288,0},{320,32},{352,64},{256,96},{416,128},{448,160},{480,192},{... | collective-permute-start | bytes 405512 | tf_op jit(solution)/shard_map/ppermute | solution.py:460
  28.0 24.0 %collective-permute-start = (bf16[528,128]{1,0:T(8,128)(2,1)S(1)}, bf16[528,128]{1,0:T(8,128)(2,1)S(1)}, u32[]{:S(2)}, u32[]{:S(2)}) collective-permute-start(bf16[528,128]{1,0:T(8,128)(2,1)S(1)} %shard_map.171.after), channel_id=1, source_target_pairs={{128,0},{160,32},{192,64},{224,96},{288,128},{320,160},{352,192},{... | collective-permute-start | bytes 405512 | tf_op jit(solution)/shard_map/ppermute | solution.py:460
  29.3 0.6 copy-start.11
  52.0 1.2 copy-start
  54.1 16.0 %all-to-all-start.1 = ((bf16[4,512,128]{2,1,0:T(8,128)(2,1)}), bf16[4,512,128]{2,1,0:T(8,128)(2,1)S(1)}, u32[]{:S(2)}, u32[]{:S(2)}) async-start(bf16[4,512,128]{2,1,0:T(8,128)(2,1)} %shard_map.173.after), calls=%async_computation.1 | async-start | bytes 1048576 | tf_op jit(solution)/shard_map/all_to_all | solution.py:487
  70.2 0.8 copy-start.5
  71.0 41.7 %copy-start.1 = (f32[4,512,8]{2,1,0:T(8,128)S(1)}, f32[4,512,8]{2,1,0:T(8,128)}, u32[]{:S(2)}) copy-start(f32[4,512,8]{2,1,0:T(8,128)} %maximum_maximum_fusion.taps) | copy-start | bytes 196612
  71.0 41.7 %copy-start.4 = (s32[1,6]{1,0:T(1,128)S(1)}, s32[1,6]{1,0:T(1,128)}, u32[]{:S(2)}) copy-start(s32[1,6]{1,0:T(1,128)} %lengths.7) | copy-start | bytes 76
  80.1 37.7 %copy-start.2 = (bf16[2,2,256,128]{3,2,1,0:T(8,128)(2,1)S(1)}, bf16[2,2,256,128]{3,2,1,0:T(8,128)(2,1)}, u32[]{:S(2)}) copy-start(bf16[2,2,256,128]{3,2,1,0:T(8,128)(2,1)} %get-tuple-element.46.kept) | copy-start | bytes 786436
  80.1 14.2 %all-to-all-start.2 = ((bf16[8,2,24,128]{3,2,1,0:T(8,128)(2,1)}), bf16[8,2,24,128]{3,2,1,0:T(8,128)(2,1)S(1)}, u32[]{:S(2)}, u32[]{:S(2)}) async-start(bf16[8,2,24,128]{3,2,1,0:T(8,128)(2,1)} %bitcast.56), calls=%async_computation.2 | async-start | bytes 196608 | tf_op jit(solution)/shard_map/all_to_all | solution.py:487
  89.1 5.2 %collective-permute-start.3 = (bf16[4,8,512]{2,1,0:T(8,128)(2,1)}, bf16[4,8,512]{2,1,0:T(8,128)(2,1)S(1)}, u32[]{:S(2)}, u32[]{:S(2)}) collective-permute-start(bf16[4,8,512]{2,1,0:T(8,128)(2,1)} %get-tuple-element.45), channel_id=1, source_target_pairs={{32,0},{64,32},{96,64},{128,96},{160,128},{192,160},{224,192},{256... | collective-permute-start | bytes 98312 | tf_op jit(solution)/shard_map/ppermute | solution.py:407
  95.0 26.0 %all-to-all-start.3 = ((bf16[16,2,24,128]{3,2,1,0:T(8,128)(2,1)}), bf16[16,2,24,128]{3,2,1,0:T(8,128)(2,1)S(1)}, u32[]{:S(2)}, u32[]{:S(2)}) async-start(bf16[16,2,24,128]{3,2,1,0:T(8,128)(2,1)} %shard_map.179), calls=%async_computation.3 | async-start | bytes 393216 | tf_op jit(solution)/shard_map/all_to_all | solution.py:487
  107.8 10.0 %collective-permute-start.4 = (bf16[2,2,256,128]{3,2,1,0:T(8,128)(2,1)}, bf16[2,2,256,128]{3,2,1,0:T(8,128)(2,1)S(1)}, u32[]{:S(2)}, u32[]{:S(2)}) collective-permute-start(bf16[2,2,256,128]{3,2,1,0:T(8,128)(2,1)} %get-tuple-element.47), channel_id=1, source_target_pairs={{0,2},{1,3},{2,0},{3,1},{4,6},{5,7},{6,4},{7,5},{8,10},{9,11},{10,... | collective-permute-start | bytes 786440 | tf_op jit(solution)/shard_map/ppermute | solution.py:591
  117.9 11.2 %collective-permute-start.5 = (bf16[2,256,128]{2,1,0:T(8,128)(2,1)S(1)}, bf16[2,256,128]{2,1,0:T(8,128)(2,1)S(1)}, u32[]{:S(2)}, u32[]{:S(2)}) collective-permute-start(bf16[2,256,128]{2,1,0:T(8,128)(2,1)S(1)} %get-tuple-element.49), channel_id=1, source_target_pairs={{0,1},{1,0},{2,3},{3,2},{4,5},{5,4},{6,7},{7,6},{8,9},{9,8},{10,11... | collective-permute-start | bytes 393224 | tf_op jit(solution)/shard_map/ppermute | solution.py:591
  121.1 8.6 %collective-permute-start.6 = (f32[2,24,128]{2,1,0:T(8,128)S(1)}, f32[2,24,128]{2,1,0:T(8,128)S(1)}, u32[]{:S(2)}, u32[]{:S(2)}) collective-permute-start(f32[2,24,128]{2,1,0:T(8,128)S(1)} %shard_map.180.mine), channel_id=1, source_target_pairs={{0,4},{4,0},{8,12},{12,8},{16,20},{20,16},{24,28},{28,24},{1,5},{5... | collective-permute-start | bytes 73736 | tf_op jit(solution)/shard_map/ppermute | solution.py:637

commit v5 on v4

--- a/solution.py
+++ b/solution.py
@@ -77,8 +77,9 @@
     rows_out[0, 0] = cum
     rows_out[0, 1] = from_start
     rows_out[0, 2] = to_end
-    gt = jnp.transpose(gy[0].astype(F32))
-    gyt[0] = gt.astype(BF16)
+    gt = jnp.transpose(gy[0])
+    gyt[0] = gt
+    gt = gt.astype(F32)
     scaled = jnp.concatenate(
         [gt[h * HEAD : (h + 1) * HEAD] * from_start[h : h + 1] for h in range(heads)], axis=0
     ).astype(BF16)
@@ -153,7 +154,7 @@
     def _():
         lag_masks(first, lengths, here, away)
 
-    xt = jnp.transpose(x[0].astype(F32)).astype(BF16)
+    xt = jnp.transpose(x[0])
     lagged[0, 0] = xt
     for j in range(1, 4):
         lagged[0, j] = lag(xt, halo[0], here, away, j).astype(BF16)
@@ -323,7 +324,7 @@
     for j in range(1, 4):
         far = dot(right[0], away[j - 1].astype(BF16), TN)
         total = total + w[:, j : j + 1] * (dot(pre[0], here[j - 1]) + far)
-    out[0] = jnp.transpose(total).astype(BF16)
+    out[0] = jnp.transpose(total.astype(BF16))
 
 
 def spread_kernel(parts, after, out):
@@ -472,7 +473,7 @@
             grid=(groups,),
             in_specs=[SMEM] * 3 + [plain(a) for a in (step, gy, cm)],
             out_specs=[
-                pl.BlockSpec((1, size, 128), lambda g, i: ((g + i[0]) % groups, 0, 0)),
+                pl.BlockSpec((1, size, 128), lambda g, i: ((g + i[0]) & (groups - 1), 0, 0)),
                 plain(wide),
                 plain(per_row),
             ],
@@ -516,7 +517,7 @@
     (states,) = call(
         scan_kernel,
         (),
-        [(whole(a.shape), a) for a in (got, near, far)] + [(ANY, upd)],
+        [(whole(a.shape), a) for a in (got, near, far)] + [(ANY, in_hbm(upd))],
         [(whole(states.shape), states)],
         flops=10**7,
         nbytes=10**6,
@@ -543,7 +544,8 @@
     shares = array((copies // halves, halves, each, ROWS, 128), BF16)
     step_out = array((groups, heads, rows), F32)
     edges = array((groups, HALO, features), BF16)
-    assert parts == groups == 4
+    assert parts == groups == 4 and each & (each - 1) == 0
+    shift_each = each.bit_length() - 1
     index = jnp.concatenate([lax.axis_index("tensor").astype(jnp.int32).reshape(1), shift])
 
     def turned(a):
@@ -561,14 +563,14 @@
             in_specs=[
                 SMEM,
                 pl.BlockSpec(
-                    (1, features, 128), lambda r, i: (((i[0] ^ r) + i[1]) % groups, 0, 0)
+                    (1, features, 128), lambda r, i: (((i[0] ^ r) + i[1]) & (groups - 1), 0, 0)
                 ),
             ]
             + [turned(a) for a in ins[1:]],
             out_specs=[
                 pl.BlockSpec(
                     (copies // halves, 1, 1, ROWS, 128),
-                    lambda r, i: (0, (i[0] ^ r) // each, (i[0] ^ r) % each, 0, 0),
+                    lambda r, i: (0, (i[0] ^ r) >> shift_each, (i[0] ^ r) & (each - 1), 0, 0),
                 )
             ]
             + [turned(a) for a in (step_out, wide, edges)]
@@ -604,7 +606,7 @@
     (grad_input,) = call(
         input_kernel,
         (groups,),
-        [(SMEM, first), (SMEM, doc_lengths)] + [(by_group(a), a) for a in (in_hbm(pre), right, taps)],
+        [(SMEM, first), (SMEM, doc_lengths)] + [(by_group(a), a) for a in (pre, right, taps)],
         [(by_group(natural), natural)],
         flops=10**9,
         nbytes=4 * 10**6,

time: 131 us -> 130 us (level)
  no operation moved by 1% of the time
where the time goes in v5:
time: 130 us; the launch traced here: 129 us
  starting transfers between devices  55 us (42%)
  Pallas kernels  34.5 us (27%)
  waiting for transfers between devices  25.5 us (20%)
  local copies, waits for them, and re-layouts  11.4 us (9%)
  other arithmetic  2.02 us (2%)
    all_to_all x4, starting transfers between devices, across(): lax.all_to_all(block, axis, 0, 0, axis_index_groups=among, tiled=True)  33.6 us
    pallas_call x10, Pallas kernels, call(): pl.pallas_call(kernel, grid=grid, in_specs=[s for s, _ in ins], out_specs...  21.3 us
    ppermute x2, waiting for transfers between devices, to_earlier(): return lax.ppermute(block, 'context', route)  14.9 us
    unnamed x30, local copies, waits for them, and re-layouts  10.9 us
    pallas_call x1, Pallas kernels, body(): pl.pallas_call(carry_kernel, grid_spec=pltpu.PrefetchScalarGridSpec(num_s...  9.06 us
    ppermute x2, starting transfers between devices, exchanged(): return lax.ppermute(block, 'tensor', [(i, i ^ bit) for i in range(parts)])  8.03 us
    all_to_all x4, waiting for transfers between devices, across(): lax.all_to_all(block, axis, 0, 0, axis_index_groups=among, tiled=True)  6.27 us
    ppermute x1, starting transfers between devices, body(): other = lax.ppermute(mine, 'dp', [(i, i ^ 1) for i in range(copies)])  6.09 us
  transfers between devices with their start and end apart: 11, of which 6 were waited for; matrix products, arithmetic and copies ran while one was open for 4% of the time, Pallas kernels for 15%

profile of v5, /device:TPU:1, one launch (start us, length us, event | category | flops | bytes accessed | tf_op | source)
XLA Modules:
  0.0 129.2 jit_solution(9409122885667179619)
XLA Ops:
  0.7 1.8 %copy.67 = bf16[1,256,4,128]{3,1,2,0:T(8,128)(2,1)} copy(bf16[1,256,4,128]{3,2,1,0:T(4,128)(2,1)} %param.14) | data formatting | bytes 524288 | tf_op args[3]
  2.4 2.4 %copy.65 = bf16[1,256,4,512]{3,1,2,0:T(8,128)(2,1)} copy(bf16[1,256,4,512]{3,2,1,0:T(4,128)(2,1)} %param.12) | data formatting | bytes 2097152 | tf_op args[1]
  4.8 4.1 %shard_map.170 = (bf16[4,528,128]{2,1,0:T(8,128)(2,1)}, bf16[4,512,256]{2,1,0:T(8,128)(2,1)}, f32[4,3,8,256]{3,2,1,0:T(8,128)}) custom-call(s32[1]{0:T(128)} %bitcast.2.shift, s32[1]{0:T(128)} %bitcast.first, s32[1,6]{1,0:T(1,128)} %lengths.7, f32[4,8]{1,0:T(4,128)} %rate.3, f32[4,8,256]{2,1,0:T(8,128)} %bitcast.57, bf16[4,256,512]{2,1,0:T(8,128)(2,1)} %bitcast.48, ...), custom_call_target="tpu_custom_call" | custom-call | flops 1000000000 | bytes 4000000 | tf_op jit(solution)/shard_map/pallas_call | solution.py:469
  8.9 6.6 %all-to-all-start = ((bf16[4,528,128]{2,1,0:T(8,128)(2,1)}), bf16[4,528,128]{2,1,0:T(8,128)(2,1)S(1)}, u32[]{:S(2)}, u32[]{:S(2)}) async-start(bf16[4,528,128]{2,1,0:T(8,128)(2,1)} %get-tuple-element.33), calls=%async_computation | async-start | bytes 1081344 | tf_op jit(solution)/shard_map/all_to_all | solution.py:488
  15.5 0.2 copy.68
  15.7 1.0 copy-done.6
  16.7 3.4 %collective-permute-start.2 = (bf16[8,4,512]{2,0,1:T(8,128)(2,1)S(1)}, bf16[8,4,512]{2,0,1:T(8,128)(2,1)S(1)}, u32[]{:S(2)}, u32[]{:S(2)}) collective-permute-start(bf16[8,4,512]{2,0,1:T(8,128)(2,1)S(1)} %slice_bitcast_fusion), channel_id=1, source_target_pairs={{0,32},{32,64},{64,96},{96,128},{128,160},{160,192},{192,224},{224... | collective-permute-start | bytes 98312 | tf_op jit(solution)/shard_map/ppermute | solution.py:408
  20.1 0.4 copy.54
  20.5 0.4 copy.55
  20.8 0.1 pad.2.clone
  20.9 1.4 %maximum_maximum_fusion.taps = f32[4,512,8]{2,1,0:T(8,128)} fusion(f32[4,512,1]{2,1,0:T(8,128)S(1)} %copy.55, f32[4,512,4]{2,1,0:T(8,128)S(1)} %bitcast.46, f32[8]{0:T(128)S(1)} %pad.2.clone), kind=kLoop, calls=%fused_computation | loop fusion | flops 32768 | bytes 106528 | tf_op jit(solution)/shard_map/concatenate | solution.py:434
  22.3 0.7 copy.66
  23.0 3.6 %all-to-all-done.got = bf16[4,528,128]{2,1,0:T(8,128)(2,1)S(1)} async-done(((bf16[4,528,128]{2,1,0:T(8,128)(2,1)}), bf16[4,528,128]{2,1,0:T(8,128)(2,1)S(1)}, u32[]{:S(2)}, u32[]{:S(2)}) %all-to-all-start) | async-done | bytes 540704 | tf_op jit(solution)/shard_map/all_to_all | solution.py:488
  26.6 0.1 shard_map.171.after
  26.7 1.3 %collective-permute-start.1 = (bf16[528,128]{1,0:T(8,128)(2,1)S(1)}, bf16[528,128]{1,0:T(8,128)(2,1)S(1)}, u32[]{:S(2)}, u32[]{:S(2)}) collective-permute-start(bf16[528,128]{1,0:T(8,128)(2,1)S(1)} %shard_map.171.after), channel_id=1, source_target_pairs={{288,0},{320,32},{352,64},{256,96},{416,128},{448,160},{480,192},{... | collective-permute-start | bytes 405512 | tf_op jit(solution)/shard_map/ppermute | solution.py:461
  28.0 1.3 %collective-permute-start = (bf16[528,128]{1,0:T(8,128)(2,1)S(1)}, bf16[528,128]{1,0:T(8,128)(2,1)S(1)}, u32[]{:S(2)}, u32[]{:S(2)}) collective-permute-start(bf16[528,128]{1,0:T(8,128)(2,1)S(1)} %shard_map.171.after), channel_id=1, source_target_pairs={{128,0},{160,32},{192,64},{224,96},{288,128},{320,160},{352,192},{... | collective-permute-start | bytes 405512 | tf_op jit(solution)/shard_map/ppermute | solution.py:461
  29.3 0.0 copy-start.11
  29.3 0.6 copy-done.11
  29.9 7.1 %shard_map.172 = (bf16[4,4,512,256]{3,2,1,0:T(8,128)(2,1)}, bf16[4,512,256]{2,1,0:T(8,128)(2,1)}, bf16[4,512,256]{2,1,0:T(8,128)(2,1)}, bf16[4,512,256]{2,1,0:T(8,128)(2,1)}) custom-call(s32[1]{0:T(128)} %bitcast.first, s32[1,6]{1,0:T(1,128)} %lengths.7, bf16[4,256,512]{2,1,0:T(8,128)(2,1)} %bitcast.47, bf16[4,8,512]{2,1,0:T(8,128)(2,1)} %bitcast.65, ...), custom_call_target="tpu_custom_call" | custom-call | flops 4000000000 | bytes 10000000 | tf_op jit(solution)/shard_map/pallas_call | solution.py:392
  37.0 5.5 %collective-permute-done.1.far = bf16[528,128]{1,0:T(8,128)(2,1)S(1)} collective-permute-done((bf16[528,128]{1,0:T(8,128)(2,1)S(1)}, bf16[528,128]{1,0:T(8,128)(2,1)S(1)}, u32[]{:S(2)}, u32[]{:S(2)}) %collective-permute-start.1) | collective-permute-done | bytes 135200 | tf_op jit(solution)/shard_map/ppermute | solution.py:461
  42.5 9.5 %collective-permute-done.near = bf16[528,128]{1,0:T(8,128)(2,1)S(1)} collective-permute-done((bf16[528,128]{1,0:T(8,128)(2,1)S(1)}, bf16[528,128]{1,0:T(8,128)(2,1)S(1)}, u32[]{:S(2)}, u32[]{:S(2)}) %collective-permute-start) | collective-permute-done | bytes 135200 | tf_op jit(solution)/shard_map/ppermute | solution.py:461
  52.0 0.9 shard_map.173.after
  52.9 5.2 %all-to-all-start.1 = ((bf16[4,512,128]{2,1,0:T(8,128)(2,1)}), bf16[4,512,128]{2,1,0:T(8,128)(2,1)S(1)}, u32[]{:S(2)}, u32[]{:S(2)}) async-start(bf16[4,512,128]{2,1,0:T(8,128)(2,1)} %shard_map.173.after), calls=%async_computation.1 | async-start | bytes 1048576 | tf_op jit(solution)/shard_map/all_to_all | solution.py:488
  58.1 0.6 pad_add_fusion.index
  58.7 7.5 %shard_map.174 = (bf16[4,512,256]{2,1,0:T(8,128)(2,1)}, f32[4,3,8,256]{3,2,1,0:T(8,128)}, bf16[4,256,128]{2,1,0:T(8,128)(2,1)}, bf16[4,256,128]{2,1,0:T(8,128)(2,1)}) custom-call(s32[1]{0:T(128)} %bitcast.first, s32[1,6]{1,0:T(1,128)} %lengths.7, f32[4,8]{1,0:T(4,128)} %skip.1, bf16[4,512,256]{2,1,0:T(8,128)(2,1)} %get-tuple-element.36.conv, ...), custom_call_target="tpu_custom_call" | custom-call | flops 16000000000 | bytes 10000000 | tf_op jit(solution)/shard_map/pallas_call | solution.py:392
  66.2 2.7 %all-to-all-done.1.grad = bf16[4,512,128]{2,1,0:T(8,128)(2,1)S(1)} async-done(((bf16[4,512,128]{2,1,0:T(8,128)(2,1)}), bf16[4,512,128]{2,1,0:T(8,128)(2,1)S(1)}, u32[]{:S(2)}, u32[]{:S(2)}) %all-to-all-start.1) | async-done | bytes 524320 | tf_op jit(solution)/shard_map/all_to_all | solution.py:488
  68.9 0.8 copy-done.5
  69.8 9.1 %shard_map.175 = (bf16[4,2,2,24,128]{4,3,2,1,0:T(8,128)(2,1)}, f32[4,8,256]{2,1,0:T(8,128)}, bf16[4,512,256]{2,1,0:T(8,128)(2,1)}, bf16[4,8,512]{2,1,0:T(8,128)(...) custom-call(s32[2]{0:T(128)} %pad_add_fusion.index, f32[4,8]{1,0:T(4,128)} %rate.3, ...), custom_call_target="tpu_custom_call" | custom-call | flops 1000000000 | bytes 8000000 | tf_op jit(solution)/shard_map/pallas_call | solution.py:558
  78.8 9.0 %all-to-all-start.2 = ((bf16[8,2,24,128]{3,2,1,0:T(8,128)(2,1)}), bf16[8,2,24,128]{3,2,1,0:T(8,128)(2,1)S(1)}, u32[]{:S(2)}, u32[]{:S(2)}) async-start(bf16[8,2,24,128]{3,2,1,0:T(8,128)(2,1)} %bitcast.56), calls=%async_computation.2 | async-start | bytes 196608 | tf_op jit(solution)/shard_map/all_to_all | solution.py:488
  87.9 1.3 collective-permute-start.3
  89.2 3.9 %collective-permute-done.3.right.after = bf16[4,8,512]{2,1,0:T(8,128)(2,1)S(1)} collective-permute-done((bf16[4,8,512]{2,1,0:T(8,128)(2,1)}, bf16[4,8,512]{2,1,0:T(8,128)(2,1)S(1)}, u32[]{:S(2)}, u32[]{:S(2)}) %collective-permute-start.3) | collective-permute-done | bytes 32800 | tf_op jit(solution)/shard_map/ppermute | solution.py:408
  93.0 0.0 all-to-all-done.2.parts
  93.0 0.7 shard_map.179
  93.8 12.8 %all-to-all-start.3 = ((bf16[16,2,24,128]{3,2,1,0:T(8,128)(2,1)}), bf16[16,2,24,128]{3,2,1,0:T(8,128)(2,1)S(1)}, u32[]{:S(2)}, u32[]{:S(2)}) async-start(bf16[16,2,24,128]{3,2,1,0:T(8,128)(2,1)} %shard_map.179), calls=%async_computation.3 | async-start | bytes 393216 | tf_op jit(solution)/shard_map/all_to_all | solution.py:488
  106.6 4.8 %collective-permute-start.4 = (bf16[2,2,256,128]{3,2,1,0:T(8,128)(2,1)}, bf16[2,2,256,128]{3,2,1,0:T(8,128)(2,1)S(1)}, u32[]{:S(2)}, u32[]{:S(2)}) collective-permute-start(bf16[2,2,256,128]{3,2,1,0:T(8,128)(2,1)} %get-tuple-element.47), channel_id=1, source_target_pairs={{0,2},{1,3},{2,0},{3,1},{4,6},{5,7},{6,4},{7,5},{8,10},{9,11},{10,... | collective-permute-start | bytes 786440 | tf_op jit(solution)/shard_map/ppermute | solution.py:593
  111.4 0.0 copy-start.3
  111.4 1.2 copy-done.3
  112.6 3.5 %shard_map.176.after.refs_0_ = bf16[4,256,512]{2,1,0:T(8,128)(2,1)S(1)} custom-call(s32[1]{0:T(128)} %bitcast.first, s32[1,6]{1,0:T(1,128)S(1)} %copy-done.4, bf16[4,512,256]{2,1,0:T(8,128)(2,1)S(1)} %copy-done.3, bf16[4,8,512]{2,1,0:T(8,128)(2,1)S(1)} %collective-permute-done.3.right.after, f32[4,512,8]{2,1,0:T(8,128)S(1)} %copy-done), custom_call_target="tpu_custom_call" | custom-call | flops 1000000000 | bytes 4000000 | tf_op jit(solution)/shard_map/pallas_call | solution.py:392
  116.1 0.4 collective-permute-done.4.got
  116.5 0.1 shard_map.177
  116.6 3.2 %collective-permute-start.5 = (bf16[2,256,128]{2,1,0:T(8,128)(2,1)S(1)}, bf16[2,256,128]{2,1,0:T(8,128)(2,1)S(1)}, u32[]{:S(2)}, u32[]{:S(2)}) collective-permute-start(bf16[2,256,128]{2,1,0:T(8,128)(2,1)S(1)} %get-tuple-element.49), channel_id=1, source_target_pairs={{0,1},{1,0},{2,3},{3,2},{4,5},{5,4},{6,7},{7,6},{8,9},{9,8},{10,11... | collective-permute-start | bytes 393224 | tf_op jit(solution)/shard_map/ppermute | solution.py:593
  119.8 0.0 all-to-all-done.3.parts
  119.9 6.1 %collective-permute-start.6 = (f32[2,24,128]{2,1,0:T(8,128)S(1)}, f32[2,24,128]{2,1,0:T(8,128)S(1)}, u32[]{:S(2)}, u32[]{:S(2)}) collective-permute-start(f32[2,24,128]{2,1,0:T(8,128)S(1)} %shard_map.180.mine), channel_id=1, source_target_pairs={{0,4},{4,0},{8,12},{12,8},{16,20},{20,16},{24,28},{28,24},{1,5},{5... | collective-permute-start | bytes 73736 | tf_op jit(solution)/shard_map/ppermute | solution.py:639
  126.0 1.8 %copy.57 = bf16[1,256,4,512]{3,2,1,0:T(4,128)(2,1)} copy(bf16[1,256,4,512]{3,1,2,0:T(8,128)(2,1)S(1)} %bitcast.45) | data formatting | bytes 2097152
  127.8 0.0 collective-permute-done.5.got
  127.8 0.7 shard_map.178
  128.5 0.0 collective-permute-done.6.other
  128.5 0.7 shard_map.181
  (22 shorter events, 0.1 us)
Async XLA Ops:
  0.6 14.9 %copy-start.7 = (bf16[1,256,4,512]{3,2,1,0:T(4,128)(2,1)S(1)}, bf16[1,256,4,512]{3,2,1,0:T(4,128)(2,1)}, u32[]{:S(2)}) copy-start(bf16[1,256,4,512]{3,2,1,0:T(4,128)(2,1)} %param.11) | copy-start | bytes 3145732
  2.4 17.7 %copy-start.9 = (f32[4,4,512]{2,1,0:T(4,128)S(1)}, f32[4,4,512]{2,1,0:T(4,128)}, u32[]{:S(2)}) copy-start(f32[4,4,512]{2,1,0:T(4,128)} %param.18) | copy-start | bytes 98308
  4.8 15.6 %copy-start.10 = (f32[4,512]{1,0:T(4,128)S(1)}, f32[4,512]{1,0:T(4,128)}, u32[]{:S(2)}) copy-start(f32[4,512]{1,0:T(4,128)} %param.19) | copy-start | bytes 24580
  8.9 13.4 %copy-start.8 = (bf16[1,256,4,128]{3,2,1,0:T(4,128)(2,1)S(1)}, bf16[1,256,4,128]{3,2,1,0:T(4,128)(2,1)}, u32[]{:S(2)}) copy-start(bf16[1,256,4,128]{3,2,1,0:T(4,128)(2,1)} %param.13) | copy-start | bytes 786436
  8.9 17.7 %all-to-all-start = ((bf16[4,528,128]{2,1,0:T(8,128)(2,1)}), bf16[4,528,128]{2,1,0:T(8,128)(2,1)S(1)}, u32[]{:S(2)}, u32[]{:S(2)}) async-start(bf16[4,528,128]{2,1,0:T(8,128)(2,1)} %get-tuple-element.33), calls=%async_computation | async-start | bytes 1081344 | tf_op jit(solution)/shard_map/all_to_all | solution.py:488
  15.7 1.0 copy-start.6
  16.7 12.6 %collective-permute-start.2 = (bf16[8,4,512]{2,0,1:T(8,128)(2,1)S(1)}, bf16[8,4,512]{2,0,1:T(8,128)(2,1)S(1)}, u32[]{:S(2)}, u32[]{:S(2)}) collective-permute-start(bf16[8,4,512]{2,0,1:T(8,128)(2,1)S(1)} %slice_bitcast_fusion), channel_id=1, source_target_pairs={{0,32},{32,64},{64,96},{96,128},{128,160},{160,192},{192,224},{224... | collective-permute-start | bytes 98312 | tf_op jit(solution)/shard_map/ppermute | solution.py:408
  26.7 2.6 %copy-start.2 = (bf16[528,128]{1,0:T(8,128)(2,1)}, bf16[528,128]{1,0:T(8,128)(2,1)S(1)}, u32[]{:S(2)}) copy-start(bf16[528,128]{1,0:T(8,128)(2,1)S(1)} %shard_map.171.after) | copy-start | bytes 405508
  26.7 15.8 %collective-permute-start.1 = (bf16[528,128]{1,0:T(8,128)(2,1)S(1)}, bf16[528,128]{1,0:T(8,128)(2,1)S(1)}, u32[]{:S(2)}, u32[]{:S(2)}) collective-permute-start(bf16[528,128]{1,0:T(8,128)(2,1)S(1)} %shard_map.171.after), channel_id=1, source_target_pairs={{288,0},{320,32},{352,64},{256,96},{416,128},{448,160},{480,192},{... | collective-permute-start | bytes 405512 | tf_op jit(solution)/shard_map/ppermute | solution.py:461
  28.0 24.0 %collective-permute-start = (bf16[528,128]{1,0:T(8,128)(2,1)S(1)}, bf16[528,128]{1,0:T(8,128)(2,1)S(1)}, u32[]{:S(2)}, u32[]{:S(2)}) collective-permute-start(bf16[528,128]{1,0:T(8,128)(2,1)S(1)} %shard_map.171.after), channel_id=1, source_target_pairs={{128,0},{160,32},{192,64},{224,96},{288,128},{320,160},{352,192},{... | collective-permute-start | bytes 405512 | tf_op jit(solution)/shard_map/ppermute | solution.py:461
  29.3 0.6 copy-start.11
  52.9 16.0 %all-to-all-start.1 = ((bf16[4,512,128]{2,1,0:T(8,128)(2,1)}), bf16[4,512,128]{2,1,0:T(8,128)(2,1)S(1)}, u32[]{:S(2)}, u32[]{:S(2)}) async-start(bf16[4,512,128]{2,1,0:T(8,128)(2,1)} %shard_map.173.after), calls=%async_computation.1 | async-start | bytes 1048576 | tf_op jit(solution)/shard_map/all_to_all | solution.py:488
  68.9 0.8 copy-start.5
  69.8 41.6 %copy-start = (f32[4,512,8]{2,1,0:T(8,128)S(1)}, f32[4,512,8]{2,1,0:T(8,128)}, u32[]{:S(2)}) copy-start(f32[4,512,8]{2,1,0:T(8,128)} %maximum_maximum_fusion.taps) | copy-start | bytes 196612
  69.8 41.6 %copy-start.4 = (s32[1,6]{1,0:T(1,128)S(1)}, s32[1,6]{1,0:T(1,128)}, u32[]{:S(2)}) copy-start(s32[1,6]{1,0:T(1,128)} %lengths.7) | copy-start | bytes 76
  78.8 37.7 %copy-start.1 = (bf16[2,2,256,128]{3,2,1,0:T(8,128)(2,1)S(1)}, bf16[2,2,256,128]{3,2,1,0:T(8,128)(2,1)}, u32[]{:S(2)}) copy-start(bf16[2,2,256,128]{3,2,1,0:T(8,128)(2,1)} %get-tuple-element.46.kept) | copy-start | bytes 786436
  78.8 14.2 %all-to-all-start.2 = ((bf16[8,2,24,128]{3,2,1,0:T(8,128)(2,1)}), bf16[8,2,24,128]{3,2,1,0:T(8,128)(2,1)S(1)}, u32[]{:S(2)}, u32[]{:S(2)}) async-start(bf16[8,2,24,128]{3,2,1,0:T(8,128)(2,1)} %bitcast.56), calls=%async_computation.2 | async-start | bytes 196608 | tf_op jit(solution)/shard_map/all_to_all | solution.py:488
  87.9 5.2 %collective-permute-start.3 = (bf16[4,8,512]{2,1,0:T(8,128)(2,1)}, bf16[4,8,512]{2,1,0:T(8,128)(2,1)S(1)}, u32[]{:S(2)}, u32[]{:S(2)}) collective-permute-start(bf16[4,8,512]{2,1,0:T(8,128)(2,1)} %get-tuple-element.45), channel_id=1, source_target_pairs={{32,0},{64,32},{96,64},{128,96},{160,128},{192,160},{224,192},{256... | collective-permute-start | bytes 98312 | tf_op jit(solution)/shard_map/ppermute | solution.py:408
  93.8 26.1 %all-to-all-start.3 = ((bf16[16,2,24,128]{3,2,1,0:T(8,128)(2,1)}), bf16[16,2,24,128]{3,2,1,0:T(8,128)(2,1)S(1)}, u32[]{:S(2)}, u32[]{:S(2)}) async-start(bf16[16,2,24,128]{3,2,1,0:T(8,128)(2,1)} %shard_map.179), calls=%async_computation.3 | async-start | bytes 393216 | tf_op jit(solution)/shard_map/all_to_all | solution.py:488
  106.6 10.0 %collective-permute-start.4 = (bf16[2,2,256,128]{3,2,1,0:T(8,128)(2,1)}, bf16[2,2,256,128]{3,2,1,0:T(8,128)(2,1)S(1)}, u32[]{:S(2)}, u32[]{:S(2)}) collective-permute-start(bf16[2,2,256,128]{3,2,1,0:T(8,128)(2,1)} %get-tuple-element.47), channel_id=1, source_target_pairs={{0,2},{1,3},{2,0},{3,1},{4,6},{5,7},{6,4},{7,5},{8,10},{9,11},{10,... | collective-permute-start | bytes 786440 | tf_op jit(solution)/shard_map/ppermute | solution.py:593
  111.4 1.2 copy-start.3
  116.6 11.2 %collective-permute-start.5 = (bf16[2,256,128]{2,1,0:T(8,128)(2,1)S(1)}, bf16[2,256,128]{2,1,0:T(8,128)(2,1)S(1)}, u32[]{:S(2)}, u32[]{:S(2)}) collective-permute-start(bf16[2,256,128]{2,1,0:T(8,128)(2,1)S(1)} %get-tuple-element.49), channel_id=1, source_target_pairs={{0,1},{1,0},{2,3},{3,2},{4,5},{5,4},{6,7},{7,6},{8,9},{9,8},{10,11... | collective-permute-start | bytes 393224 | tf_op jit(solution)/shard_map/ppermute | solution.py:593
  119.9 8.6 %collective-permute-start.6 = (f32[2,24,128]{2,1,0:T(8,128)S(1)}, f32[2,24,128]{2,1,0:T(8,128)S(1)}, u32[]{:S(2)}, u32[]{:S(2)}) collective-permute-start(f32[2,24,128]{2,1,0:T(8,128)S(1)} %shard_map.180.mine), channel_id=1, source_target_pairs={{0,4},{4,0},{8,12},{12,8},{16,20},{20,16},{24,28},{28,24},{1,5},{5... | collective-permute-start | bytes 73736 | tf_op jit(solution)/shard_map/ppermute | solution.py:639
